TPU v7x, 512 devices: a whole 4x4x16 slice. The times are simulated.
512 devices in a mesh: slab: 32 (over z, core), row: 16 (over y, x).
Axes of the slice: x: 4, y: 4, z: 16, core: 2. Of those that a mesh axis runs over, the one named last changes fastest.
Arguments:
- schur_own: float32 [32, 8192, 768], P('slab', 'row'), may hold values from -16 to 16, as said below
- outgoing: float32 [32, 8192, 768], P('slab', 'row'), may hold values from -12 to 12, as said below
Outputs:
- factor: float32 [32, 8192, 512], P('slab', 'row')
- trailing: float32 [32, 8192, 256], P('slab', 'row')
Inputs may be any that keep to these rules, and one draw needn't show every extreme that they name: On every slab s, rows 0 .. 767 of schur_own[s] are symmetric, and so are those of outgoing[s]; schur_own[s] minus previous[s] there is positive definite (for slab 0, schur_own[0] itself). `outgoing`: rows 0 .. 767 of each slab are symmetric.
All inputs are finite; a program needn't handle non-finite values.
Results may differ from a plain program's by a relative error of at most 0.0001.
Values sent between devices are 32-bit elements; how exact they have to be, the bound alone decides.
No kernel may reach another device: no remote copies, remote signals or barrier semaphores. Data moves between devices by JAX's collectives and lax.ppermute only.
A program may use at most 64 MiB of HBM per device.

v0:
```python
import jax
import jax.numpy as jnp
from jax import lax
from jax.sharding import PartitionSpec as P

NB = 256
PANELS = 2
PANELW = 512


def passed_along(array, axis, by):
    size = lax.axis_size(axis)
    pairs = [(i, i + by) for i in range(size) if 0 <= i + by < size]
    return lax.ppermute(array, axis, pairs)


def per_device(schur_own, outgoing):
    own_block = schur_own[0]
    sent_block = outgoing[0]
    rows_here = own_block.shape[0]
    width_held = own_block.shape[1]
    row_count = lax.axis_size("row")
    row_index = lax.axis_index("row")
    owners = min((width_held + rows_here - 1) // rows_here, row_count)
    global_rows = row_index * rows_here + jnp.arange(rows_here)
    identity = jnp.eye(NB, dtype=jnp.float32)
    received = passed_along(sent_block, "slab", 1)
    head_cols = own_block[:, :PANELW] - received[:, :PANELW]
    trail_cols = own_block[:, PANELW:] - received[:, PANELW:]
    factors = []
    for panel_index in range(PANELS):
        first_col = panel_index * NB
        head_left = PANELW - first_col - NB
        panel_cols = head_cols[:, first_col : first_col + NB]
        start_row = jnp.minimum(row_index, owners - 1) * rows_here
        weight = (row_index < owners).astype(jnp.float32)
        buffer = jnp.zeros((owners * rows_here, NB), jnp.float32)
        buffer = lax.dynamic_update_slice(buffer, panel_cols * weight, (start_row, jnp.int32(0)))
        gathered = lax.psum(buffer, "row")
        shared_rows = gathered[:width_held]
        diag_factor = lax.linalg.cholesky(shared_rows[first_col : first_col + NB])
        inverse = lax.linalg.triangular_solve(diag_factor, identity, left_side=True, lower=True)
        window = jnp.dot(shared_rows[first_col + NB :], inverse.T, precision=lax.Precision.HIGHEST)
        row_mask = (global_rows >= first_col).astype(jnp.float32)[:, None]
        lower_cols = jnp.dot(panel_cols, inverse.T, precision=lax.Precision.HIGHEST) * row_mask
        update = jnp.dot(lower_cols, window.T, precision=lax.Precision.HIGHEST)
        head_cols = head_cols.at[:, first_col + NB :].add(-update[:, :head_left])
        trail_cols = trail_cols - update[:, head_left:]
        factors.append(lower_cols)
    trail_mask = (global_rows >= PANELW).astype(jnp.float32)[:, None]
    factor = jnp.concatenate(factors, axis=1)
    return (factor[None], (trail_cols * trail_mask)[None])


def solution(mesh):
    in_specs = (P("slab", "row", None), P("slab", "row", None))
    out_specs = (P("slab", "row", None), P("slab", "row", None))
    return jax.shard_map(
        per_device, mesh=mesh, in_specs=in_specs, out_specs=out_specs, check_vma=False
    )
```

profile of v0, /device:TPU:6, one launch (start us, length us, event | category | flops | bytes accessed | tf_op | source)
XLA Modules:
  0.0 421.6 jit_solution(6405917216239900913)
XLA Ops:
  7.2 3.0 copy.5
  10.2 2.9 collective-permute-start
  13.1 1.9 copy.4
  15.3 1.7 slice_subtract_fusion
  17.0 1.1 broadcast.104.clone
  19.1 139.7 %all-reduce.4.cloned.1.call-done = f32[1024,256]{0,1:T(8,128)} async-done(((f32[1024,256]{0,1:T(8,128)}), f32[1024,256]{0,1:T(8,128)}) %all-reduce.4.cloned.1.call-update) | async-done | bytes 1048592 | tf_op jit(solution)/shard_map/psum | solution.py:39
  158.7 1.0 slice.146
  159.8 1.0 fusion.9
  160.8 11.7 %custom-call.17 = f32[128,128]{1,0:T(8,128)S(1)} custom-call(f32[128,128]{1,0:T(8,128)S(1)} %slice.147), custom_call_target="Cholesky" | custom-call | tf_op jit(solution)/shard_map/cholesky/custom-call.2 | solution.py:41
  172.6 9.8 %custom-call.18 = f32[1,128,128]{1,2,0:T(8,128)S(1)} custom-call(f32[1,128,128]{2,1,0:T(8,128)S(1)} %get-tuple-element.61), custom_call_target="InvertDiagBlocksLowerTriangular" | custom-call | tf_op jit(solution)/shard_map/cholesky/custom-call.4 | solution.py:41
  183.1 11.7 %custom-call.19 = f32[128,128]{1,0:T(8,128)S(1)} custom-call(f32[128,128]{1,0:T(8,128)S(1)} %convolution_subtract_fusion.3), custom_call_target="Cholesky" | custom-call | tf_op jit(solution)/shard_map/cholesky/custom-call.3 | solution.py:41
  196.9 4.1 while.5
  197.7 1.3 bitcast_dynamic-update-slice_fusion.6
  199.7 1.3 bitcast_dynamic-update-slice_fusion.6
  201.0 19.7 %custom-call.20 = f32[2,128,128]{1,2,0:T(8,128)S(1)} custom-call(f32[2,128,128]{2,1,0:T(8,128)S(1)} %get-tuple-element.30), custom_call_target="InvertDiagBlocksLowerTriangular" | custom-call | tf_op jit(solution)/shard_map/triangular_solve/custom-call.0 | solution.py:42
  222.3 2.0 fusion.4
  224.3 1.0 fusion.38
  225.4 1.1 broadcast.104
  227.4 117.2 %all-reduce.6.cloned.1.call-done = f32[1024,256]{0,1:T(8,128)} async-done(((f32[1024,256]{0,1:T(8,128)}), f32[1024,256]{0,1:T(8,128)}) %all-reduce.6.cloned.1.call-update) | async-done | bytes 1048592 | tf_op jit(solution)/shard_map/psum | solution.py:39
  344.6 1.0 slice.158
  345.7 1.0 bitcast_add_fusion
  346.9 11.7 %custom-call.21 = f32[128,128]{1,0:T(8,128)S(1)} custom-call(f32[128,128]{1,0:T(8,128)S(1)} %slice.159), custom_call_target="Cholesky" | custom-call | tf_op jit(solution)/shard_map/cholesky/custom-call.2 | solution.py:41
  358.6 9.8 %custom-call.22 = f32[1,128,128]{1,2,0:T(8,128)S(1)} custom-call(f32[1,128,128]{2,1,0:T(8,128)S(1)} %get-tuple-element.57), custom_call_target="InvertDiagBlocksLowerTriangular" | custom-call | tf_op jit(solution)/shard_map/cholesky/custom-call.4 | solution.py:41
  369.2 11.9 %custom-call.23 = f32[128,128]{1,0:T(8,128)S(1)} custom-call(f32[128,128]{1,0:T(8,128)S(1)} %convolution_subtract_fusion.2), custom_call_target="Cholesky" | custom-call | tf_op jit(solution)/shard_map/cholesky/custom-call.3 | solution.py:41
  383.7 3.9 while.6
  384.3 1.4 bitcast_dynamic-update-slice_fusion.7
  386.3 1.4 bitcast_dynamic-update-slice_fusion.7
  387.7 19.7 %custom-call.24 = f32[2,128,128]{1,2,0:T(8,128)S(1)} custom-call(f32[2,128,128]{2,1,0:T(8,128)S(1)} %get-tuple-element.31), custom_call_target="InvertDiagBlocksLowerTriangular" | custom-call | tf_op jit(solution)/shard_map/triangular_solve/custom-call.0 | solution.py:42
  409.0 1.5 fusion.7
  410.6 1.9 fusion.2
  412.4 1.0 copy.15
  413.4 1.3 copy.14
  (58 shorter events, 11.7 us)
Async XLA Ops:
  7.2 151.6 %all-reduce.4.cloned.1.call-start = ((), (), s32[]{:S(2)}) async-start(), calls=%async_computation | async-start | bytes 2097152 | tf_op jit(solution)/shard_map/psum | solution.py:39
  10.2 5.1 %collective-permute-start = (f32[512,768]{0,1:T(8,128)}, f32[512,768]{0,1:T(8,128)}, u32[]{:S(2)}, u32[]{:S(2)}) collective-permute-start(f32[512,768]{0,1:T(8,128)} %bitcast.1), channel_id=1, source_target_pairs={{0,16},{16,32},{32,48},{48,64},{64,80},{80,96},{96,112},{112,128},... | collective-permute-start | bytes 4718600 | tf_op jit(solution)/shard_map/ppermute | solution.py:14
  15.0 2.0 copy-start
  18.9 325.7 %all-reduce.6.cloned.1.call-start = ((), (), s32[]{:S(2)}) async-start(), calls=%async_computation.1 | async-start | bytes 2097152 | tf_op jit(solution)/shard_map/psum | solution.py:39
Sparse Core Ops, SparseCore 0:
  19.1 139.6 all-reduce.3
  227.5 117.0 all-reduce.5
where the time goes:
time: 422 us
  waiting for transfers between devices  257 us (61%)
  other arithmetic  114 us (27%)
  local copies, waits for them, and re-layouts  19.8 us (5%)
  between operations  16.9 us (4%)
  matrix products  10.7 us (3%)
    psum x2, waiting for transfers between devices, per_device(): gathered = lax.psum(buffer, 'row')  257 us
    another operation x13, other arithmetic, per_device(): diag_factor = lax.linalg.cholesky(shared_rows[first_col:first_col + NB])  68.7 us
    another operation x5, other arithmetic, per_device(): lax.linalg.triangular_solve(diag_factor, identity, left_side=True, lower=...  39.4 us
  transfers between devices with their start and end apart: 3, of which 3 were waited for; matrix products, arithmetic and copies ran while one was open for 0% of the time, Pallas kernels for 0%

commit v1 on v0

v1 whole, which is shorter than its diff:
```python
import jax
import jax.numpy as jnp
from jax import lax
from jax.experimental import pallas as pl
from jax.experimental.pallas import tpu as pltpu
from jax.sharding import PartitionSpec as P

NB = 256
PANELW = 512
COLS = 768
STRIP = 32
SUB = 8
LANES = 128
VMEM_BYTES = 48 * 1024 * 1024


def dot(a, b, contract):
    return lax.dot_general(
        a, b, ((contract[:1], contract[1:]), ((), ())),
        precision=lax.Precision.HIGHEST, preferred_element_type=jnp.float32,
    )


def eliminate_strip(rows, first):
    groups = len(rows)
    lane = lax.broadcasted_iota(jnp.int32, (SUB, NB), 1)
    sub = lax.broadcasted_iota(jnp.int32, (SUB, NB), 0)
    for t in range(groups):
        col = first + SUB * t
        in_block = (lane >= col) & (lane < col + SUB)
        columns = [
            [jnp.broadcast_to(rows[g][:, col + j : col + j + 1], (SUB, LANES)) for j in range(SUB)]
            for g in range(t, groups)
        ]
        a = [
            [jnp.broadcast_to(columns[0][k][i : i + 1, :], (SUB, LANES)) if i >= k else None
             for k in range(SUB)]
            for i in range(SUB)
        ]
        start = jnp.where(in_block, (lane == col + sub).astype(jnp.float32), rows[t])
        u = [jnp.broadcast_to(start[i : i + 1, :], (SUB, NB)) for i in range(SUB)]
        inv = [None] * SUB
        low = [[None] * SUB for _ in range(SUB)]
        for j in range(SUB):
            inv[j] = lax.rsqrt(a[j][j])
            for k in range(j + 1, SUB):
                low[k][j] = a[k][j] * inv[j]
            for k in range(j + 1, SUB):
                for m in range(j + 1, k + 1):
                    a[k][m] = a[k][m] - low[k][j] * low[m][j]
        wide = lambda x: jnp.concatenate([x, x], axis=1)
        for j in range(SUB):
            u[j] = u[j] * wide(inv[j])
            for k in range(j + 1, SUB):
                u[k] = u[k] - wide(low[k][j]) * u[j]
        packed = u[0]
        for j in range(1, SUB):
            packed = jnp.where(sub == j, u[j], packed)
        rows[t] = packed
        for g in range(t + 1, groups):
            col_g = columns[g - t]
            total = jnp.where(in_block, 0.0, rows[g])
            for j in range(SUB):
                col_g[j] = col_g[j] * inv[j]
                for k in range(j + 1, SUB):
                    col_g[k] = col_g[k] - col_g[j] * low[k][j]
                total = total - wide(col_g[j]) * u[j]
            rows[g] = total
    return rows


def invert_factor(work, between=None):
    groups = STRIP // SUB
    for s in range(NB // STRIP):
        first = STRIP * s
        after = first + STRIP
        rows = [work[first + SUB * g : first + SUB * (g + 1), :] for g in range(groups)]
        rows = eliminate_strip(rows, first)
        strip = jnp.concatenate(rows, axis=0)
        lane = lax.broadcasted_iota(jnp.int32, (STRIP, NB), 1)
        row = lax.broadcasted_iota(jnp.int32, (STRIP, NB), 0) + first
        strip = jnp.where((lane > row) & (lane < after), 0.0, strip)
        work[first:after, :] = jnp.where(lane < after, strip, 0.0)
        if between is not None:
            between(s)
        if after < NB:
            base = after // LANES * LANES
            update = dot(strip[:, base:], strip, (0, 0))[after - base :, :]
            lane = lax.broadcasted_iota(jnp.int32, (NB - after, NB), 1)
            below = jnp.where((lane >= first) & (lane < after), 0.0, work[after:, :])
            work[after:, :] = below - update


def first_kernel(block, inverse):
    inverse[...] = block[...]
    invert_factor(inverse)


def second_kernel(row_index, inverse0, head, own, prev, factor, trailing, work, middle, tail):
    x0 = inverse0[...]
    w1 = dot(x0, head[:NB, :NB], (1, 0))
    w2 = dot(x0, head[:NB, NB:], (1, 0))
    work[...] = head[NB:, :NB] - dot(w1, w1, (0, 0))
    cross = head[NB:, NB:] - dot(w1, w2, (0, 0))
    rows_here = own.shape[0]
    piece = rows_here // (NB // STRIP)

    def between(s):
        at = pl.ds(s * piece, piece)
        lower = dot(own[at, :NB] - prev[at, :NB], x0, (1, 1))
        factor[at, :NB] = lower
        middle[at, :] = own[at, NB:PANELW] - prev[at, NB:PANELW] - dot(lower, w1, (1, 0))
        tail[at, :] = own[at, PANELW:] - prev[at, PANELW:] - dot(lower, w2, (1, 0))

    invert_factor(work, between)
    x1 = work[...]
    w3 = dot(x1, cross, (1, 0))
    first_row = row_index[0] * rows_here
    row = first_row + lax.broadcasted_iota(jnp.int32, (rows_here, NB), 0)
    lower = jnp.where(row >= NB, dot(middle[...], x1, (1, 1)), 0.0)
    factor[:, NB:] = lower
    trailing[...] = jnp.where(row >= PANELW, tail[...] - dot(lower, w3, (1, 0)), 0.0)


def spread(block):
    return lax.all_to_all(block, "row", 0, 0, tiled=True)[0]


def gather(chunk):
    count = lax.axis_size("row")
    sent = jnp.broadcast_to(chunk[None], (count,) + chunk.shape)
    full = lax.all_to_all(sent, "row", 0, 0, tiled=True)
    return full.reshape((-1, chunk.shape[1]))


def per_device(schur_own, outgoing):
    own = schur_own[0]
    out = outgoing[0]
    count = lax.axis_size("row")
    slabs = lax.axis_size("slab")
    pairs = [(s, s + 1) for s in range(slabs - 1)]
    vmem = pl.BlockSpec(memory_space=pltpu.VMEM)
    params = pltpu.CompilerParams(vmem_limit_bytes=VMEM_BYTES)

    part = NB // count
    both = jnp.concatenate(
        [x[:NB, :NB].reshape(count, part, NB) for x in (own, out)], axis=1
    )
    shared = spread(both)
    chunk = shared[:part] - lax.ppermute(shared[part:], "slab", pairs)
    prev_right = lax.ppermute(out[:, NB:], "slab", pairs)
    first = gather(chunk)
    inverse0 = pl.pallas_call(
        first_kernel,
        out_shape=jax.ShapeDtypeStruct((NB, NB), jnp.float32),
        in_specs=[vmem], out_specs=vmem, compiler_params=params,
        cost_estimate=pl.CostEstimate(flops=6 * NB**3, bytes_accessed=8 * NB**2, transcendentals=NB),
        name="panel_inverse",
    )(first)
    head_chunk = spread((own[:, NB:] - prev_right).reshape(count, -1, COLS - NB))
    head = gather(head_chunk)
    prev_left = lax.ppermute(out[:, :NB], "slab", pairs)
    prev = jnp.concatenate([prev_left, prev_right], axis=1)
    rows_here = own.shape[0]
    factor, trailing = pl.pallas_call(
        second_kernel,
        out_shape=(
            jax.ShapeDtypeStruct((rows_here, PANELW), jnp.float32),
            jax.ShapeDtypeStruct((rows_here, COLS - PANELW), jnp.float32),
        ),
        in_specs=[pl.BlockSpec(memory_space=pltpu.SMEM)] + [vmem] * 4,
        out_specs=(vmem, vmem),
        scratch_shapes=[
            pltpu.VMEM((NB, NB), jnp.float32),
            pltpu.VMEM((rows_here, NB), jnp.float32),
            pltpu.VMEM((rows_here, NB), jnp.float32),
        ],
        compiler_params=params,
        name="panel_update",
    )(lax.axis_index("row").astype(jnp.int32)[None], inverse0, head, own, prev)
    return factor[None], trailing[None]


def solution(mesh):
    specs = (P("slab", "row", None), P("slab", "row", None))
    return jax.shard_map(
        per_device, mesh=mesh, in_specs=specs, out_specs=specs, check_vma=False
    )
```

time: 422 us -> 102 us (0.24)
  the two profiles are of different devices: /device:TPU:6 before, /device:TPU:99 now
where the time goes in v1:
time: 102 us
  starting transfers between devices  41 us (40%)
  waiting for transfers between devices  25.1 us (25%)
  Pallas kernels  24.2 us (24%)
  local copies, waits for them, and re-layouts  7.13 us (7%)
  other arithmetic  3.58 us (4%)
    pallas_call x1, Pallas kernels, per_device(): pl.pallas_call(second_kernel, out_shape=(jax.ShapeDtypeStruct((rows_here,...  14.7 us
    all_to_all x2, waiting for transfers between devices, spread(): return lax.all_to_all(block, 'row', 0, 0, tiled=True)[0]  14.5 us
    all_to_all x2, starting transfers between devices, spread(): return lax.all_to_all(block, 'row', 0, 0, tiled=True)[0]  12.2 us
    all_to_all x2, starting transfers between devices, gather(): full = lax.all_to_all(sent, 'row', 0, 0, tiled=True)  11.5 us
    pallas_call x1, Pallas kernels, per_device(): pl.pallas_call(first_kernel, out_shape=jax.ShapeDtypeStruct((NB, NB), jnp...  9.46 us
    ppermute x1, starting transfers between devices, per_device(): prev_left = lax.ppermute(out[:, :NB], 'slab', pairs)  7.18 us
    all_to_all x2, waiting for transfers between devices, gather(): full = lax.all_to_all(sent, 'row', 0, 0, tiled=True)  6.45 us
    ppermute x1, starting transfers between devices, per_device(): prev_right = lax.ppermute(out[:, NB:], 'slab', pairs)  5.3 us
  transfers between devices with their start and end apart: 7, of which 5 were waited for; matrix products, arithmetic and copies ran while one was open for 6% of the time, Pallas kernels for 9%

profile of v1, /device:TPU:99, one launch (start us, length us, event | category | flops | bytes accessed | tf_op | source)
XLA Modules:
  0.0 101.8 jit_solution(15946988313084709094)
XLA Ops:
  0.6 0.0 copy-start
  0.6 2.4 %slice.48 = f32[512,512]{1,0:T(8,128)} slice(f32[512,768]{1,0:T(8,128)} %bitcast.23), slice={[0:512], [256:768]} | slice | bytes 2097152 | tf_op jit(solution)/shard_map/slice | solution.py:151
  3.0 5.3 %collective-permute-start.1 = (f32[512,512]{1,0:T(8,128)}, f32[512,512]{1,0:T(8,128)S(1)}, u32[]{:S(2)}, u32[]{:S(2)}) collective-permute-start(f32[512,512]{1,0:T(8,128)} %slice.48), channel_id=1, source_target_pairs={{0,16},{16,32},{32,48},{48,64},{64,80},{80,96},{96,112},{112,128},... | collective-permute-start | bytes 3145736 | tf_op jit(solution)/shard_map/ppermute | solution.py:151
  8.3 1.0 slice.44
  9.3 0.0 copy-done
  9.3 0.8 pad_maximum_fusion.1
  10.2 6.9 %all-to-all-start = ((f32[16,32,256]{2,1,0:T(8,128)}), f32[16,32,256]{2,1,0:T(8,128)S(1)}, u32[]{:S(2)}, u32[]{:S(2)}) async-start(f32[16,32,256]{2,1,0:T(8,128)} %pad_maximum_fusion.1), calls=%async_computation | async-start | bytes 1048576 | tf_op jit(solution)/shard_map/all_to_all | solution.py:126
  17.1 3.3 %collective-permute-done.1 = f32[512,512]{1,0:T(8,128)S(1)} collective-permute-done((f32[512,512]{1,0:T(8,128)}, f32[512,512]{1,0:T(8,128)S(1)}, u32[]{:S(2)}, u32[]{:S(2)}) %collective-permute-start.1) | collective-permute-done | bytes 1048608 | tf_op jit(solution)/shard_map/ppermute | solution.py:151
  20.4 0.0 copy-start.1
  20.4 1.3 %slice_subtract_fusion = f32[512,512]{1,0:T(8,128)} fusion(f32[512,512]{1,0:T(8,128)S(1)} %collective-permute-done.1, f32[512,768]{1,0:T(8,128)S(1)} %bitcast.19), kind=kLoop, calls=%fused_computation.1 | loop fusion | flops 262144 | bytes 3145728 | tf_op jit(solution)/shard_map/sub | solution.py:160
  21.6 4.2 %all-to-all-done = f32[16,32,256]{2,1,0:T(8,128)S(1)} async-done(((f32[16,32,256]{2,1,0:T(8,128)}), f32[16,32,256]{2,1,0:T(8,128)S(1)}, u32[]{:S(2)}, u32[]{:S(2)}) %all-to-all-start) | async-done | bytes 524320 | tf_op jit(solution)/shard_map/all_to_all | solution.py:126
  25.8 5.3 %all-to-all-start.2 = ((f32[16,32,512]{2,1,0:T(8,128)}), f32[16,32,512]{2,1,0:T(8,128)}, u32[]{:S(2)}, u32[]{:S(2)}) async-start(f32[16,32,512]{2,1,0:T(8,128)} %bitcast.22), calls=%async_computation.2 | async-start | bytes 2097152 | tf_op jit(solution)/shard_map/all_to_all | solution.py:126
  31.1 4.9 %collective-permute-start = (f32[16,256]{1,0:T(8,128)S(1)}, f32[16,256]{1,0:T(8,128)S(1)}, u32[]{:S(2)}, u32[]{:S(2)}) collective-permute-start(f32[16,256]{1,0:T(8,128)S(1)} %slice_bitcast_fusion.1), channel_id=1, source_target_pairs={{0,16},{16,32},{32,48},{48,64},{64,80},{80,96},{96,112},{112,128},... | collective-permute-start | bytes 49160 | tf_op jit(solution)/shard_map/ppermute | solution.py:150
  36.0 0.8 collective-permute-done
  36.8 10.4 %all-to-all-done.2 = f32[16,32,512]{2,1,0:T(8,128)} async-done(((f32[16,32,512]{2,1,0:T(8,128)}), f32[16,32,512]{2,1,0:T(8,128)}, u32[]{:S(2)}, u32[]{:S(2)}) %all-to-all-start.2) | async-done | bytes 1048608 | tf_op jit(solution)/shard_map/all_to_all | solution.py:126
  47.2 0.7 broadcast_in_dim.23
  47.9 0.0 copy-done.1
  47.9 6.1 %all-to-all-start.1 = ((f32[16,16,256]{2,1,0:T(8,128)}), f32[16,16,256]{2,1,0:T(8,128)S(1)}, u32[]{:S(2)}, u32[]{:S(2)}) async-start(f32[16,16,256]{2,1,0:T(8,128)} %broadcast_in_dim.23), calls=%async_computation.1 | async-start | bytes 524288 | tf_op jit(solution)/shard_map/all_to_all | solution.py:132
  54.0 0.8 slice_bitcast_fusion
  54.8 6.5 %all-to-all-done.1 = f32[16,16,256]{2,1,0:T(8,128)S(1)} async-done(((f32[16,16,256]{2,1,0:T(8,128)}), f32[16,16,256]{2,1,0:T(8,128)S(1)}, u32[]{:S(2)}, u32[]{:S(2)}) %all-to-all-start.1) | async-done | bytes 262176 | tf_op jit(solution)/shard_map/all_to_all | solution.py:132
  61.3 1.1 %broadcast_in_dim.25 = f32[16,32,512]{2,1,0:T(8,128)} broadcast(f32[32,512]{1,0:T(8,128)S(1)} %slice_bitcast_fusion), dimensions={1,2} | broadcast | bytes 1114112 | tf_op jit(solution)/shard_map/broadcast_in_dim | solution.py:131
  62.4 5.5 %all-to-all-start.3 = ((f32[16,32,512]{2,1,0:T(8,128)}), f32[16,32,512]{2,1,0:T(8,128)}, u32[]{:S(2)}, u32[]{:S(2)}) async-start(f32[16,32,512]{2,1,0:T(8,128)} %broadcast_in_dim.25), calls=%async_computation.3 | async-start | bytes 2097152 | tf_op jit(solution)/shard_map/all_to_all | solution.py:132
  67.8 1.1 %slice.50 = f32[512,256]{1,0:T(8,128)S(1)} slice(f32[512,768]{1,0:T(8,128)} %bitcast.25), slice={[0:512], [0:256]} | slice | bytes 1048576 | tf_op jit(solution)/shard_map/slice | solution.py:162
  68.9 7.2 %collective-permute-start.2 = (f32[512,256]{1,0:T(8,128)S(1)}, f32[512,256]{1,0:T(8,128)}, u32[]{:S(2)}, u32[]{:S(2)}) collective-permute-start(f32[512,256]{1,0:T(8,128)S(1)} %slice.50), channel_id=1, source_target_pairs={{0,16},{16,32},{32,48},{48,64},{64,80},{80,96},{96,112},{112,128},... | collective-permute-start | bytes 1572872 | tf_op jit(solution)/shard_map/ppermute | solution.py:162
  76.1 9.5 %panel_inverse.1.inverse0 = f32[256,256]{1,0:T(8,128)S(1)} custom-call(f32[256,256]{1,0:T(8,128)S(1)} %bitcast.21), custom_call_target="tpu_custom_call" | custom-call | flops 100663296 | bytes 524288 | tf_op jit(solution)/shard_map/panel_inverse/pallas_call | solution.py:153
  85.6 0.0 collective-permute-done.2
  85.6 1.5 %pad_maximum_fusion.prev = f32[512,768]{1,0:T(8,128)S(1)} fusion(f32[512,512]{1,0:T(8,128)} %copy-done.1, f32[512,256]{1,0:T(8,128)} %collective-permute-done.2), kind=kLoop, calls=%fused_computation | loop fusion | flops 393216 | bytes 3145728 | tf_op jit(solution)/shard_map/concatenate | solution.py:163
  87.0 0.0 all-to-all-done.3
  87.1 14.7 %panel_update.1 = (f32[512,512]{1,0:T(8,128)}, f32[512,256]{1,0:T(8,128)}) custom-call(s32[1]{0:T(128)} %bitcast.row_index, f32[256,256]{1,0:T(8,128)S(1)} %panel_inverse.1.inverse0, f32[512,512]{1,0:T(8,128)} %bitcast.10.head, f32[512,768]{1,0:T(8,128)S(1)} %bitcast.20, f32[512,768]{1,0:T(8,128)S(1)} %pad_maximum_fusion.prev), custom_call_target="tpu_custom_call" | custom-call | tf_op jit(solution)/shard_map/panel_update/pallas_call | solution.py:165
  (3 shorter events, 0.0 us)
Async XLA Ops:
  0.6 8.7 %copy-start = (f32[1,512,768]{2,1,0:T(8,128)S(1)}, f32[1,512,768]{2,1,0:T(8,128)}, u32[]{:S(2)}) copy-start(f32[1,512,768]{2,1,0:T(8,128)} %param.2) | copy-start | bytes 4718596
  3.0 17.3 %collective-permute-start.1 = (f32[512,512]{1,0:T(8,128)}, f32[512,512]{1,0:T(8,128)S(1)}, u32[]{:S(2)}, u32[]{:S(2)}) collective-permute-start(f32[512,512]{1,0:T(8,128)} %slice.48), channel_id=1, source_target_pairs={{0,16},{16,32},{32,48},{48,64},{64,80},{80,96},{96,112},{112,128},... | collective-permute-start | bytes 3145736 | tf_op jit(solution)/shard_map/ppermute | solution.py:151
  10.2 15.7 %all-to-all-start = ((f32[16,32,256]{2,1,0:T(8,128)}), f32[16,32,256]{2,1,0:T(8,128)S(1)}, u32[]{:S(2)}, u32[]{:S(2)}) async-start(f32[16,32,256]{2,1,0:T(8,128)} %pad_maximum_fusion.1), calls=%async_computation | async-start | bytes 1048576 | tf_op jit(solution)/shard_map/all_to_all | solution.py:126
  20.4 27.5 %copy-start.1 = (f32[512,512]{1,0:T(8,128)}, f32[512,512]{1,0:T(8,128)S(1)}, u32[]{:S(2)}) copy-start(f32[512,512]{1,0:T(8,128)S(1)} %collective-permute-done.1) | copy-start | bytes 3145732
  25.8 21.3 %all-to-all-start.2 = ((f32[16,32,512]{2,1,0:T(8,128)}), f32[16,32,512]{2,1,0:T(8,128)}, u32[]{:S(2)}, u32[]{:S(2)}) async-start(f32[16,32,512]{2,1,0:T(8,128)} %bitcast.22), calls=%async_computation.2 | async-start | bytes 2097152 | tf_op jit(solution)/shard_map/all_to_all | solution.py:126
  31.1 5.7 %collective-permute-start = (f32[16,256]{1,0:T(8,128)S(1)}, f32[16,256]{1,0:T(8,128)S(1)}, u32[]{:S(2)}, u32[]{:S(2)}) collective-permute-start(f32[16,256]{1,0:T(8,128)S(1)} %slice_bitcast_fusion.1), channel_id=1, source_target_pairs={{0,16},{16,32},{32,48},{48,64},{64,80},{80,96},{96,112},{112,128},... | collective-permute-start | bytes 49160 | tf_op jit(solution)/shard_map/ppermute | solution.py:150
  47.9 13.3 %all-to-all-start.1 = ((f32[16,16,256]{2,1,0:T(8,128)}), f32[16,16,256]{2,1,0:T(8,128)S(1)}, u32[]{:S(2)}, u32[]{:S(2)}) async-start(f32[16,16,256]{2,1,0:T(8,128)} %broadcast_in_dim.23), calls=%async_computation.1 | async-start | bytes 524288 | tf_op jit(solution)/shard_map/all_to_all | solution.py:132
  62.4 24.7 %all-to-all-start.3 = ((f32[16,32,512]{2,1,0:T(8,128)}), f32[16,32,512]{2,1,0:T(8,128)}, u32[]{:S(2)}, u32[]{:S(2)}) async-start(f32[16,32,512]{2,1,0:T(8,128)} %broadcast_in_dim.25), calls=%async_computation.3 | async-start | bytes 2097152 | tf_op jit(solution)/shard_map/all_to_all | solution.py:132
  68.9 16.7 %collective-permute-start.2 = (f32[512,256]{1,0:T(8,128)S(1)}, f32[512,256]{1,0:T(8,128)}, u32[]{:S(2)}, u32[]{:S(2)}) collective-permute-start(f32[512,256]{1,0:T(8,128)S(1)} %slice.50), channel_id=1, source_target_pairs={{0,16},{16,32},{32,48},{48,64},{64,80},{80,96},{96,112},{112,128},... | collective-permute-start | bytes 1572872 | tf_op jit(solution)/shard_map/ppermute | solution.py:162

commit v2 on v1

--- a/solution.py
+++ b/solution.py
@@ -1,13 +1,16 @@
+import functools
+
 import jax
 import jax.numpy as jnp
 from jax import lax
 from jax.experimental import pallas as pl
 from jax.experimental.pallas import tpu as pltpu
-from jax.sharding import PartitionSpec as P
+from jax.sharding import Mesh, PartitionSpec as P
 
 NB = 256
 PANELW = 512
 COLS = 768
+ROWS_Y = 4
 STRIP = 32
 SUB = 8
 LANES = 128
@@ -69,9 +72,9 @@
     return rows
 
 
-def invert_factor(work, between=None):
+def invert_factor(work, strips=range(NB // STRIP), between=None):
     groups = STRIP // SUB
-    for s in range(NB // STRIP):
+    for s in strips:
         first = STRIP * s
         after = first + STRIP
         rows = [work[first + SUB * g : first + SUB * (g + 1), :] for g in range(groups)]
@@ -91,17 +94,19 @@
             work[after:, :] = below - update
 
 
-def first_kernel(block, inverse):
+def first_kernel(strips, block, inverse):
     inverse[...] = block[...]
-    invert_factor(inverse)
+    invert_factor(inverse, strips)
 
 
 def second_kernel(row_index, inverse0, head, own, prev, factor, trailing, work, middle, tail):
     x0 = inverse0[...]
-    w1 = dot(x0, head[:NB, :NB], (1, 0))
-    w2 = dot(x0, head[:NB, NB:], (1, 0))
-    work[...] = head[NB:, :NB] - dot(w1, w1, (0, 0))
-    cross = head[NB:, NB:] - dot(w1, w2, (0, 0))
+    half = head.shape[0] // 2
+    pick = lambda at, source: head[pl.ds(at, half), source].reshape((NB, NB))
+    w1 = dot(x0, pick(0, 0), (1, 0))
+    w2 = dot(x0, pick(0, 1), (1, 1))
+    work[...] = pick(half, 0) - dot(w1, w1, (0, 0))
+    cross = pick(half, 1) - dot(w2, w1, (0, 0))
     rows_here = own.shape[0]
     piece = rows_here // (NB // STRIP)
 
@@ -112,9 +117,9 @@
         middle[at, :] = own[at, NB:PANELW] - prev[at, NB:PANELW] - dot(lower, w1, (1, 0))
         tail[at, :] = own[at, PANELW:] - prev[at, PANELW:] - dot(lower, w2, (1, 0))
 
-    invert_factor(work, between)
+    invert_factor(work, between=between)
     x1 = work[...]
-    w3 = dot(x1, cross, (1, 0))
+    w3 = dot(x1, cross, (1, 1))
     first_row = row_index[0] * rows_here
     row = first_row + lax.broadcasted_iota(jnp.int32, (rows_here, NB), 0)
     lower = jnp.where(row >= NB, dot(middle[...], x1, (1, 1)), 0.0)
@@ -122,46 +127,52 @@
     trailing[...] = jnp.where(row >= PANELW, tail[...] - dot(lower, w3, (1, 0)), 0.0)
 
 
-def spread(block):
-    return lax.all_to_all(block, "row", 0, 0, tiled=True)[0]
-
-
-def gather(chunk):
-    count = lax.axis_size("row")
-    sent = jnp.broadcast_to(chunk[None], (count,) + chunk.shape)
-    full = lax.all_to_all(sent, "row", 0, 0, tiled=True)
-    return full.reshape((-1, chunk.shape[1]))
+def exchange(blocks, axis):
+    return lax.all_to_all(blocks, axis, 0, 0, tiled=True)
+
+
+def copies(chunk, axis):
+    return jnp.broadcast_to(chunk[None], (lax.axis_size(axis),) + chunk.shape)
 
 
 def per_device(schur_own, outgoing):
     own = schur_own[0]
     out = outgoing[0]
-    count = lax.axis_size("row")
-    slabs = lax.axis_size("slab")
-    pairs = [(s, s + 1) for s in range(slabs - 1)]
+    rows_here = own.shape[0]
+    across = lax.axis_size("x")
+    plane = lax.axis_size("y") * across
+    row_index = lax.axis_index("y") * across + lax.axis_index("x")
+    pairs = [(s, s + 1) for s in range(lax.axis_size("slab") - 1)]
     vmem = pl.BlockSpec(memory_space=pltpu.VMEM)
     params = pltpu.CompilerParams(vmem_limit_bytes=VMEM_BYTES)
 
-    part = NB // count
-    both = jnp.concatenate(
-        [x[:NB, :NB].reshape(count, part, NB) for x in (own, out)], axis=1
-    )
-    shared = spread(both)
-    chunk = shared[:part] - lax.ppermute(shared[part:], "slab", pairs)
-    prev_right = lax.ppermute(out[:, NB:], "slab", pairs)
-    first = gather(chunk)
-    inverse0 = pl.pallas_call(
-        first_kernel,
-        out_shape=jax.ShapeDtypeStruct((NB, NB), jnp.float32),
-        in_specs=[vmem], out_specs=vmem, compiler_params=params,
-        cost_estimate=pl.CostEstimate(flops=6 * NB**3, bytes_accessed=8 * NB**2, transcendentals=NB),
-        name="panel_inverse",
-    )(first)
-    head_chunk = spread((own[:, NB:] - prev_right).reshape(count, -1, COLS - NB))
-    head = gather(head_chunk)
-    prev_left = lax.ppermute(out[:, :NB], "slab", pairs)
-    prev = jnp.concatenate([prev_left, prev_right], axis=1)
-    rows_here = own.shape[0]
+    def inverse_step(block, strips, name):
+        return pl.pallas_call(
+            functools.partial(first_kernel, strips),
+            out_shape=jax.ShapeDtypeStruct((NB, NB), jnp.float32),
+            in_specs=[vmem], out_specs=vmem, compiler_params=params,
+            cost_estimate=pl.CostEstimate(
+                flops=3 * NB**3, bytes_accessed=8 * NB**2, transcendentals=NB),
+            name=name,
+        )(block)
+
+    corner = own[:NB, :NB] - lax.ppermute(out[:NB, :NB], "slab", pairs)
+    prev = lax.ppermute(out, "slab", pairs)
+    part = exchange(corner.reshape(across, -1, NB), "x")[0]
+    part = exchange(copies(part, "y"), "y")[0]
+    first = exchange(copies(part, "x"), "x").reshape(NB, NB)
+
+    head = own[:, NB:PANELW] - prev[:, NB:PANELW]
+    side = own[:NB, :PANELW] - prev[:NB, :PANELW]
+    side = jnp.concatenate([side[:, :NB], side[:, NB:]], axis=0)
+    mine = jnp.where(row_index == 1, side, head)
+    mine, first = lax.optimization_barrier((mine, first))
+    shared = exchange(mine.reshape(plane, -1, NB), ("y", "x"))[:2]
+    start = inverse_step(first, range(0, 4), "inverse_left")
+    shared, start = lax.optimization_barrier((shared, start))
+    shared = exchange(copies(shared, ("y", "x")), ("y", "x"))
+    inverse0 = inverse_step(start, range(4, 8), "inverse_right")
+
     factor, trailing = pl.pallas_call(
         second_kernel,
         out_shape=(
@@ -177,12 +188,13 @@
         ],
         compiler_params=params,
         name="panel_update",
-    )(lax.axis_index("row").astype(jnp.int32)[None], inverse0, head, own, prev)
+    )(row_index.astype(jnp.int32)[None], inverse0, shared, own, prev)
     return factor[None], trailing[None]
 
 
 def solution(mesh):
-    specs = (P("slab", "row", None), P("slab", "row", None))
+    planes = Mesh(mesh.devices.reshape(mesh.shape["slab"], ROWS_Y, -1), ("slab", "y", "x"))
+    specs = (P("slab", ("y", "x"), None), P("slab", ("y", "x"), None))
     return jax.shard_map(
-        per_device, mesh=mesh, in_specs=specs, out_specs=specs, check_vma=False
+        per_device, mesh=planes, in_specs=specs, out_specs=specs, check_vma=False
     )

time: 102 us -> 111 us (1.088)
  the two profiles are of different devices: /device:TPU:99 before, /device:TPU:224 now
where the time goes in v2:
time: 111 us; the launch traced here: 110 us
  waiting for transfers between devices  42.2 us (38%)
  Pallas kernels  23.9 us (22%)
  starting transfers between devices  23.7 us (21%)
  blocking collectives  11.7 us (11%)
  local copies, waits for them, and re-layouts  6.06 us (5%)
  other arithmetic  2.06 us (2%)
    all_to_all x4, waiting for transfers between devices, exchange(): return lax.all_to_all(blocks, axis, 0, 0, tiled=True)  25.5 us
    ppermute x1, waiting for transfers between devices, per_device(): corner = own[:NB, :NB] - lax.ppermute(out[:NB, :NB], 'slab', pairs)  16.7 us
    all_to_all x4, starting transfers between devices, exchange(): return lax.all_to_all(blocks, axis, 0, 0, tiled=True)  16.6 us
    pallas_call x1, Pallas kernels, per_device(): pl.pallas_call(second_kernel, out_shape=(jax.ShapeDtypeStruct((rows_here,...  14.6 us
    all_to_all x1, blocking collectives, exchange(): return lax.all_to_all(blocks, axis, 0, 0, tiled=True)  11.7 us
    pallas_call x2, Pallas kernels, inverse_step(): pl.pallas_call(functools.partial(first_kernel, strips), out_shape=jax.Sha...  9.31 us
    ppermute x1, starting transfers between devices, per_device(): corner = own[:NB, :NB] - lax.ppermute(out[:NB, :NB], 'slab', pairs)  5.15 us
    broadcast_in_dim x5, local copies, waits for them, and re-layouts, copies(): return jnp.broadcast_to(chunk[None], (lax.axis_size(axis),) + chunk.shape)  2.55 us
  transfers between devices with their start and end apart: 6, of which 5 were waited for; matrix products, arithmetic and copies ran while one was open for 4% of the time, Pallas kernels for 8%

profile of v2, /device:TPU:224, one launch (start us, length us, event | category | flops | bytes accessed | tf_op | source)
XLA Modules:
  0.0 110.4 jit_solution(11134314440948377552)
XLA Ops:
  0.6 1.9 %collective-permute-start = (f32[512,768]{1,0:T(8,128)}, f32[512,768]{1,0:T(8,128)S(1)}, u32[]{:S(2)}, u32[]{:S(2)}) collective-permute-start(f32[512,768]{1,0:T(8,128)} %bitcast.19), channel_id=1, source_target_pairs={{0,16},{16,32},{32,48},{48,64},{64,80},{80,96},{96,112},{112,128},... | collective-permute-start | bytes 4718600 | tf_op jit(solution)/shard_map/ppermute | solution.py:160
  2.6 1.0 slice.51
  3.5 5.1 %collective-permute-start.1 = (f32[256,256]{1,0:T(8,128)S(1)}, f32[256,256]{1,0:T(8,128)S(1)}, u32[]{:S(2)}, u32[]{:S(2)}) collective-permute-start(f32[256,256]{1,0:T(8,128)S(1)} %slice.51), channel_id=1, source_target_pairs={{0,16},{16,32},{32,48},{48,64},{64,80},{80,96},{96,112},{112,128},... | collective-permute-start | bytes 786440 | tf_op jit(solution)/shard_map/ppermute | solution.py:159
  8.7 16.7 %collective-permute-done.1 = f32[256,256]{1,0:T(8,128)S(1)} collective-permute-done((f32[256,256]{1,0:T(8,128)S(1)}, f32[256,256]{1,0:T(8,128)S(1)}, u32[]{:S(2)}, u32[]{:S(2)}) %collective-permute-start.1) | collective-permute-done | bytes 262176 | tf_op jit(solution)/shard_map/ppermute | solution.py:159
  25.4 0.0 copy-start
  25.4 1.1 %slice_subtract_fusion.2 = f32[256,256]{1,0:T(8,128)S(1)} fusion(f32[256,256]{1,0:T(8,128)S(1)} %collective-permute-done.1, f32[512,768]{1,0:T(8,128)} %bitcast.12), kind=kLoop, calls=%fused_computation.3 | loop fusion | flops 65536 | bytes 786432 | tf_op jit(solution)/shard_map/sub | solution.py:159
  26.5 11.7 %all_to_all.25 = f32[4,64,256]{2,1,0:T(8,128)S(1)} all-to-all(f32[4,64,256]{2,1,0:T(8,128)S(1)} %bitcast.18), channel_id=1, replica_groups=mesh['slab'=32,'y'=4,'x'=4] {'x'}, dimensions={0} | all-to-all | bytes 524288 | tf_op jit(solution)/shard_map/all_to_all | solution.py:131
  38.2 0.7 broadcast_in_dim.31
  38.9 4.5 %all-to-all-start.1 = ((f32[4,64,256]{2,1,0:T(8,128)}), f32[4,64,256]{2,1,0:T(8,128)S(1)}, u32[]{:S(2)}, u32[]{:S(2)}) async-start(f32[4,64,256]{2,1,0:T(8,128)} %broadcast_in_dim.31), calls=%async_computation.1 | async-start | bytes 524288 | tf_op jit(solution)/shard_map/all_to_all | solution.py:131
  43.4 6.7 %all-to-all-done.1 = f32[4,64,256]{2,1,0:T(8,128)S(1)} async-done(((f32[4,64,256]{2,1,0:T(8,128)}), f32[4,64,256]{2,1,0:T(8,128)S(1)}, u32[]{:S(2)}, u32[]{:S(2)}) %all-to-all-start.1) | async-done | bytes 262176 | tf_op jit(solution)/shard_map/all_to_all | solution.py:131
  50.1 0.7 broadcast_in_dim.33
  50.8 3.4 %all-to-all-start.2 = ((f32[4,64,256]{2,1,0:T(8,128)}), f32[4,64,256]{2,1,0:T(8,128)S(1)}, u32[]{:S(2)}, u32[]{:S(2)}) async-start(f32[4,64,256]{2,1,0:T(8,128)} %broadcast_in_dim.33), calls=%async_computation.2 | async-start | bytes 524288 | tf_op jit(solution)/shard_map/all_to_all | solution.py:131
  54.2 0.0 collective-permute-done.prev
  54.2 0.0 copy-done
  54.2 0.1 slice_subtract_fusion.1
  54.3 0.9 fusion
  55.2 5.6 %all-to-all-done.2 = f32[4,64,256]{2,1,0:T(8,128)S(1)} async-done(((f32[4,64,256]{2,1,0:T(8,128)}), f32[4,64,256]{2,1,0:T(8,128)S(1)}, u32[]{:S(2)}, u32[]{:S(2)}) %all-to-all-start.2) | async-done | bytes 262176 | tf_op jit(solution)/shard_map/all_to_all | solution.py:131
  60.8 4.2 %all-to-all-start.3 = ((f32[16,32,256]{2,1,0:T(8,128)}), f32[16,32,256]{2,1,0:T(8,128)}, u32[]{:S(2)}, u32[]{:S(2)}) async-start(f32[16,32,256]{2,1,0:T(8,128)} %bitcast.17), calls=%async_computation.3 | async-start | bytes 1048576 | tf_op jit(solution)/shard_map/all_to_all | solution.py:131
  65.1 5.1 %inverse_left.1.block = f32[256,256]{1,0:T(8,128)S(1)} custom-call(f32[256,256]{1,0:T(8,128)S(1)} %bitcast.16), custom_call_target="tpu_custom_call" | custom-call | flops 50331648 | bytes 524288 | tf_op jit(solution)/shard_map/inverse_left/pallas_call | solution.py:150
  70.2 0.0 copy-start.1
  70.2 0.7 copy-done.1
  70.9 4.4 %all-to-all-done.3 = f32[16,32,256]{2,1,0:T(8,128)} async-done(((f32[16,32,256]{2,1,0:T(8,128)}), f32[16,32,256]{2,1,0:T(8,128)}, u32[]{:S(2)}, u32[]{:S(2)}) %all-to-all-start.3) | async-done | bytes 524320 | tf_op jit(solution)/shard_map/all_to_all | solution.py:131
  75.2 0.8 slice.54
  76.1 1.1 broadcast_in_dim.34
  77.2 4.5 %all-to-all-start.4 = ((f32[16,2,32,256]{3,2,1,0:T(8,128)}), f32[16,2,32,256]{3,2,1,0:T(8,128)}, u32[]{:S(2)}, u32[]{:S(2)}) async-start(f32[16,2,32,256]{3,2,1,0:T(8,128)} %broadcast_in_dim.34), calls=%async_computation.4 | async-start | bytes 2097152 | tf_op jit(solution)/shard_map/all_to_all | solution.py:131
  81.7 0.0 copy-start.2
  81.7 0.9 copy-done.2
  82.7 4.2 %inverse_right.1.inverse0 = f32[256,256]{1,0:T(8,128)S(1)} custom-call(f32[256,256]{1,0:T(8,128)S(1)} %copy-done.2), custom_call_target="tpu_custom_call" | custom-call | flops 50331648 | bytes 524288 | tf_op jit(solution)/shard_map/inverse_right/pallas_call | solution.py:150
  86.9 8.9 %all-to-all-done.4.head = f32[16,2,32,256]{3,2,1,0:T(8,128)} async-done(((f32[16,2,32,256]{3,2,1,0:T(8,128)}), f32[16,2,32,256]{3,2,1,0:T(8,128)}, u32[]{:S(2)}, u32[]{:S(2)}) %all-to-all-start.4) | async-done | bytes 1048608 | tf_op jit(solution)/shard_map/all_to_all | solution.py:131
  95.8 14.6 %panel_update.1 = (f32[512,512]{1,0:T(8,128)}, f32[512,256]{1,0:T(8,128)}) custom-call(s32[1]{0:T(128)} %bitcast.row_index, f32[256,256]{1,0:T(8,128)S(1)} %inverse_right.1.inverse0, f32[16,2,32,256]{3,2,1,0:T(8,128)} %all-to-all-done.4.head, f32[512,768]{1,0:T(8,128)S(1)} %bitcast.15, f32[512,768]{1,0:T(8,128)S(1)} %collective-permute-done.prev), custom_call_target="tpu_custom_call" | custom-call | tf_op jit(solution)/shard_map/panel_update/pallas_call | solution.py:176
  (3 shorter events, 0.0 us)
Async XLA Ops:
  0.6 53.6 %collective-permute-start = (f32[512,768]{1,0:T(8,128)}, f32[512,768]{1,0:T(8,128)S(1)}, u32[]{:S(2)}, u32[]{:S(2)}) collective-permute-start(f32[512,768]{1,0:T(8,128)} %bitcast.19), channel_id=1, source_target_pairs={{0,16},{16,32},{32,48},{48,64},{64,80},{80,96},{96,112},{112,128},... | collective-permute-start | bytes 4718600 | tf_op jit(solution)/shard_map/ppermute | solution.py:160
  3.5 21.9 %collective-permute-start.1 = (f32[256,256]{1,0:T(8,128)S(1)}, f32[256,256]{1,0:T(8,128)S(1)}, u32[]{:S(2)}, u32[]{:S(2)}) collective-permute-start(f32[256,256]{1,0:T(8,128)S(1)} %slice.51), channel_id=1, source_target_pairs={{0,16},{16,32},{32,48},{48,64},{64,80},{80,96},{96,112},{112,128},... | collective-permute-start | bytes 786440 | tf_op jit(solution)/shard_map/ppermute | solution.py:159
  25.4 28.8 %copy-start = (f32[1,512,768]{2,1,0:T(8,128)S(1)}, f32[1,512,768]{2,1,0:T(8,128)}, u32[]{:S(2)}) copy-start(f32[1,512,768]{2,1,0:T(8,128)} %param.2) | copy-start | bytes 4718596
  38.9 11.1 %all-to-all-start.1 = ((f32[4,64,256]{2,1,0:T(8,128)}), f32[4,64,256]{2,1,0:T(8,128)S(1)}, u32[]{:S(2)}, u32[]{:S(2)}) async-start(f32[4,64,256]{2,1,0:T(8,128)} %broadcast_in_dim.31), calls=%async_computation.1 | async-start | bytes 524288 | tf_op jit(solution)/shard_map/all_to_all | solution.py:131
  50.8 10.1 %all-to-all-start.2 = ((f32[4,64,256]{2,1,0:T(8,128)}), f32[4,64,256]{2,1,0:T(8,128)S(1)}, u32[]{:S(2)}, u32[]{:S(2)}) async-start(f32[4,64,256]{2,1,0:T(8,128)} %broadcast_in_dim.33), calls=%async_computation.2 | async-start | bytes 524288 | tf_op jit(solution)/shard_map/all_to_all | solution.py:131
  60.8 14.4 %all-to-all-start.3 = ((f32[16,32,256]{2,1,0:T(8,128)}), f32[16,32,256]{2,1,0:T(8,128)}, u32[]{:S(2)}, u32[]{:S(2)}) async-start(f32[16,32,256]{2,1,0:T(8,128)} %bitcast.17), calls=%async_computation.3 | async-start | bytes 1048576 | tf_op jit(solution)/shard_map/all_to_all | solution.py:131
  70.2 0.7 copy-start.1
  77.2 18.6 %all-to-all-start.4 = ((f32[16,2,32,256]{3,2,1,0:T(8,128)}), f32[16,2,32,256]{3,2,1,0:T(8,128)}, u32[]{:S(2)}, u32[]{:S(2)}) async-start(f32[16,2,32,256]{3,2,1,0:T(8,128)} %broadcast_in_dim.34), calls=%async_computation.4 | async-start | bytes 2097152 | tf_op jit(solution)/shard_map/all_to_all | solution.py:131
  81.7 1.0 copy-start.2

commit v3 on v1

v3 whole, which is shorter than its diff:
```python
import jax
import jax.numpy as jnp
from jax import lax
from jax.experimental import pallas as pl
from jax.experimental.pallas import tpu as pltpu
from jax.sharding import PartitionSpec as P

NB = 256
PANELW = 512
COLS = 768
ACROSS = 4
STRIP = 32
SUB = 8
LANES = 128
VMEM_BYTES = 48 * 1024 * 1024


def dot(a, b, contract):
    return lax.dot_general(
        a, b, ((contract[:1], contract[1:]), ((), ())),
        precision=lax.Precision.HIGHEST, preferred_element_type=jnp.float32,
    )


def eliminate_strip(rows, first):
    groups = len(rows)
    lane = lax.broadcasted_iota(jnp.int32, (SUB, NB), 1)
    sub = lax.broadcasted_iota(jnp.int32, (SUB, NB), 0)
    for t in range(groups):
        col = first + SUB * t
        in_block = (lane >= col) & (lane < col + SUB)
        columns = [
            [jnp.broadcast_to(rows[g][:, col + j : col + j + 1], (SUB, LANES)) for j in range(SUB)]
            for g in range(t, groups)
        ]
        a = [
            [jnp.broadcast_to(columns[0][k][i : i + 1, :], (SUB, LANES)) if i >= k else None
             for k in range(SUB)]
            for i in range(SUB)
        ]
        start = jnp.where(in_block, (lane == col + sub).astype(jnp.float32), rows[t])
        u = [jnp.broadcast_to(start[i : i + 1, :], (SUB, NB)) for i in range(SUB)]
        inv = [None] * SUB
        low = [[None] * SUB for _ in range(SUB)]
        for j in range(0, SUB, 2):
            p, q = a[j][j], a[j + 1][j]
            det = p * a[j + 1][j + 1] - q * q
            inv[j] = lax.rsqrt(p)
            inv[j + 1] = (p * inv[j]) * lax.rsqrt(det)
            for k in range(j + 1, SUB):
                low[k][j] = a[k][j] * inv[j]
            for k in range(j + 2, SUB):
                low[k][j + 1] = (a[k][j + 1] - low[k][j] * low[j + 1][j]) * inv[j + 1]
                for m in range(j + 2, k + 1):
                    a[k][m] = a[k][m] - low[k][j] * low[m][j]
                    a[k][m] = a[k][m] - low[k][j + 1] * low[m][j + 1]
        wide = lambda x: jnp.concatenate([x, x], axis=1)
        for j in range(SUB):
            u[j] = u[j] * wide(inv[j])
            for k in range(j + 1, SUB):
                u[k] = u[k] - wide(low[k][j]) * u[j]
        packed = u[0]
        for j in range(1, SUB):
            packed = jnp.where(sub == j, u[j], packed)
        rows[t] = packed
        for g in range(t + 1, groups):
            col_g = columns[g - t]
            total = jnp.where(in_block, 0.0, rows[g])
            for j in range(SUB):
                col_g[j] = col_g[j] * inv[j]
                for k in range(j + 1, SUB):
                    col_g[k] = col_g[k] - col_g[j] * low[k][j]
                total = total - wide(col_g[j]) * u[j]
            rows[g] = total
    return rows


def thirds(x):
    high = x.astype(jnp.bfloat16)
    rest = x - high.astype(jnp.float32)
    middle = rest.astype(jnp.bfloat16)
    return high, middle, (rest - middle.astype(jnp.float32)).astype(jnp.bfloat16)


def gram(parts, columns):
    high, middle, low = parts
    left = jnp.concatenate([x[:, columns] for x in (high, high, middle, high, low, middle)], axis=0)
    right = jnp.concatenate([high, middle, high, low, high, middle], axis=0)
    return lax.dot_general(
        left, right, (((0,), (0,)), ((), ())), preferred_element_type=jnp.float32
    )


def invert_factor(work, between=None):
    groups = STRIP // SUB
    for half in range(NB // LANES):
        top = half * LANES
        columns = slice(top, top + LANES)
        strips = []
        for s in range(LANES // STRIP):
            first = top + STRIP * s
            after = first + STRIP
            rows = [work[first + SUB * g : first + SUB * (g + 1), :] for g in range(groups)]
            rows = eliminate_strip(rows, first)
            strip = jnp.concatenate(rows, axis=0)
            lane = lax.broadcasted_iota(jnp.int32, (STRIP, NB), 1)
            row = lax.broadcasted_iota(jnp.int32, (STRIP, NB), 0) + first
            strip = jnp.where((lane > row) & (lane < after), 0.0, strip)
            work[first:after, :] = jnp.where(lane < after, strip, 0.0)
            end = top + LANES
            if after < end:
                update = gram(thirds(strip), columns)[after - top :, :]
                lane = lax.broadcasted_iota(jnp.int32, (end - after, NB), 1)
                below = jnp.where((lane >= first) & (lane < after), 0.0, work[after:end, :])
                work[after:end, :] = below - update
            if between is not None:
                between(first // STRIP)
            strips.append(strip)
        if top + LANES < NB:
            upper = jnp.concatenate(strips, axis=0)
            lane = lax.broadcasted_iota(jnp.int32, (LANES, NB), 1)
            row = lax.broadcasted_iota(jnp.int32, (LANES, NB), 0) + top
            upper = jnp.where((lane > row) & (lane < top + LANES), 0.0, upper)
            update = gram(thirds(upper), slice(top + LANES, top + 2 * LANES))
            below = jnp.where(lane < top + LANES, 0.0, work[top + LANES :, :])
            work[top + LANES :, :] = below - update


def pack_kernel(own, prev, packed):
    value = own[...] - prev[...]
    strip_row = lax.broadcasted_iota(jnp.int32, (LANES, LANES), 0) // STRIP
    strip_col = lax.broadcasted_iota(jnp.int32, (LANES, LANES), 1) // STRIP
    packed[:LANES, :] = jnp.where(strip_row <= strip_col, value[:LANES, :LANES], value[LANES:, LANES:])
    packed[LANES : 2 * LANES, :] = value[:LANES, LANES:]
    strip = lax.broadcasted_iota(jnp.int32, (STRIP, LANES), 1) // STRIP
    diagonal = jnp.zeros((STRIP, LANES), jnp.float32)
    for i in range(LANES // STRIP):
        rows = value[LANES + STRIP * i : LANES + STRIP * (i + 1), LANES:]
        diagonal = jnp.where(strip == i, rows, diagonal)
    packed[2 * LANES :, :] = diagonal


def first_kernel(row_index, kept, one, two, three, inverse):
    packed = jnp.where(row_index[0] < ACROSS, kept[...], one[...] + two[...] + three[...])
    strip_row = lax.broadcasted_iota(jnp.int32, (LANES, LANES), 0) // STRIP
    strip_col = lax.broadcasted_iota(jnp.int32, (LANES, LANES), 1) // STRIP
    mixed = packed[:LANES, :]
    diagonal = jnp.concatenate([packed[2 * LANES :, :]] * (LANES // STRIP), axis=0)
    inverse[:LANES, :LANES] = mixed
    inverse[:LANES, LANES:] = packed[LANES : 2 * LANES, :]
    inverse[LANES:, :LANES] = jnp.zeros((LANES, LANES), jnp.float32)
    inverse[LANES:, LANES:] = jnp.where(strip_row < strip_col, mixed.T, diagonal)
    invert_factor(inverse)


def second_kernel(row_index, inverse0, head, own, prev, factor, trailing, work, middle, tail):
    x0 = inverse0[...]
    half = head.shape[0] // 2
    pick = lambda at, source: head[pl.ds(at, half), source].reshape((NB, NB))
    w1 = dot(x0, pick(0, 0), (1, 0))
    w2 = dot(x0, pick(0, 1), (1, 1))
    work[...] = pick(half, 0) - dot(w1, w1, (0, 0))
    cross = pick(half, 1) - dot(w2, w1, (0, 0))
    rows_here = own.shape[0]
    piece = rows_here // (NB // STRIP)

    def between(s):
        at = pl.ds(s * piece, piece)
        lower = dot(own[at, :NB] - prev[at, :NB], x0, (1, 1))
        factor[at, :NB] = lower
        middle[at, :] = own[at, NB:PANELW] - prev[at, NB:PANELW] - dot(lower, w1, (1, 0))
        tail[at, :] = own[at, PANELW:] - prev[at, PANELW:] - dot(lower, w2, (1, 0))

    invert_factor(work, between=between)
    x1 = work[...]
    w3 = dot(x1, cross, (1, 1))
    first_row = row_index[0] * rows_here
    row = first_row + lax.broadcasted_iota(jnp.int32, (rows_here, NB), 0)
    lower = jnp.where(row >= NB, dot(middle[...], x1, (1, 1)), 0.0)
    factor[:, NB:] = lower
    trailing[...] = jnp.where(row >= PANELW, tail[...] - dot(lower, w3, (1, 0)), 0.0)


def exchange(blocks):
    return lax.all_to_all(blocks, "row", 0, 0, tiled=True)


def head_shares(block, row_index, count):
    side = jnp.concatenate([block[:NB, :NB], block[:NB, NB:PANELW]], axis=0)
    mine = jnp.where(row_index == 1, side, block[:, NB:PANELW])
    return mine.reshape(count, -1, NB)


def per_device(schur_own, outgoing):
    own = schur_own[0]
    out = outgoing[0]
    rows_here = own.shape[0]
    count = lax.axis_size("row")
    row_index = lax.axis_index("row").astype(jnp.int32)
    pairs = [(s, s + 1) for s in range(lax.axis_size("slab") - 1)]
    vmem = pl.BlockSpec(memory_space=pltpu.VMEM)
    smem = pl.BlockSpec(memory_space=pltpu.SMEM)
    params = pltpu.CompilerParams(vmem_limit_bytes=VMEM_BYTES)

    prev_corner = lax.ppermute(out[:NB, :NB], "slab", pairs)
    corner = pl.BlockSpec((NB, NB), lambda i: (0, 0))
    packed_rows = 2 * LANES + STRIP
    packed = pl.pallas_call(
        pack_kernel,
        grid=(1,),
        out_shape=jax.ShapeDtypeStruct((packed_rows, LANES), jnp.float32),
        in_specs=[corner, corner],
        out_specs=pl.BlockSpec((packed_rows, LANES), lambda i: (0, 0)),
        compiler_params=params,
        name="pack_corner",
    )(own, prev_corner)
    sent = [lax.ppermute(packed, "row", [(0, d)]) for d in (2, 1, 3)]
    out_shares, _ = lax.optimization_barrier((head_shares(out, row_index, count), prev_corner))
    prev_shares = lax.ppermute(out_shares, "slab", pairs)
    kept = jnp.where(row_index == 0, packed, sent[0] + sent[1] + sent[2])
    kept, prev_shares = lax.optimization_barrier((kept, prev_shares))
    down = [
        lax.ppermute(kept, "row", [(x, ACROSS * d + x) for x in range(ACROSS)]) for d in (2, 1, 3)
    ]
    shares = exchange(head_shares(own, row_index, count) - prev_shares)[:2]
    *down, shares = lax.optimization_barrier((*down, shares))
    head = exchange(jnp.broadcast_to(shares[None], (count,) + shares.shape))
    out, _ = lax.optimization_barrier((out, kept))
    prev = lax.ppermute(out, "slab", pairs)

    inverse0 = pl.pallas_call(
        first_kernel,
        out_shape=jax.ShapeDtypeStruct((NB, NB), jnp.float32),
        in_specs=[smem] + [vmem] * 4,
        out_specs=vmem,
        compiler_params=params,
        cost_estimate=pl.CostEstimate(
            flops=400 * NB**3, bytes_accessed=8 * NB**2, transcendentals=NB),
        name="panel_inverse",
    )(row_index[None], kept, *down)

    factor, trailing = pl.pallas_call(
        second_kernel,
        out_shape=(
            jax.ShapeDtypeStruct((rows_here, PANELW), jnp.float32),
            jax.ShapeDtypeStruct((rows_here, COLS - PANELW), jnp.float32),
        ),
        in_specs=[smem] + [vmem] * 4,
        out_specs=(vmem, vmem),
        scratch_shapes=[
            pltpu.VMEM((NB, NB), jnp.float32),
            pltpu.VMEM((rows_here, NB), jnp.float32),
            pltpu.VMEM((rows_here, NB), jnp.float32),
        ],
        compiler_params=params,
        name="panel_update",
    )(row_index[None], inverse0, head, own, prev)
    return factor[None], trailing[None]


def solution(mesh):
    specs = (P("slab", "row", None), P("slab", "row", None))
    return jax.shard_map(
        per_device, mesh=mesh, in_specs=specs, out_specs=specs, check_vma=False
    )
```

time: 102 us -> 90.1 us (0.88)
  the two profiles are of different devices: /device:TPU:99 before, /device:TPU:224 now
where the time goes in v3:
time: 90.1 us; the launch traced here: 89.4 us
  starting transfers between devices  35.8 us (40%)
  waiting for transfers between devices  27.4 us (30%)
  Pallas kernels  21 us (23%)
  local copies, waits for them, and re-layouts  2.32 us (3%)
  other arithmetic  2.07 us (2%)
    all_to_all x2, waiting for transfers between devices, exchange(): return lax.all_to_all(blocks, 'row', 0, 0, tiled=True)  17.1 us
    pallas_call x1, Pallas kernels, per_device(): pl.pallas_call(second_kernel, out_shape=(jax.ShapeDtypeStruct((rows_here,...  13.5 us
    all_to_all x2, starting transfers between devices, exchange(): return lax.all_to_all(blocks, 'row', 0, 0, tiled=True)  11.5 us
    ppermute x3, starting transfers between devices, per_device(): lax.ppermute(kept, 'row', [(x, ACROSS * d + x) for x in range(ACROSS)])  7.64 us
    pallas_call x1, Pallas kernels, per_device(): pl.pallas_call(first_kernel, out_shape=jax.ShapeDtypeStruct((NB, NB), jnp...  7.46 us
    ppermute x3, starting transfers between devices, per_device(): sent = [lax.ppermute(packed, 'row', [(0, d)]) for d in (2, 1, 3)]  7.27 us
    ppermute x1, starting transfers between devices, per_device(): prev = lax.ppermute(out, 'slab', pairs)  4.81 us
    ppermute x1, waiting for transfers between devices, per_device(): prev_corner = lax.ppermute(out[:NB, :NB], 'slab', pairs)  4.64 us
  transfers between devices with their start and end apart: 11, of which 7 were waited for; matrix products, arithmetic and copies ran while one was open for 4% of the time, Pallas kernels for 8%

profile of v3, /device:TPU:224, one launch (start us, length us, event | category | flops | bytes accessed | tf_op | source)
XLA Modules:
  0.0 89.4 jit_solution(10131858322427012062)
XLA Ops:
  0.6 0.0 copy-start
  0.6 1.2 %fusion.1 = (f32[256,256]{1,0:T(8,128)S(1)}, f32[256,256]{1,0:T(8,128)S(1)}) fusion(f32[512,768]{1,0:T(8,128)} %bitcast.2), kind=kLoop, calls=%fused_computation.4 | loop fusion | bytes 1048576 | tf_op jit(solution)/shard_map/slice | solution.py:189
  1.8 1.9 %collective-permute-start = (f32[256,256]{1,0:T(8,128)S(1)}, f32[256,256]{1,0:T(8,128)S(1)}, u32[]{:S(2)}, u32[]{:S(2)}) collective-permute-start(f32[256,256]{1,0:T(8,128)S(1)} %get-tuple-element.25), channel_id=1, source_target_pairs={{0,16},{16,32},{32,48},{48,64},{64,80},{80,96},{96,112},{112,128},... | collective-permute-start | bytes 786440 | tf_op jit(solution)/shard_map/ppermute | solution.py:205
  3.8 1.1 %slice_select_fusion.1 = f32[512,256]{1,0:T(8,128)S(1)} fusion(f32[512,768]{1,0:T(8,128)} %bitcast.2, f32[256,256]{1,0:T(8,128)S(1)} %get-tuple-element.24, f32[256,256]{1,0:T(8,128)S(1)} %get-tuple-element.25, pred[]{:T(512)S(6)} %eq.8), kind=kLoop, calls=%fused_computation.1 | loop fusion | flops 262144 | bytes 1572865 | tf_op jit(solution)/shard_map/jit(_where)/select_n | solution.py:190
  4.9 4.6 %collective-permute-done.prev = f32[256,256]{1,0:T(8,128)S(1)} collective-permute-done((f32[256,256]{1,0:T(8,128)S(1)}, f32[256,256]{1,0:T(8,128)S(1)}, u32[]{:S(2)}, u32[]{:S(2)}) %collective-permute-start) | collective-permute-done | bytes 262176 | tf_op jit(solution)/shard_map/ppermute | solution.py:205
  9.5 2.7 %collective-permute-start.4 = (f32[16,32,256]{2,1,0:T(8,128)S(1)}, f32[16,32,256]{2,1,0:T(8,128)S(1)}, u32[]{:S(2)}, u32[]{:S(2)}) collective-permute-start(f32[16,32,256]{2,1,0:T(8,128)S(1)} %bitcast.12), channel_id=1, source_target_pairs={{0,16},{16,32},{32,48},{48,64},{64,80},{80,96},{96,112},{112,128},... | collective-permute-start | bytes 1572872 | tf_op jit(solution)/shard_map/ppermute | solution.py:219
  12.2 0.0 copy-done
  12.2 4.7 %collective-permute-start.3 = (f32[288,128]{1,0:T(8,128)S(1)}, f32[288,128]{1,0:T(8,128)S(1)}, u32[]{:S(2)}, u32[]{:S(2)}) collective-permute-start(f32[288,128]{1,0:T(8,128)S(1)} %pack_corner.1), channel_id=1, source_target_pairs={{0,3},{16,19},{32,35},{48,51},{64,67},{80,83},{96,99},{112,115},{1... | collective-permute-start | bytes 442376 | tf_op jit(solution)/shard_map/ppermute | solution.py:217
  16.9 1.3 %collective-permute-start.2 = (f32[288,128]{1,0:T(8,128)S(1)}, f32[288,128]{1,0:T(8,128)S(1)}, u32[]{:S(2)}, u32[]{:S(2)}) collective-permute-start(f32[288,128]{1,0:T(8,128)S(1)} %pack_corner.1), channel_id=1, source_target_pairs={{0,1},{16,17},{32,33},{48,49},{64,65},{80,81},{96,97},{112,113},{1... | collective-permute-start | bytes 442376 | tf_op jit(solution)/shard_map/ppermute | solution.py:217
  18.2 1.3 %collective-permute-start.1 = (f32[288,128]{1,0:T(8,128)S(1)}, f32[288,128]{1,0:T(8,128)S(1)}, u32[]{:S(2)}, u32[]{:S(2)}) collective-permute-start(f32[288,128]{1,0:T(8,128)S(1)} %pack_corner.1), channel_id=1, source_target_pairs={{0,2},{16,18},{32,34},{48,50},{64,66},{80,82},{96,98},{112,114},{1... | collective-permute-start | bytes 442376 | tf_op jit(solution)/shard_map/ppermute | solution.py:217
  19.6 0.0 collective-permute-done.3
  19.6 1.3 %collective-permute-done.2 = f32[288,128]{1,0:T(8,128)S(1)} collective-permute-done((f32[288,128]{1,0:T(8,128)S(1)}, f32[288,128]{1,0:T(8,128)S(1)}, u32[]{:S(2)}, u32[]{:S(2)}) %collective-permute-start.2) | collective-permute-done | bytes 147488 | tf_op jit(solution)/shard_map/ppermute | solution.py:217
  20.9 1.9 %collective-permute-done.1 = f32[288,128]{1,0:T(8,128)S(1)} collective-permute-done((f32[288,128]{1,0:T(8,128)S(1)}, f32[288,128]{1,0:T(8,128)S(1)}, u32[]{:S(2)}, u32[]{:S(2)}) %collective-permute-start.1) | collective-permute-done | bytes 147488 | tf_op jit(solution)/shard_map/ppermute | solution.py:217
  22.8 0.0 collective-permute-done.4
  22.9 4.8 %collective-permute-start.8 = (f32[512,768]{1,0:T(8,128)}, f32[512,768]{1,0:T(8,128)}, u32[]{:S(2)}, u32[]{:S(2)}) collective-permute-start(f32[512,768]{1,0:T(8,128)} %bitcast.2), channel_id=1, source_target_pairs={{0,16},{16,32},{32,48},{48,64},{64,80},{80,96},{96,112},{112,128},... | collective-permute-start | bytes 4718600 | tf_op jit(solution)/shard_map/ppermute | solution.py:229
  27.7 0.1 slice_select_fusion
  27.8 0.9 sub.3
  28.6 5.1 %all-to-all-start = ((f32[16,32,256]{2,1,0:T(8,128)}), f32[16,32,256]{2,1,0:T(8,128)S(1)}, u32[]{:S(2)}, u32[]{:S(2)}) async-start(f32[16,32,256]{2,1,0:T(8,128)} %sub.3), calls=%async_computation | async-start | bytes 1048576 | tf_op jit(solution)/shard_map/all_to_all | solution.py:185
  33.7 5.0 %collective-permute-start.7 = (f32[288,128]{1,0:T(8,128)S(1)}, f32[288,128]{1,0:T(8,128)S(1)}, u32[]{:S(2)}, u32[]{:S(2)}) collective-permute-start(f32[288,128]{1,0:T(8,128)S(1)} %add_select_fusion.kept), channel_id=1, source_target_pairs={{0,12},{1,13},{2,14},{3,15},{16,28},{17,29},{18,30},{19,31},{32,44... | collective-permute-start | bytes 442376 | tf_op jit(solution)/shard_map/ppermute | solution.py:223
  38.7 1.3 %collective-permute-start.6 = (f32[288,128]{1,0:T(8,128)S(1)}, f32[288,128]{1,0:T(8,128)S(1)}, u32[]{:S(2)}, u32[]{:S(2)}) collective-permute-start(f32[288,128]{1,0:T(8,128)S(1)} %add_select_fusion.kept), channel_id=1, source_target_pairs={{0,4},{1,5},{2,6},{3,7},{16,20},{17,21},{18,22},{19,23},{32,36},{3... | collective-permute-start | bytes 442376 | tf_op jit(solution)/shard_map/ppermute | solution.py:223
  40.0 1.3 %collective-permute-start.5 = (f32[288,128]{1,0:T(8,128)S(1)}, f32[288,128]{1,0:T(8,128)S(1)}, u32[]{:S(2)}, u32[]{:S(2)}) collective-permute-start(f32[288,128]{1,0:T(8,128)S(1)} %add_select_fusion.kept), channel_id=1, source_target_pairs={{0,8},{1,9},{2,10},{3,11},{16,24},{17,25},{18,26},{19,27},{32,40},... | collective-permute-start | bytes 442376 | tf_op jit(solution)/shard_map/ppermute | solution.py:223
  41.4 3.7 %all-to-all-done = f32[16,32,256]{2,1,0:T(8,128)S(1)} async-done(((f32[16,32,256]{2,1,0:T(8,128)}), f32[16,32,256]{2,1,0:T(8,128)S(1)}, u32[]{:S(2)}, u32[]{:S(2)}) %all-to-all-start) | async-done | bytes 524320 | tf_op jit(solution)/shard_map/all_to_all | solution.py:185
  45.1 0.3 collective-permute-done.7.three
  45.4 0.0 collective-permute-done.6.two
  45.4 2.0 %collective-permute-done.5.one = f32[288,128]{1,0:T(8,128)S(1)} collective-permute-done((f32[288,128]{1,0:T(8,128)S(1)}, f32[288,128]{1,0:T(8,128)S(1)}, u32[]{:S(2)}, u32[]{:S(2)}) %collective-permute-start.5) | collective-permute-done | bytes 147488 | tf_op jit(solution)/shard_map/ppermute | solution.py:223
  47.4 1.1 %broadcast_in_dim.17 = f32[16,2,32,256]{3,2,1,0:T(8,128)} broadcast(f32[2,32,256]{2,1,0:T(8,128)S(1)} %slice.35), dimensions={1,2,3} | broadcast | bytes 1114112 | tf_op jit(solution)/shard_map/broadcast_in_dim | solution.py:227
  48.5 6.4 %all-to-all-start.1 = ((f32[16,2,32,256]{3,2,1,0:T(8,128)}), f32[16,2,32,256]{3,2,1,0:T(8,128)S(1)}, u32[]{:S(2)}, u32[]{:S(2)}) async-start(f32[16,2,32,256]{3,2,1,0:T(8,128)} %broadcast_in_dim.17), calls=%async_computation.1 | async-start | bytes 2097152 | tf_op jit(solution)/shard_map/all_to_all | solution.py:185
  55.0 7.5 %panel_inverse.1.inverse0 = f32[256,256]{1,0:T(8,128)S(1)} custom-call(s32[1]{0:T(128)} %bitcast.row_index, f32[288,128]{1,0:T(8,128)S(1)} %add_select_fusion.kept, f32[288,128]{1,0:T(8,128)S(1)} %collective-permute-done.5.one, f32[288,128]{1,0:T(8,128)S(1)} %collective-permute-done.6.two, f32[288,128]{1,0:T(8,128)S(1)} %collective-permute-done.7.three), custom_call_target="tpu_custom_call" | custom-call | flops 6710886400 | bytes 524288 | tf_op jit(solution)/shard_map/panel_inverse/pallas_call | solution.py:231
  62.4 13.4 %all-to-all-done.1.head = f32[16,2,32,256]{3,2,1,0:T(8,128)S(1)} async-done(((f32[16,2,32,256]{3,2,1,0:T(8,128)}), f32[16,2,32,256]{3,2,1,0:T(8,128)S(1)}, u32[]{:S(2)}, u32[]{:S(2)}) %all-to-all-start.1) | async-done | bytes 1048608 | tf_op jit(solution)/shard_map/all_to_all | solution.py:185
  75.8 0.0 collective-permute-done.8.prev
  75.9 13.5 %panel_update.1 = (f32[512,512]{1,0:T(8,128)}, f32[512,256]{1,0:T(8,128)}) custom-call(s32[1]{0:T(128)} %bitcast.row_index, f32[256,256]{1,0:T(8,128)S(1)} %panel_inverse.1.inverse0, f32[16,2,32,256]{3,2,1,0:T(8,128)S(1)} %all-to-all-done.1.head, f32[512,768]{1,0:T(8,128)S(1)} %bitcast.10, f32[512,768]{1,0:T(8,128)} %collective-permute-done.8.prev), custom_call_target="tpu_custom_call" | custom-call | tf_op jit(solution)/shard_map/panel_update/pallas_call | solution.py:242
  (4 shorter events, 0.1 us)
Async XLA Ops:
  0.6 11.6 %copy-start = (f32[1,512,768]{2,1,0:T(8,128)S(1)}, f32[1,512,768]{2,1,0:T(8,128)}, u32[]{:S(2)}) copy-start(f32[1,512,768]{2,1,0:T(8,128)} %param.2) | copy-start | bytes 4718596
  1.8 7.7 %collective-permute-start = (f32[256,256]{1,0:T(8,128)S(1)}, f32[256,256]{1,0:T(8,128)S(1)}, u32[]{:S(2)}, u32[]{:S(2)}) collective-permute-start(f32[256,256]{1,0:T(8,128)S(1)} %get-tuple-element.25), channel_id=1, source_target_pairs={{0,16},{16,32},{32,48},{48,64},{64,80},{80,96},{96,112},{112,128},... | collective-permute-start | bytes 786440 | tf_op jit(solution)/shard_map/ppermute | solution.py:205
  9.5 13.3 %collective-permute-start.4 = (f32[16,32,256]{2,1,0:T(8,128)S(1)}, f32[16,32,256]{2,1,0:T(8,128)S(1)}, u32[]{:S(2)}, u32[]{:S(2)}) collective-permute-start(f32[16,32,256]{2,1,0:T(8,128)S(1)} %bitcast.12), channel_id=1, source_target_pairs={{0,16},{16,32},{32,48},{48,64},{64,80},{80,96},{96,112},{112,128},... | collective-permute-start | bytes 1572872 | tf_op jit(solution)/shard_map/ppermute | solution.py:219
  12.2 7.3 %collective-permute-start.3 = (f32[288,128]{1,0:T(8,128)S(1)}, f32[288,128]{1,0:T(8,128)S(1)}, u32[]{:S(2)}, u32[]{:S(2)}) collective-permute-start(f32[288,128]{1,0:T(8,128)S(1)} %pack_corner.1), channel_id=1, source_target_pairs={{0,3},{16,19},{32,35},{48,51},{64,67},{80,83},{96,99},{112,115},{1... | collective-permute-start | bytes 442376 | tf_op jit(solution)/shard_map/ppermute | solution.py:217
  16.9 4.0 %collective-permute-start.2 = (f32[288,128]{1,0:T(8,128)S(1)}, f32[288,128]{1,0:T(8,128)S(1)}, u32[]{:S(2)}, u32[]{:S(2)}) collective-permute-start(f32[288,128]{1,0:T(8,128)S(1)} %pack_corner.1), channel_id=1, source_target_pairs={{0,1},{16,17},{32,33},{48,49},{64,65},{80,81},{96,97},{112,113},{1... | collective-permute-start | bytes 442376 | tf_op jit(solution)/shard_map/ppermute | solution.py:217
  18.2 4.6 %collective-permute-start.1 = (f32[288,128]{1,0:T(8,128)S(1)}, f32[288,128]{1,0:T(8,128)S(1)}, u32[]{:S(2)}, u32[]{:S(2)}) collective-permute-start(f32[288,128]{1,0:T(8,128)S(1)} %pack_corner.1), channel_id=1, source_target_pairs={{0,2},{16,18},{32,34},{48,50},{64,66},{80,82},{96,98},{112,114},{1... | collective-permute-start | bytes 442376 | tf_op jit(solution)/shard_map/ppermute | solution.py:217
  22.9 53.0 %collective-permute-start.8 = (f32[512,768]{1,0:T(8,128)}, f32[512,768]{1,0:T(8,128)}, u32[]{:S(2)}, u32[]{:S(2)}) collective-permute-start(f32[512,768]{1,0:T(8,128)} %bitcast.2), channel_id=1, source_target_pairs={{0,16},{16,32},{32,48},{48,64},{64,80},{80,96},{96,112},{112,128},... | collective-permute-start | bytes 4718600 | tf_op jit(solution)/shard_map/ppermute | solution.py:229
  28.6 16.4 %all-to-all-start = ((f32[16,32,256]{2,1,0:T(8,128)}), f32[16,32,256]{2,1,0:T(8,128)S(1)}, u32[]{:S(2)}, u32[]{:S(2)}) async-start(f32[16,32,256]{2,1,0:T(8,128)} %sub.3), calls=%async_computation | async-start | bytes 1048576 | tf_op jit(solution)/shard_map/all_to_all | solution.py:185
  33.7 11.7 %collective-permute-start.7 = (f32[288,128]{1,0:T(8,128)S(1)}, f32[288,128]{1,0:T(8,128)S(1)}, u32[]{:S(2)}, u32[]{:S(2)}) collective-permute-start(f32[288,128]{1,0:T(8,128)S(1)} %add_select_fusion.kept), channel_id=1, source_target_pairs={{0,12},{1,13},{2,14},{3,15},{16,28},{17,29},{18,30},{19,31},{32,44... | collective-permute-start | bytes 442376 | tf_op jit(solution)/shard_map/ppermute | solution.py:223
  38.7 6.7 %collective-permute-start.6 = (f32[288,128]{1,0:T(8,128)S(1)}, f32[288,128]{1,0:T(8,128)S(1)}, u32[]{:S(2)}, u32[]{:S(2)}) collective-permute-start(f32[288,128]{1,0:T(8,128)S(1)} %add_select_fusion.kept), channel_id=1, source_target_pairs={{0,4},{1,5},{2,6},{3,7},{16,20},{17,21},{18,22},{19,23},{32,36},{3... | collective-permute-start | bytes 442376 | tf_op jit(solution)/shard_map/ppermute | solution.py:223
  40.0 7.4 %collective-permute-start.5 = (f32[288,128]{1,0:T(8,128)S(1)}, f32[288,128]{1,0:T(8,128)S(1)}, u32[]{:S(2)}, u32[]{:S(2)}) collective-permute-start(f32[288,128]{1,0:T(8,128)S(1)} %add_select_fusion.kept), channel_id=1, source_target_pairs={{0,8},{1,9},{2,10},{3,11},{16,24},{17,25},{18,26},{19,27},{32,40},... | collective-permute-start | bytes 442376 | tf_op jit(solution)/shard_map/ppermute | solution.py:223
  48.5 27.3 %all-to-all-start.1 = ((f32[16,2,32,256]{3,2,1,0:T(8,128)}), f32[16,2,32,256]{3,2,1,0:T(8,128)S(1)}, u32[]{:S(2)}, u32[]{:S(2)}) async-start(f32[16,2,32,256]{3,2,1,0:T(8,128)} %broadcast_in_dim.17), calls=%async_computation.1 | async-start | bytes 2097152 | tf_op jit(solution)/shard_map/all_to_all | solution.py:185

commit v4 on v3

--- a/solution.py
+++ b/solution.py
@@ -127,7 +127,7 @@
 
 
 def pack_kernel(own, prev, packed):
-    value = own[...] - prev[...]
+    value = own[...] - prev[...].reshape((NB, NB))
     strip_row = lax.broadcasted_iota(jnp.int32, (LANES, LANES), 0) // STRIP
     strip_col = lax.broadcasted_iota(jnp.int32, (LANES, LANES), 1) // STRIP
     packed[:LANES, :] = jnp.where(strip_row <= strip_col, value[:LANES, :LANES], value[LANES:, LANES:])
@@ -153,32 +153,57 @@
     invert_factor(inverse)
 
 
-def second_kernel(row_index, inverse0, head, own, prev, factor, trailing, work, middle, tail):
+def second_kernel(
+    row_index, inverse0, head, own, prev, factor, trailing,
+    work, before, middle, left, right, tail, arrive, leave,
+):
+    fetch = pltpu.make_async_copy(prev, before, arrive)
+    fetch.start()
     x0 = inverse0[...]
     half = head.shape[0] // 2
     pick = lambda at, source: head[pl.ds(at, half), source].reshape((NB, NB))
     w1 = dot(x0, pick(0, 0), (1, 0))
+    work[...] = pick(half, 0) - dot(w1, w1, (0, 0))
     w2 = dot(x0, pick(0, 1), (1, 1))
-    work[...] = pick(half, 0) - dot(w1, w1, (0, 0))
     cross = pick(half, 1) - dot(w2, w1, (0, 0))
     rows_here = own.shape[0]
-    piece = rows_here // (NB // STRIP)
+    steps = LANES // STRIP
+    piece = rows_here // steps
+    row = row_index[0] * rows_here + lax.broadcasted_iota(jnp.int32, (rows_here, NB), 0)
+    window = []
+    writes = [
+        pltpu.make_async_copy(left, factor.at[:, pl.ds(0, NB)], leave.at[0]),
+        pltpu.make_async_copy(right, factor.at[:, pl.ds(NB, NB)], leave.at[1]),
+        pltpu.make_async_copy(tail, trailing, leave.at[2]),
+    ]
 
     def between(s):
-        at = pl.ds(s * piece, piece)
-        lower = dot(own[at, :NB] - prev[at, :NB], x0, (1, 1))
-        factor[at, :NB] = lower
-        middle[at, :] = own[at, NB:PANELW] - prev[at, NB:PANELW] - dot(lower, w1, (1, 0))
-        tail[at, :] = own[at, PANELW:] - prev[at, PANELW:] - dot(lower, w2, (1, 0))
-
-    invert_factor(work, between=between)
-    x1 = work[...]
-    w3 = dot(x1, cross, (1, 1))
-    first_row = row_index[0] * rows_here
-    row = first_row + lax.broadcasted_iota(jnp.int32, (rows_here, NB), 0)
-    lower = jnp.where(row >= NB, dot(middle[...], x1, (1, 1)), 0.0)
-    factor[:, NB:] = lower
-    trailing[...] = jnp.where(row >= PANELW, tail[...] - dot(lower, w3, (1, 0)), 0.0)
+        at = pl.ds(s % steps * piece, piece)
+        if s == 0:
+            fetch.wait()
+        if s < steps:
+            lower = dot(own[at, :NB] - before[at, :NB], x0, (1, 1))
+            left[at, :] = lower
+            middle[at, :] = own[at, NB:PANELW] - before[at, NB:PANELW] - dot(lower, w1, (1, 0))
+            tail[at, :] = own[at, PANELW:] - before[at, PANELW:] - dot(lower, w2, (1, 0))
+            return
+        if s == steps:
+            writes[0].start()
+            window.append(dot(work[:LANES, :LANES], cross[:, :LANES], (1, 1)))
+        lower = dot(middle[at, :LANES], work[:LANES, :LANES], (1, 1))
+        right[at, :LANES] = jnp.where(row[s % steps * piece :][:piece, :LANES] >= NB, lower, 0.0)
+        tail[at, :] = tail[at, :] - dot(lower, window[0], (1, 0))
+
+    invert_factor(work, between)
+    x1 = work[LANES:, :]
+    rest = dot(x1, cross, (1, 1))
+    lower = dot(middle[...], x1, (1, 1))
+    right[:, LANES:] = jnp.where(row[:, :LANES] >= NB, lower, 0.0)
+    writes[1].start()
+    tail[...] = jnp.where(row >= PANELW, tail[...] - dot(lower, rest, (1, 0)), 0.0)
+    writes[2].start()
+    for write in writes:
+        write.wait()
 
 
 def exchange(blocks):
@@ -202,28 +227,29 @@
     smem = pl.BlockSpec(memory_space=pltpu.SMEM)
     params = pltpu.CompilerParams(vmem_limit_bytes=VMEM_BYTES)
 
-    prev_corner = lax.ppermute(out[:NB, :NB], "slab", pairs)
-    corner = pl.BlockSpec((NB, NB), lambda i: (0, 0))
+    part = (PANELW // count, NB // count)
+    corner = out[:NB, :NB].reshape(count, part[1], NB)
+    sent = jnp.concatenate([head_shares(out, row_index, count), corner], axis=1)
+    came = lax.ppermute(sent, "slab", pairs)
+    shares = exchange(head_shares(own, row_index, count) - came[:, : part[0]])[:2]
     packed_rows = 2 * LANES + STRIP
     packed = pl.pallas_call(
         pack_kernel,
         grid=(1,),
         out_shape=jax.ShapeDtypeStruct((packed_rows, LANES), jnp.float32),
-        in_specs=[corner, corner],
+        in_specs=[
+            pl.BlockSpec((NB, NB), lambda i: (0, 0)),
+            pl.BlockSpec((count, part[1], NB), lambda i: (0, part[0] // part[1], 0)),
+        ],
         out_specs=pl.BlockSpec((packed_rows, LANES), lambda i: (0, 0)),
         compiler_params=params,
         name="pack_corner",
-    )(own, prev_corner)
-    sent = [lax.ppermute(packed, "row", [(0, d)]) for d in (2, 1, 3)]
-    out_shares, _ = lax.optimization_barrier((head_shares(out, row_index, count), prev_corner))
-    prev_shares = lax.ppermute(out_shares, "slab", pairs)
-    kept = jnp.where(row_index == 0, packed, sent[0] + sent[1] + sent[2])
-    kept, prev_shares = lax.optimization_barrier((kept, prev_shares))
+    )(own, came)
+    along = [lax.ppermute(packed, "row", [(0, d)]) for d in (2, 1, 3)]
+    kept = jnp.where(row_index == 0, packed, along[0] + along[1] + along[2])
     down = [
         lax.ppermute(kept, "row", [(x, ACROSS * d + x) for x in range(ACROSS)]) for d in (2, 1, 3)
     ]
-    shares = exchange(head_shares(own, row_index, count) - prev_shares)[:2]
-    *down, shares = lax.optimization_barrier((*down, shares))
     head = exchange(jnp.broadcast_to(shares[None], (count,) + shares.shape))
     out, _ = lax.optimization_barrier((out, kept))
     prev = lax.ppermute(out, "slab", pairs)
@@ -245,13 +271,14 @@
             jax.ShapeDtypeStruct((rows_here, PANELW), jnp.float32),
             jax.ShapeDtypeStruct((rows_here, COLS - PANELW), jnp.float32),
         ),
-        in_specs=[smem] + [vmem] * 4,
-        out_specs=(vmem, vmem),
+        in_specs=[smem] + [vmem] * 3 + [pl.BlockSpec(memory_space=pl.ANY)],
+        out_specs=(pl.BlockSpec(memory_space=pl.ANY), pl.BlockSpec(memory_space=pl.ANY)),
         scratch_shapes=[
             pltpu.VMEM((NB, NB), jnp.float32),
-            pltpu.VMEM((rows_here, NB), jnp.float32),
-            pltpu.VMEM((rows_here, NB), jnp.float32),
-        ],
+            pltpu.VMEM((rows_here, COLS), jnp.float32),
+        ]
+        + [pltpu.VMEM((rows_here, NB), jnp.float32)] * 4
+        + [pltpu.SemaphoreType.DMA, pltpu.SemaphoreType.DMA((3,))],
         compiler_params=params,
         name="panel_update",
     )(row_index[None], inverse0, head, own, prev)

time: 90.1 us -> 94.4 us (1.048)
  the two profiles are of different devices: /device:TPU:224 before, /device:TPU:113 now
where the time goes in v4:
time: 94.4 us; the launch traced here: 93.9 us
  waiting for transfers between devices  25.9 us (27%)
  blocking collectives  22.2 us (24%)
  starting transfers between devices  21.4 us (23%)
  Pallas kernels  20 us (21%)
  local copies, waits for them, and re-layouts  2.21 us (2%)
  other arithmetic  1.46 us (2%)
    all_to_all x1, blocking collectives, exchange(): return lax.all_to_all(blocks, 'row', 0, 0, tiled=True)  22.2 us
    ppermute x3, waiting for transfers between devices, per_device(): lax.ppermute(kept, 'row', [(x, ACROSS * d + x) for x in range(ACROSS)])  17 us
    pallas_call x1, Pallas kernels, per_device(): pl.pallas_call(second_kernel, out_shape=(jax.ShapeDtypeStruct((rows_here,...  12.5 us
    ppermute x1, waiting for transfers between devices, per_device(): came = lax.ppermute(sent, 'slab', pairs)  8.85 us
    pallas_call x1, Pallas kernels, per_device(): pl.pallas_call(first_kernel, out_shape=jax.ShapeDtypeStruct((NB, NB), jnp...  7.46 us
    all_to_all x1, starting transfers between devices, exchange(): return lax.all_to_all(blocks, 'row', 0, 0, tiled=True)  5.89 us
    ppermute x1, starting transfers between devices, per_device(): prev = lax.ppermute(out, 'slab', pairs)  5.6 us
    ppermute x1, starting transfers between devices, per_device(): came = lax.ppermute(sent, 'slab', pairs)  5.32 us
  transfers between devices with their start and end apart: 9, of which 2 were waited for; matrix products, arithmetic and copies ran while one was open for 1% of the time, Pallas kernels for 8%

profile of v4, /device:TPU:113, one launch (start us, length us, event | category | flops | bytes accessed | tf_op | source)
XLA Modules:
  0.0 93.9 jit_solution(17954322803634915297)
XLA Ops:
  0.6 1.1 %fusion.1 = (f32[256,256]{1,0:T(8,128)S(1)}, f32[256,256]{1,0:T(8,128)S(1)}) fusion(f32[512,768]{1,0:T(8,128)} %bitcast.2), kind=kLoop, calls=%fused_computation.6 | loop fusion | bytes 1048576 | tf_op jit(solution)/shard_map/slice | solution.py:214
  1.7 0.0 copy-start
  1.7 1.2 %slice_select_fusion.1 = f32[512,256]{1,0:T(8,128)S(1)} fusion(f32[512,768]{1,0:T(8,128)} %bitcast.2, f32[256,256]{1,0:T(8,128)S(1)} %get-tuple-element.10, f32[256,256]{1,0:T(8,128)S(1)} %get-tuple-element.11, pred[]{:T(512)S(6)} %eq.8), kind=kLoop, calls=%fused_computation.3 | loop fusion | flops 262144 | bytes 1572865 | tf_op jit(solution)/shard_map/jit(_where)/select_n | solution.py:215
  3.0 0.1 pad_maximum_fusion
  3.0 5.3 %collective-permute-start = (f32[16,48,256]{2,1,0:T(8,128)S(1)}, f32[16,48,256]{2,1,0:T(8,128)S(1)}, u32[]{:S(2)}, u32[]{:S(2)}) collective-permute-start(f32[16,48,256]{2,1,0:T(8,128)S(1)} %pad_maximum_fusion), channel_id=1, source_target_pairs={{0,16},{16,32},{32,48},{48,64},{64,80},{80,96},{96,112},{112,128},... | collective-permute-start | bytes 2359304 | tf_op jit(solution)/shard_map/ppermute | solution.py:233
  8.4 0.0 copy-done
  8.4 8.9 %collective-permute-done.prev = f32[16,48,256]{2,1,0:T(8,128)S(1)} collective-permute-done((f32[16,48,256]{2,1,0:T(8,128)S(1)}, f32[16,48,256]{2,1,0:T(8,128)S(1)}, u32[]{:S(2)}, u32[]{:S(2)}) %collective-permute-start) | collective-permute-done | bytes 786464 | tf_op jit(solution)/shard_map/ppermute | solution.py:233
  17.3 0.7 collective-permute-start.3
  18.0 0.7 collective-permute-start.2
  18.6 0.7 collective-permute-start.1
  19.3 0.1 slice_select_fusion
  19.4 0.0 collective-permute-done.3
  19.4 0.0 collective-permute-done.2
  19.4 0.0 collective-permute-done.1
  19.5 5.6 %collective-permute-start.7 = (f32[512,768]{1,0:T(8,128)}, f32[512,768]{1,0:T(8,128)}, u32[]{:S(2)}, u32[]{:S(2)}) collective-permute-start(f32[512,768]{1,0:T(8,128)} %bitcast.2), channel_id=1, source_target_pairs={{0,16},{16,32},{32,48},{48,64},{64,80},{80,96},{96,112},{112,128},... | collective-permute-start | bytes 4718600 | tf_op jit(solution)/shard_map/ppermute | solution.py:255
  25.1 0.1 slice_subtract_fusion
  25.2 22.2 %all_to_all.10 = f32[16,32,256]{2,1,0:T(8,128)S(1)} all-to-all(f32[16,32,256]{2,1,0:T(8,128)S(1)} %slice_subtract_fusion), channel_id=1, replica_groups=mesh['slab'=32,'row'=16] {'row'}, dimensions={0} | all-to-all | bytes 1048576 | tf_op jit(solution)/shard_map/all_to_all | solution.py:210
  47.3 1.1 %broadcast_in_dim.17 = f32[16,2,32,256]{3,2,1,0:T(8,128)} broadcast(f32[2,32,256]{2,1,0:T(8,128)S(1)} %slice.40), dimensions={1,2,3} | broadcast | bytes 1114112 | tf_op jit(solution)/shard_map/broadcast_in_dim | solution.py:253
  48.4 5.9 %all-to-all-start.1 = ((f32[16,2,32,256]{3,2,1,0:T(8,128)}), f32[16,2,32,256]{3,2,1,0:T(8,128)S(1)}, u32[]{:S(2)}, u32[]{:S(2)}) async-start(f32[16,2,32,256]{3,2,1,0:T(8,128)} %broadcast_in_dim.17), calls=%async_computation.1 | async-start | bytes 2097152 | tf_op jit(solution)/shard_map/all_to_all | solution.py:210
  54.3 0.7 collective-permute-start.6
  55.0 0.7 collective-permute-start.5
  55.6 1.3 %collective-permute-start.4 = (f32[288,128]{1,0:T(8,128)S(1)}, f32[288,128]{1,0:T(8,128)S(1)}, u32[]{:S(2)}, u32[]{:S(2)}) collective-permute-start(f32[288,128]{1,0:T(8,128)S(1)} %add_select_fusion.kept), channel_id=1, source_target_pairs={{0,8},{1,9},{2,10},{3,11},{16,24},{17,25},{18,26},{19,27},{32,40},... | collective-permute-start | bytes 442376 | tf_op jit(solution)/shard_map/ppermute | solution.py:251
  56.9 0.0 collective-permute-done.6.three
  57.0 0.0 collective-permute-done.5.two
  57.0 17.0 %collective-permute-done.4.one = f32[288,128]{1,0:T(8,128)S(1)} collective-permute-done((f32[288,128]{1,0:T(8,128)S(1)}, f32[288,128]{1,0:T(8,128)S(1)}, u32[]{:S(2)}, u32[]{:S(2)}) %collective-permute-start.4) | collective-permute-done | bytes 147488 | tf_op jit(solution)/shard_map/ppermute | solution.py:251
  74.0 7.5 %panel_inverse.1.inverse0 = f32[256,256]{1,0:T(8,128)S(1)} custom-call(s32[1]{0:T(128)} %bitcast.row_index, f32[288,128]{1,0:T(8,128)S(1)} %add_select_fusion.kept, f32[288,128]{1,0:T(8,128)S(1)} %collective-permute-done.4.one, f32[288,128]{1,0:T(8,128)S(1)} %collective-permute-done.5.two, f32[288,128]{1,0:T(8,128)S(1)} %collective-permute-done.6.three), custom_call_target="tpu_custom_call" | custom-call | flops 6710886400 | bytes 524288 | tf_op jit(solution)/shard_map/panel_inverse/pallas_call | solution.py:257
  81.4 0.0 all-to-all-done.1.head
  81.4 0.0 collective-permute-done.7.prev
  81.5 12.5 %panel_update.1 = (f32[512,512]{1,0:T(8,128)}, f32[512,256]{1,0:T(8,128)}) custom-call(s32[1]{0:T(128)} %bitcast.row_index, f32[256,256]{1,0:T(8,128)S(1)} %panel_inverse.1.inverse0, f32[16,2,32,256]{3,2,1,0:T(8,128)S(1)} %all-to-all-done.1.head, f32[512,768]{1,0:T(8,128)S(1)} %bitcast.11, f32[512,768]{1,0:T(8,128)} %collective-permute-done.7.prev), custom_call_target="tpu_custom_call" | custom-call | tf_op jit(solution)/shard_map/panel_update/pallas_call | solution.py:268
  (4 shorter events, 0.1 us)
Async XLA Ops:
  1.7 6.6 %copy-start = (f32[1,512,768]{2,1,0:T(8,128)S(1)}, f32[1,512,768]{2,1,0:T(8,128)}, u32[]{:S(2)}) copy-start(f32[1,512,768]{2,1,0:T(8,128)} %param.2) | copy-start | bytes 4718596
  3.0 14.2 %collective-permute-start = (f32[16,48,256]{2,1,0:T(8,128)S(1)}, f32[16,48,256]{2,1,0:T(8,128)S(1)}, u32[]{:S(2)}, u32[]{:S(2)}) collective-permute-start(f32[16,48,256]{2,1,0:T(8,128)S(1)} %pad_maximum_fusion), channel_id=1, source_target_pairs={{0,16},{16,32},{32,48},{48,64},{64,80},{80,96},{96,112},{112,128},... | collective-permute-start | bytes 2359304 | tf_op jit(solution)/shard_map/ppermute | solution.py:233
  17.3 2.1 %collective-permute-start.3 = (f32[288,128]{1,0:T(8,128)S(1)}, f32[288,128]{1,0:T(8,128)S(1)}, u32[]{:S(2)}, u32[]{:S(2)}) collective-permute-start(f32[288,128]{1,0:T(8,128)S(1)} %pack_corner.1), channel_id=1, source_target_pairs={{0,3},{16,19},{32,35},{48,51},{64,67},{80,83},{96,99},{112,115},{1... | collective-permute-start | bytes 442376 | tf_op jit(solution)/shard_map/ppermute | solution.py:248
  18.0 1.4 %collective-permute-start.2 = (f32[288,128]{1,0:T(8,128)S(1)}, f32[288,128]{1,0:T(8,128)S(1)}, u32[]{:S(2)}, u32[]{:S(2)}) collective-permute-start(f32[288,128]{1,0:T(8,128)S(1)} %pack_corner.1), channel_id=1, source_target_pairs={{0,1},{16,17},{32,33},{48,49},{64,65},{80,81},{96,97},{112,113},{1... | collective-permute-start | bytes 442376 | tf_op jit(solution)/shard_map/ppermute | solution.py:248
  18.6 0.8 collective-permute-start.1
  19.5 62.0 %collective-permute-start.7 = (f32[512,768]{1,0:T(8,128)}, f32[512,768]{1,0:T(8,128)}, u32[]{:S(2)}, u32[]{:S(2)}) collective-permute-start(f32[512,768]{1,0:T(8,128)} %bitcast.2), channel_id=1, source_target_pairs={{0,16},{16,32},{32,48},{48,64},{64,80},{80,96},{96,112},{112,128},... | collective-permute-start | bytes 4718600 | tf_op jit(solution)/shard_map/ppermute | solution.py:255
  48.4 33.0 %all-to-all-start.1 = ((f32[16,2,32,256]{3,2,1,0:T(8,128)}), f32[16,2,32,256]{3,2,1,0:T(8,128)S(1)}, u32[]{:S(2)}, u32[]{:S(2)}) async-start(f32[16,2,32,256]{3,2,1,0:T(8,128)} %broadcast_in_dim.17), calls=%async_computation.1 | async-start | bytes 2097152 | tf_op jit(solution)/shard_map/all_to_all | solution.py:210
  54.3 2.6 %collective-permute-start.6 = (f32[288,128]{1,0:T(8,128)S(1)}, f32[288,128]{1,0:T(8,128)S(1)}, u32[]{:S(2)}, u32[]{:S(2)}) collective-permute-start(f32[288,128]{1,0:T(8,128)S(1)} %add_select_fusion.kept), channel_id=1, source_target_pairs={{0,12},{1,13},{2,14},{3,15},{16,28},{17,29},{18,30},{19,31},{32,44... | collective-permute-start | bytes 442376 | tf_op jit(solution)/shard_map/ppermute | solution.py:251
  55.0 2.0 %collective-permute-start.5 = (f32[288,128]{1,0:T(8,128)S(1)}, f32[288,128]{1,0:T(8,128)S(1)}, u32[]{:S(2)}, u32[]{:S(2)}) collective-permute-start(f32[288,128]{1,0:T(8,128)S(1)} %add_select_fusion.kept), channel_id=1, source_target_pairs={{0,4},{1,5},{2,6},{3,7},{16,20},{17,21},{18,22},{19,23},{32,36},{3... | collective-permute-start | bytes 442376 | tf_op jit(solution)/shard_map/ppermute | solution.py:251
  55.6 18.3 %collective-permute-start.4 = (f32[288,128]{1,0:T(8,128)S(1)}, f32[288,128]{1,0:T(8,128)S(1)}, u32[]{:S(2)}, u32[]{:S(2)}) collective-permute-start(f32[288,128]{1,0:T(8,128)S(1)} %add_select_fusion.kept), channel_id=1, source_target_pairs={{0,8},{1,9},{2,10},{3,11},{16,24},{17,25},{18,26},{19,27},{32,40},... | collective-permute-start | bytes 442376 | tf_op jit(solution)/shard_map/ppermute | solution.py:251

commit v5 on v4

--- a/solution.py
+++ b/solution.py
@@ -231,7 +231,9 @@
     corner = out[:NB, :NB].reshape(count, part[1], NB)
     sent = jnp.concatenate([head_shares(out, row_index, count), corner], axis=1)
     came = lax.ppermute(sent, "slab", pairs)
-    shares = exchange(head_shares(own, row_index, count) - came[:, : part[0]])[:2]
+    mine = head_shares(own, row_index, count) - came[:, : part[0]]
+    mine, came = lax.optimization_barrier((mine, came))
+    shares = exchange(mine)[:2]
     packed_rows = 2 * LANES + STRIP
     packed = pl.pallas_call(
         pack_kernel,
@@ -247,12 +249,13 @@
     )(own, came)
     along = [lax.ppermute(packed, "row", [(0, d)]) for d in (2, 1, 3)]
     kept = jnp.where(row_index == 0, packed, along[0] + along[1] + along[2])
+    out, _ = lax.optimization_barrier((out, kept))
+    prev = lax.ppermute(out, "slab", pairs)
     down = [
         lax.ppermute(kept, "row", [(x, ACROSS * d + x) for x in range(ACROSS)]) for d in (2, 1, 3)
     ]
+    *down, shares = lax.optimization_barrier((*down, shares))
     head = exchange(jnp.broadcast_to(shares[None], (count,) + shares.shape))
-    out, _ = lax.optimization_barrier((out, kept))
-    prev = lax.ppermute(out, "slab", pairs)
 
     inverse0 = pl.pallas_call(
         first_kernel,

time: 94.4 us -> 91.1 us (0.965)
  the two profiles are of different devices: /device:TPU:113 before, /device:TPU:65 now
where the time goes in v5:
time: 91.1 us; the launch traced here: 90.6 us
  starting transfers between devices  35.8 us (39%)
  waiting for transfers between devices  29.5 us (32%)
  Pallas kernels  20 us (22%)
  other arithmetic  2.25 us (2%)
  local copies, waits for them, and re-layouts  2.21 us (2%)
    all_to_all x2, waiting for transfers between devices, exchange(): return lax.all_to_all(blocks, 'row', 0, 0, tiled=True)  14.5 us
    pallas_call x1, Pallas kernels, per_device(): pl.pallas_call(second_kernel, out_shape=(jax.ShapeDtypeStruct((rows_here,...  12.5 us
    all_to_all x2, starting transfers between devices, exchange(): return lax.all_to_all(blocks, 'row', 0, 0, tiled=True)  11.1 us
    ppermute x1, waiting for transfers between devices, per_device(): came = lax.ppermute(sent, 'slab', pairs)  8.78 us
    pallas_call x1, Pallas kernels, per_device(): pl.pallas_call(first_kernel, out_shape=jax.ShapeDtypeStruct((NB, NB), jnp...  7.46 us
    ppermute x3, starting transfers between devices, per_device(): lax.ppermute(kept, 'row', [(x, ACROSS * d + x) for x in range(ACROSS)])  7.08 us
    ppermute x3, starting transfers between devices, per_device(): along = [lax.ppermute(packed, 'row', [(0, d)]) for d in (2, 1, 3)]  6.99 us
    ppermute x1, starting transfers between devices, per_device(): prev = lax.ppermute(out, 'slab', pairs)  6.51 us
  transfers between devices with their start and end apart: 10, of which 6 were waited for; matrix products, arithmetic and copies ran while one was open for 1% of the time, Pallas kernels for 8%

profile of v5, /device:TPU:65, one launch (start us, length us, event | category | flops | bytes accessed | tf_op | source)
XLA Modules:
  0.0 90.6 jit_solution(17099207282263831570)
XLA Ops:
  0.6 1.1 %fusion = (f32[256,256]{1,0:T(8,128)S(1)}, f32[256,256]{1,0:T(8,128)S(1)}) fusion(f32[512,768]{1,0:T(8,128)} %bitcast.3), kind=kLoop, calls=%fused_computation.5 | loop fusion | bytes 1048576 | tf_op jit(solution)/shard_map/slice | solution.py:214
  1.7 0.0 copy-start
  1.7 1.2 %slice_select_fusion = f32[512,256]{1,0:T(8,128)S(1)} fusion(f32[512,768]{1,0:T(8,128)} %bitcast.3, f32[256,256]{1,0:T(8,128)S(1)} %get-tuple-element.20, f32[256,256]{1,0:T(8,128)S(1)} %get-tuple-element.21, pred[]{:T(512)S(6)} %eq.8), kind=kLoop, calls=%fused_computation.2 | loop fusion | flops 262144 | bytes 1572865 | tf_op jit(solution)/shard_map/jit(_where)/select_n | solution.py:215
  3.0 0.1 pad_maximum_fusion
  3.0 4.1 %collective-permute-start = (f32[16,48,256]{2,1,0:T(8,128)S(1)}, f32[16,48,256]{2,1,0:T(8,128)S(1)}, u32[]{:S(2)}, u32[]{:S(2)}) collective-permute-start(f32[16,48,256]{2,1,0:T(8,128)S(1)} %pad_maximum_fusion), channel_id=1, source_target_pairs={{0,16},{16,32},{32,48},{48,64},{64,80},{80,96},{96,112},{112,128},... | collective-permute-start | bytes 2359304 | tf_op jit(solution)/shard_map/ppermute | solution.py:233
  7.1 0.0 copy-done
  7.2 0.1 slice_select_fusion.1
  7.3 8.8 %collective-permute-done.prev = f32[16,48,256]{2,1,0:T(8,128)S(1)} collective-permute-done((f32[16,48,256]{2,1,0:T(8,128)S(1)}, f32[16,48,256]{2,1,0:T(8,128)S(1)}, u32[]{:S(2)}, u32[]{:S(2)}) %collective-permute-start) | collective-permute-done | bytes 786464 | tf_op jit(solution)/shard_map/ppermute | solution.py:233
  16.1 0.9 slice_subtract_fusion
  16.9 4.4 %collective-permute-start.3 = (f32[288,128]{1,0:T(8,128)S(1)}, f32[288,128]{1,0:T(8,128)S(1)}, u32[]{:S(2)}, u32[]{:S(2)}) collective-permute-start(f32[288,128]{1,0:T(8,128)S(1)} %pack_corner.1), channel_id=1, source_target_pairs={{0,3},{16,19},{32,35},{48,51},{64,67},{80,83},{96,99},{112,115},{1... | collective-permute-start | bytes 442376 | tf_op jit(solution)/shard_map/ppermute | solution.py:250
  21.3 1.3 %collective-permute-start.2 = (f32[288,128]{1,0:T(8,128)S(1)}, f32[288,128]{1,0:T(8,128)S(1)}, u32[]{:S(2)}, u32[]{:S(2)}) collective-permute-start(f32[288,128]{1,0:T(8,128)S(1)} %pack_corner.1), channel_id=1, source_target_pairs={{0,1},{16,17},{32,33},{48,49},{64,65},{80,81},{96,97},{112,113},{1... | collective-permute-start | bytes 442376 | tf_op jit(solution)/shard_map/ppermute | solution.py:250
  22.6 1.3 %collective-permute-start.1 = (f32[288,128]{1,0:T(8,128)S(1)}, f32[288,128]{1,0:T(8,128)S(1)}, u32[]{:S(2)}, u32[]{:S(2)}) collective-permute-start(f32[288,128]{1,0:T(8,128)S(1)} %pack_corner.1), channel_id=1, source_target_pairs={{0,2},{16,18},{32,34},{48,50},{64,66},{80,82},{96,98},{112,114},{1... | collective-permute-start | bytes 442376 | tf_op jit(solution)/shard_map/ppermute | solution.py:250
  24.0 0.0 collective-permute-done.3
  24.0 0.8 collective-permute-done.2
  24.7 3.2 %collective-permute-done.1 = f32[288,128]{1,0:T(8,128)S(1)} collective-permute-done((f32[288,128]{1,0:T(8,128)S(1)}, f32[288,128]{1,0:T(8,128)S(1)}, u32[]{:S(2)}, u32[]{:S(2)}) %collective-permute-start.1) | collective-permute-done | bytes 147488 | tf_op jit(solution)/shard_map/ppermute | solution.py:250
  28.0 6.5 %collective-permute-start.7 = (f32[512,768]{1,0:T(8,128)}, f32[512,768]{1,0:T(8,128)}, u32[]{:S(2)}, u32[]{:S(2)}) collective-permute-start(f32[512,768]{1,0:T(8,128)} %bitcast.3), channel_id=1, source_target_pairs={{0,16},{16,32},{32,48},{48,64},{64,80},{80,96},{96,112},{112,128},... | collective-permute-start | bytes 4718600 | tf_op jit(solution)/shard_map/ppermute | solution.py:253
  34.5 5.1 %all-to-all-start = ((f32[16,32,256]{2,1,0:T(8,128)}), f32[16,32,256]{2,1,0:T(8,128)S(1)}, u32[]{:S(2)}, u32[]{:S(2)}) async-start(f32[16,32,256]{2,1,0:T(8,128)} %slice_subtract_fusion), calls=%async_computation | async-start | bytes 1048576 | tf_op jit(solution)/shard_map/all_to_all | solution.py:210
  39.6 4.5 %collective-permute-start.6 = (f32[288,128]{1,0:T(8,128)S(1)}, f32[288,128]{1,0:T(8,128)S(1)}, u32[]{:S(2)}, u32[]{:S(2)}) collective-permute-start(f32[288,128]{1,0:T(8,128)S(1)} %add_select_fusion.kept), channel_id=1, source_target_pairs={{0,12},{1,13},{2,14},{3,15},{16,28},{17,29},{18,30},{19,31},{32,44... | collective-permute-start | bytes 442376 | tf_op jit(solution)/shard_map/ppermute | solution.py:255
  44.1 1.3 %collective-permute-start.5 = (f32[288,128]{1,0:T(8,128)S(1)}, f32[288,128]{1,0:T(8,128)S(1)}, u32[]{:S(2)}, u32[]{:S(2)}) collective-permute-start(f32[288,128]{1,0:T(8,128)S(1)} %add_select_fusion.kept), channel_id=1, source_target_pairs={{0,4},{1,5},{2,6},{3,7},{16,20},{17,21},{18,22},{19,23},{32,36},{3... | collective-permute-start | bytes 442376 | tf_op jit(solution)/shard_map/ppermute | solution.py:255
  45.4 1.3 %collective-permute-start.4 = (f32[288,128]{1,0:T(8,128)S(1)}, f32[288,128]{1,0:T(8,128)S(1)}, u32[]{:S(2)}, u32[]{:S(2)}) collective-permute-start(f32[288,128]{1,0:T(8,128)S(1)} %add_select_fusion.kept), channel_id=1, source_target_pairs={{0,8},{1,9},{2,10},{3,11},{16,24},{17,25},{18,26},{19,27},{32,40},... | collective-permute-start | bytes 442376 | tf_op jit(solution)/shard_map/ppermute | solution.py:255
  46.7 2.7 %all-to-all-done = f32[16,32,256]{2,1,0:T(8,128)S(1)} async-done(((f32[16,32,256]{2,1,0:T(8,128)}), f32[16,32,256]{2,1,0:T(8,128)S(1)}, u32[]{:S(2)}, u32[]{:S(2)}) %all-to-all-start) | async-done | bytes 524320 | tf_op jit(solution)/shard_map/all_to_all | solution.py:210
  49.5 0.0 collective-permute-done.6.three
  49.5 0.0 collective-permute-done.5.two
  49.5 2.2 %collective-permute-done.4.one = f32[288,128]{1,0:T(8,128)S(1)} collective-permute-done((f32[288,128]{1,0:T(8,128)S(1)}, f32[288,128]{1,0:T(8,128)S(1)}, u32[]{:S(2)}, u32[]{:S(2)}) %collective-permute-start.4) | collective-permute-done | bytes 147488 | tf_op jit(solution)/shard_map/ppermute | solution.py:255
  51.7 1.1 %broadcast_in_dim.17 = f32[16,2,32,256]{3,2,1,0:T(8,128)} broadcast(f32[2,32,256]{2,1,0:T(8,128)S(1)} %slice.40), dimensions={1,2,3} | broadcast | bytes 1114112 | tf_op jit(solution)/shard_map/broadcast_in_dim | solution.py:258
  52.8 6.0 %all-to-all-start.1 = ((f32[16,2,32,256]{3,2,1,0:T(8,128)}), f32[16,2,32,256]{3,2,1,0:T(8,128)S(1)}, u32[]{:S(2)}, u32[]{:S(2)}) async-start(f32[16,2,32,256]{3,2,1,0:T(8,128)} %broadcast_in_dim.17), calls=%async_computation.1 | async-start | bytes 2097152 | tf_op jit(solution)/shard_map/all_to_all | solution.py:210
  58.8 7.5 %panel_inverse.1.inverse0 = f32[256,256]{1,0:T(8,128)S(1)} custom-call(s32[1]{0:T(128)} %bitcast.row_index, f32[288,128]{1,0:T(8,128)S(1)} %add_select_fusion.kept, f32[288,128]{1,0:T(8,128)S(1)} %collective-permute-done.4.one, f32[288,128]{1,0:T(8,128)S(1)} %collective-permute-done.5.two, f32[288,128]{1,0:T(8,128)S(1)} %collective-permute-done.6.three), custom_call_target="tpu_custom_call" | custom-call | flops 6710886400 | bytes 524288 | tf_op jit(solution)/shard_map/panel_inverse/pallas_call | solution.py:260
  66.3 11.8 %all-to-all-done.1.head = f32[16,2,32,256]{3,2,1,0:T(8,128)S(1)} async-done(((f32[16,2,32,256]{3,2,1,0:T(8,128)}), f32[16,2,32,256]{3,2,1,0:T(8,128)S(1)}, u32[]{:S(2)}, u32[]{:S(2)}) %all-to-all-start.1) | async-done | bytes 1048608 | tf_op jit(solution)/shard_map/all_to_all | solution.py:210
  78.1 0.0 collective-permute-done.7.prev
  78.1 12.5 %panel_update.1 = (f32[512,512]{1,0:T(8,128)}, f32[512,256]{1,0:T(8,128)}) custom-call(s32[1]{0:T(128)} %bitcast.row_index, f32[256,256]{1,0:T(8,128)S(1)} %panel_inverse.1.inverse0, f32[16,2,32,256]{3,2,1,0:T(8,128)S(1)} %all-to-all-done.1.head, f32[512,768]{1,0:T(8,128)S(1)} %bitcast.11, f32[512,768]{1,0:T(8,128)} %collective-permute-done.7.prev), custom_call_target="tpu_custom_call" | custom-call | tf_op jit(solution)/shard_map/panel_update/pallas_call | solution.py:271
  (4 shorter events, 0.1 us)
Async XLA Ops:
  1.7 5.4 %copy-start = (f32[1,512,768]{2,1,0:T(8,128)S(1)}, f32[1,512,768]{2,1,0:T(8,128)}, u32[]{:S(2)}) copy-start(f32[1,512,768]{2,1,0:T(8,128)} %param.2) | copy-start | bytes 4718596
  3.0 13.0 %collective-permute-start = (f32[16,48,256]{2,1,0:T(8,128)S(1)}, f32[16,48,256]{2,1,0:T(8,128)S(1)}, u32[]{:S(2)}, u32[]{:S(2)}) collective-permute-start(f32[16,48,256]{2,1,0:T(8,128)S(1)} %pad_maximum_fusion), channel_id=1, source_target_pairs={{0,16},{16,32},{32,48},{48,64},{64,80},{80,96},{96,112},{112,128},... | collective-permute-start | bytes 2359304 | tf_op jit(solution)/shard_map/ppermute | solution.py:233
  16.9 7.0 %collective-permute-start.3 = (f32[288,128]{1,0:T(8,128)S(1)}, f32[288,128]{1,0:T(8,128)S(1)}, u32[]{:S(2)}, u32[]{:S(2)}) collective-permute-start(f32[288,128]{1,0:T(8,128)S(1)} %pack_corner.1), channel_id=1, source_target_pairs={{0,3},{16,19},{32,35},{48,51},{64,67},{80,83},{96,99},{112,115},{1... | collective-permute-start | bytes 442376 | tf_op jit(solution)/shard_map/ppermute | solution.py:250
  21.3 3.4 %collective-permute-start.2 = (f32[288,128]{1,0:T(8,128)S(1)}, f32[288,128]{1,0:T(8,128)S(1)}, u32[]{:S(2)}, u32[]{:S(2)}) collective-permute-start(f32[288,128]{1,0:T(8,128)S(1)} %pack_corner.1), channel_id=1, source_target_pairs={{0,1},{16,17},{32,33},{48,49},{64,65},{80,81},{96,97},{112,113},{1... | collective-permute-start | bytes 442376 | tf_op jit(solution)/shard_map/ppermute | solution.py:250
  22.6 5.3 %collective-permute-start.1 = (f32[288,128]{1,0:T(8,128)S(1)}, f32[288,128]{1,0:T(8,128)S(1)}, u32[]{:S(2)}, u32[]{:S(2)}) collective-permute-start(f32[288,128]{1,0:T(8,128)S(1)} %pack_corner.1), channel_id=1, source_target_pairs={{0,2},{16,18},{32,34},{48,50},{64,66},{80,82},{96,98},{112,114},{1... | collective-permute-start | bytes 442376 | tf_op jit(solution)/shard_map/ppermute | solution.py:250
  28.0 50.1 %collective-permute-start.7 = (f32[512,768]{1,0:T(8,128)}, f32[512,768]{1,0:T(8,128)}, u32[]{:S(2)}, u32[]{:S(2)}) collective-permute-start(f32[512,768]{1,0:T(8,128)} %bitcast.3), channel_id=1, source_target_pairs={{0,16},{16,32},{32,48},{48,64},{64,80},{80,96},{96,112},{112,128},... | collective-permute-start | bytes 4718600 | tf_op jit(solution)/shard_map/ppermute | solution.py:253
  34.5 14.9 %all-to-all-start = ((f32[16,32,256]{2,1,0:T(8,128)}), f32[16,32,256]{2,1,0:T(8,128)S(1)}, u32[]{:S(2)}, u32[]{:S(2)}) async-start(f32[16,32,256]{2,1,0:T(8,128)} %slice_subtract_fusion), calls=%async_computation | async-start | bytes 1048576 | tf_op jit(solution)/shard_map/all_to_all | solution.py:210
  39.6 9.8 %collective-permute-start.6 = (f32[288,128]{1,0:T(8,128)S(1)}, f32[288,128]{1,0:T(8,128)S(1)}, u32[]{:S(2)}, u32[]{:S(2)}) collective-permute-start(f32[288,128]{1,0:T(8,128)S(1)} %add_select_fusion.kept), channel_id=1, source_target_pairs={{0,12},{1,13},{2,14},{3,15},{16,28},{17,29},{18,30},{19,31},{32,44... | collective-permute-start | bytes 442376 | tf_op jit(solution)/shard_map/ppermute | solution.py:255
  44.1 5.4 %collective-permute-start.5 = (f32[288,128]{1,0:T(8,128)S(1)}, f32[288,128]{1,0:T(8,128)S(1)}, u32[]{:S(2)}, u32[]{:S(2)}) collective-permute-start(f32[288,128]{1,0:T(8,128)S(1)} %add_select_fusion.kept), channel_id=1, source_target_pairs={{0,4},{1,5},{2,6},{3,7},{16,20},{17,21},{18,22},{19,23},{32,36},{3... | collective-permute-start | bytes 442376 | tf_op jit(solution)/shard_map/ppermute | solution.py:255
  45.4 6.3 %collective-permute-start.4 = (f32[288,128]{1,0:T(8,128)S(1)}, f32[288,128]{1,0:T(8,128)S(1)}, u32[]{:S(2)}, u32[]{:S(2)}) collective-permute-start(f32[288,128]{1,0:T(8,128)S(1)} %add_select_fusion.kept), channel_id=1, source_target_pairs={{0,8},{1,9},{2,10},{3,11},{16,24},{17,25},{18,26},{19,27},{32,40},... | collective-permute-start | bytes 442376 | tf_op jit(solution)/shard_map/ppermute | solution.py:255
  52.8 25.3 %all-to-all-start.1 = ((f32[16,2,32,256]{3,2,1,0:T(8,128)}), f32[16,2,32,256]{3,2,1,0:T(8,128)S(1)}, u32[]{:S(2)}, u32[]{:S(2)}) async-start(f32[16,2,32,256]{3,2,1,0:T(8,128)} %broadcast_in_dim.17), calls=%async_computation.1 | async-start | bytes 2097152 | tf_op jit(solution)/shard_map/all_to_all | solution.py:210

commit v6 on v4

--- a/solution.py
+++ b/solution.py
@@ -8,7 +8,7 @@
 NB = 256
 PANELW = 512
 COLS = 768
-ACROSS = 4
+PART = 16
 STRIP = 32
 SUB = 8
 LANES = 128
@@ -126,46 +126,31 @@
             work[top + LANES :, :] = below - update
 
 
-def pack_kernel(own, prev, packed):
-    value = own[...] - prev[...].reshape((NB, NB))
-    strip_row = lax.broadcasted_iota(jnp.int32, (LANES, LANES), 0) // STRIP
-    strip_col = lax.broadcasted_iota(jnp.int32, (LANES, LANES), 1) // STRIP
-    packed[:LANES, :] = jnp.where(strip_row <= strip_col, value[:LANES, :LANES], value[LANES:, LANES:])
-    packed[LANES : 2 * LANES, :] = value[:LANES, LANES:]
-    strip = lax.broadcasted_iota(jnp.int32, (STRIP, LANES), 1) // STRIP
-    diagonal = jnp.zeros((STRIP, LANES), jnp.float32)
-    for i in range(LANES // STRIP):
-        rows = value[LANES + STRIP * i : LANES + STRIP * (i + 1), LANES:]
-        diagonal = jnp.where(strip == i, rows, diagonal)
-    packed[2 * LANES :, :] = diagonal
-
-
-def first_kernel(row_index, kept, one, two, three, inverse):
-    packed = jnp.where(row_index[0] < ACROSS, kept[...], one[...] + two[...] + three[...])
-    strip_row = lax.broadcasted_iota(jnp.int32, (LANES, LANES), 0) // STRIP
-    strip_col = lax.broadcasted_iota(jnp.int32, (LANES, LANES), 1) // STRIP
-    mixed = packed[:LANES, :]
-    diagonal = jnp.concatenate([packed[2 * LANES :, :]] * (LANES // STRIP), axis=0)
-    inverse[:LANES, :LANES] = mixed
-    inverse[:LANES, LANES:] = packed[LANES : 2 * LANES, :]
-    inverse[LANES:, :LANES] = jnp.zeros((LANES, LANES), jnp.float32)
-    inverse[LANES:, LANES:] = jnp.where(strip_row < strip_col, mixed.T, diagonal)
+def block_of(shares):
+    return shares.reshape((NB, NB))
+
+
+def first_kernel(mixed, inverse):
+    inverse[...] = block_of(mixed[:, :PART])
     invert_factor(inverse)
 
 
 def second_kernel(
-    row_index, inverse0, head, own, prev, factor, trailing,
+    row_index, inverse0, mixed, rest, own, prev, factor, trailing,
     work, before, middle, left, right, tail, arrive, leave,
 ):
     fetch = pltpu.make_async_copy(prev, before, arrive)
     fetch.start()
     x0 = inverse0[...]
-    half = head.shape[0] // 2
-    pick = lambda at, source: head[pl.ds(at, half), source].reshape((NB, NB))
-    w1 = dot(x0, pick(0, 0), (1, 0))
-    work[...] = pick(half, 0) - dot(w1, w1, (0, 0))
-    w2 = dot(x0, pick(0, 1), (1, 1))
-    cross = pick(half, 1) - dot(w2, w1, (0, 0))
+    strip_row = lax.broadcasted_iota(jnp.int32, (NB, NB), 0) // STRIP
+    strip_col = lax.broadcasted_iota(jnp.int32, (NB, NB), 1) // STRIP
+    diagonal = mixed[: STRIP // SUB, PART:].reshape((STRIP, NB))
+    diagonal = jnp.concatenate([diagonal] * (NB // STRIP), axis=0)
+    block = jnp.where(strip_row < strip_col, block_of(mixed[:, :PART]).T, diagonal)
+    w1 = dot(x0, block_of(rest[:, 0]), (1, 0))
+    work[...] = block - dot(w1, w1, (0, 0))
+    w2 = dot(x0, block_of(rest[:, 1]), (1, 1))
+    cross = block_of(rest[:, 2]) - dot(w2, w1, (0, 0))
     rows_here = own.shape[0]
     steps = LANES // STRIP
     piece = rows_here // steps
@@ -196,11 +181,11 @@
 
     invert_factor(work, between)
     x1 = work[LANES:, :]
-    rest = dot(x1, cross, (1, 1))
+    window.append(dot(x1, cross, (1, 1)))
     lower = dot(middle[...], x1, (1, 1))
     right[:, LANES:] = jnp.where(row[:, :LANES] >= NB, lower, 0.0)
     writes[1].start()
-    tail[...] = jnp.where(row >= PANELW, tail[...] - dot(lower, rest, (1, 0)), 0.0)
+    tail[...] = jnp.where(row >= PANELW, tail[...] - dot(lower, window[1], (1, 0)), 0.0)
     writes[2].start()
     for write in writes:
         write.wait()
@@ -211,9 +196,20 @@
 
 
 def head_shares(block, row_index, count):
-    side = jnp.concatenate([block[:NB, :NB], block[:NB, NB:PANELW]], axis=0)
-    mine = jnp.where(row_index == 1, side, block[:, NB:PANELW])
-    return mine.reshape(count, -1, NB)
+    first, second = block[:NB, :NB], block[NB:PANELW, NB:PANELW]
+    strip_row = jnp.arange(NB)[:, None] // STRIP
+    strip_col = jnp.arange(NB)[None, :] // STRIP
+    mixed = jnp.where((strip_row <= strip_col) | (row_index == 1), first, second)
+    strips = second.reshape(NB // STRIP, STRIP, NB)
+    own_strip = jnp.arange(NB // STRIP)[:, None, None] == strip_col[None]
+    diagonal = jnp.sum(jnp.where(own_strip, strips, 0.0), axis=0).reshape(-1, SUB, NB)
+    diagonal = jnp.pad(diagonal, ((0, count - diagonal.shape[0]), (0, 0), (0, 0)))
+    parts = [mixed.reshape(count, PART, NB), diagonal, block[:NB, NB:PANELW].reshape(count, PART, NB)]
+    return jnp.concatenate(parts, axis=1)
+
+
+def copies(share, count):
+    return jnp.broadcast_to(share[None], (count,) + share.shape)
 
 
 def per_device(schur_own, outgoing):
@@ -227,43 +223,28 @@
     smem = pl.BlockSpec(memory_space=pltpu.SMEM)
     params = pltpu.CompilerParams(vmem_limit_bytes=VMEM_BYTES)
 
-    part = (PANELW // count, NB // count)
-    corner = out[:NB, :NB].reshape(count, part[1], NB)
-    sent = jnp.concatenate([head_shares(out, row_index, count), corner], axis=1)
+    sent = head_shares(out, row_index, count)
     came = lax.ppermute(sent, "slab", pairs)
-    shares = exchange(head_shares(own, row_index, count) - came[:, : part[0]])[:2]
-    packed_rows = 2 * LANES + STRIP
-    packed = pl.pallas_call(
-        pack_kernel,
-        grid=(1,),
-        out_shape=jax.ShapeDtypeStruct((packed_rows, LANES), jnp.float32),
-        in_specs=[
-            pl.BlockSpec((NB, NB), lambda i: (0, 0)),
-            pl.BlockSpec((count, part[1], NB), lambda i: (0, part[0] // part[1], 0)),
-        ],
-        out_specs=pl.BlockSpec((packed_rows, LANES), lambda i: (0, 0)),
-        compiler_params=params,
-        name="pack_corner",
-    )(own, came)
-    along = [lax.ppermute(packed, "row", [(0, d)]) for d in (2, 1, 3)]
-    kept = jnp.where(row_index == 0, packed, along[0] + along[1] + along[2])
-    down = [
-        lax.ppermute(kept, "row", [(x, ACROSS * d + x) for x in range(ACROSS)]) for d in (2, 1, 3)
-    ]
-    head = exchange(jnp.broadcast_to(shares[None], (count,) + shares.shape))
+    own, _ = lax.optimization_barrier((own, sent))
+    kept = head_shares(own, row_index, count)
     out, _ = lax.optimization_barrier((out, kept))
     prev = lax.ppermute(out, "slab", pairs)
+    shares = exchange(kept - came)[:2]
+    mixed = exchange(copies(shares[0, : PART + SUB], count))
+    rest = jnp.stack([shares[0, PART + SUB :], shares[1, :PART], shares[1, PART + SUB :]])
+    rest, mixed = lax.optimization_barrier((copies(rest, count), mixed))
+    rest = exchange(rest)
 
     inverse0 = pl.pallas_call(
         first_kernel,
         out_shape=jax.ShapeDtypeStruct((NB, NB), jnp.float32),
-        in_specs=[smem] + [vmem] * 4,
+        in_specs=[vmem],
         out_specs=vmem,
         compiler_params=params,
         cost_estimate=pl.CostEstimate(
             flops=400 * NB**3, bytes_accessed=8 * NB**2, transcendentals=NB),
         name="panel_inverse",
-    )(row_index[None], kept, *down)
+    )(mixed)
 
     factor, trailing = pl.pallas_call(
         second_kernel,
@@ -271,7 +252,7 @@
             jax.ShapeDtypeStruct((rows_here, PANELW), jnp.float32),
             jax.ShapeDtypeStruct((rows_here, COLS - PANELW), jnp.float32),
         ),
-        in_specs=[smem] + [vmem] * 3 + [pl.BlockSpec(memory_space=pl.ANY)],
+        in_specs=[smem] + [vmem] * 4 + [pl.BlockSpec(memory_space=pl.ANY)],
         out_specs=(pl.BlockSpec(memory_space=pl.ANY), pl.BlockSpec(memory_space=pl.ANY)),
         scratch_shapes=[
             pltpu.VMEM((NB, NB), jnp.float32),
@@ -281,7 +262,7 @@
         + [pltpu.SemaphoreType.DMA, pltpu.SemaphoreType.DMA((3,))],
         compiler_params=params,
         name="panel_update",
-    )(row_index[None], inverse0, head, own, prev)
+    )(row_index[None], inverse0, mixed, rest, own, prev)
     return factor[None], trailing[None]
 
 

time: 94.4 us -> 81.7 us (0.87)
  the two profiles are of different devices: /device:TPU:113 before, /device:TPU:224 now
where the time goes in v6:
time: 81.7 us; the launch traced here: 81.2 us
  waiting for transfers between devices  37.7 us (46%)
  Pallas kernels  20 us (24%)
  starting transfers between devices  18.5 us (23%)
  other arithmetic  2.49 us (3%)
  local copies, waits for them, and re-layouts  1.76 us (2%)
    all_to_all x3, waiting for transfers between devices, exchange(): return lax.all_to_all(blocks, 'row', 0, 0, tiled=True)  27.9 us
    all_to_all x3, starting transfers between devices, exchange(): return lax.all_to_all(blocks, 'row', 0, 0, tiled=True)  14.2 us
    pallas_call x1, Pallas kernels, per_device(): pl.pallas_call(second_kernel, out_shape=(jax.ShapeDtypeStruct((rows_here,...  12.6 us
    ppermute x1, waiting for transfers between devices, per_device(): came = lax.ppermute(sent, 'slab', pairs)  9.81 us
    pallas_call x1, Pallas kernels, per_device(): pl.pallas_call(first_kernel, out_shape=jax.ShapeDtypeStruct((NB, NB), jnp...  7.44 us
    ppermute x1, starting transfers between devices, per_device(): prev = lax.ppermute(out, 'slab', pairs)  2.39 us
    ppermute x1, starting transfers between devices, per_device(): came = lax.ppermute(sent, 'slab', pairs)  1.92 us
    broadcast_in_dim x3, local copies, waits for them, and re-layouts, copies(): return jnp.broadcast_to(share[None], (count,) + share.shape)  1.75 us
  transfers between devices with their start and end apart: 5, of which 4 were waited for; matrix products, arithmetic and copies ran while one was open for 2% of the time, Pallas kernels for 9%

profile of v6, /device:TPU:224, one launch (start us, length us, event | category | flops | bytes accessed | tf_op | source)
XLA Modules:
  0.0 81.2 jit_solution(4999180031750688911)
XLA Ops:
  0.6 0.0 copy-start
  0.7 1.3 %slice_select_fusion = (f32[256,256]{1,0:T(8,128)S(1)}, f32[256,256]{1,0:T(8,128)S(1)}, f32[256,256]{1,0:T(8,128)S(1)}) fusion(f32[512,768]{1,0:T(8,128)} %bitcast.23, s32[256]{0:T(256)S(1)} %and_select_fusion, pred[]{:T(512)S(6)} %eq.35), kind=kLoop, calls=%fused_computation.7 | loop fusion | flops 196608 | bytes 1574913 | tf_op jit(solution)/shard_map/jit(_where)/select_n | solution.py:202
  2.1 1.9 %collective-permute-start = (f32[16,40,256]{2,1,0:T(8,128)S(1)}, f32[16,40,256]{2,1,0:T(8,128)S(1)}, u32[]{:S(2)}, u32[]{:S(2)}) collective-permute-start(f32[16,40,256]{2,1,0:T(8,128)S(1)} %fusion.1), channel_id=1, source_target_pairs={{0,16},{16,32},{32,48},{48,64},{64,80},{80,96},{96,112},{112,128},... | collective-permute-start | bytes 1966088 | tf_op jit(solution)/shard_map/ppermute | solution.py:227
  4.0 0.0 copy-done
  4.0 0.1 slice_select_fusion.1
  4.2 9.8 %collective-permute-done = f32[16,40,256]{2,1,0:T(8,128)S(1)} collective-permute-done((f32[16,40,256]{2,1,0:T(8,128)S(1)}, f32[16,40,256]{2,1,0:T(8,128)S(1)}, u32[]{:S(2)}, u32[]{:S(2)}) %collective-permute-start) | collective-permute-done | bytes 655392 | tf_op jit(solution)/shard_map/ppermute | solution.py:227
  14.0 0.9 %fusion.3 = f32[16,40,256]{2,1,0:T(8,128)} fusion(f32[16,40,256]{2,1,0:T(8,128)S(1)} %collective-permute-done, f32[16,16,256]{2,1,0:T(8,128)S(1)} %bitcast.18, f32[4,8,256]{2,1,0:T(8,128)S(1)} %bitcast.25, f32[16,16,256]{2,1,0:T(8,128)S(1)} %bitcast.17), kind=kLoop, calls=%fused_computation.19 | loop fusion | flops 1146880 | bytes 1867776 | tf_op jit(solution)/shard_map/sub | solution.py:232
  14.9 7.0 %all-to-all-start = ((f32[16,40,256]{2,1,0:T(8,128)}), f32[16,40,256]{2,1,0:T(8,128)S(1)}, u32[]{:S(2)}, u32[]{:S(2)}) async-start(f32[16,40,256]{2,1,0:T(8,128)} %fusion.3), calls=%async_computation | async-start | bytes 1310720 | tf_op jit(solution)/shard_map/all_to_all | solution.py:195
  22.0 2.4 %collective-permute-start.1 = (f32[512,768]{1,0:T(8,128)}, f32[512,768]{1,0:T(8,128)}, u32[]{:S(2)}, u32[]{:S(2)}) collective-permute-start(f32[512,768]{1,0:T(8,128)} %bitcast.24), channel_id=1, source_target_pairs={{0,16},{16,32},{32,48},{48,64},{64,80},{80,96},{96,112},{112,128},... | collective-permute-start | bytes 4718600 | tf_op jit(solution)/shard_map/ppermute | solution.py:231
  24.4 11.6 %all-to-all-done = f32[16,40,256]{2,1,0:T(8,128)S(1)} async-done(((f32[16,40,256]{2,1,0:T(8,128)}), f32[16,40,256]{2,1,0:T(8,128)S(1)}, u32[]{:S(2)}, u32[]{:S(2)}) %all-to-all-start) | async-done | bytes 655392 | tf_op jit(solution)/shard_map/all_to_all | solution.py:195
  35.9 0.8 broadcast_in_dim.53
  36.7 3.6 %all-to-all-start.1 = ((f32[16,24,256]{2,1,0:T(8,128)}), f32[16,24,256]{2,1,0:T(8,128)S(1)}, u32[]{:S(2)}, u32[]{:S(2)}) async-start(f32[16,24,256]{2,1,0:T(8,128)} %broadcast_in_dim.53), calls=%async_computation.1 | async-start | bytes 786432 | tf_op jit(solution)/shard_map/all_to_all | solution.py:195
  40.3 10.2 %all-to-all-done.1.mixed = f32[16,24,256]{2,1,0:T(8,128)S(1)} async-done(((f32[16,24,256]{2,1,0:T(8,128)}), f32[16,24,256]{2,1,0:T(8,128)S(1)}, u32[]{:S(2)}, u32[]{:S(2)}) %all-to-all-start.1) | async-done | bytes 393248 | tf_op jit(solution)/shard_map/all_to_all | solution.py:195
  50.5 1.0 %broadcast_in_dim.51 = f32[16,3,16,256]{3,2,1,0:T(8,128)} broadcast(f32[3,16,256]{2,1,0:T(8,128)S(1)} %pad_maximum_fusion), dimensions={1,2,3} | broadcast | bytes 835584 | tf_op jit(solution)/shard_map/broadcast_in_dim | solution.py:212
  51.4 3.6 %all-to-all-start.2 = ((f32[16,3,16,256]{3,2,1,0:T(8,128)}), f32[16,3,16,256]{3,2,1,0:T(8,128)S(1)}, u32[]{:S(2)}, u32[]{:S(2)}) async-start(f32[16,3,16,256]{3,2,1,0:T(8,128)} %broadcast_in_dim.51), calls=%async_computation.2 | async-start | bytes 1572864 | tf_op jit(solution)/shard_map/all_to_all | solution.py:195
  55.1 7.4 %panel_inverse.1.inverse0 = f32[256,256]{1,0:T(8,128)S(1)} custom-call(f32[16,24,256]{2,1,0:T(8,128)S(1)} %all-to-all-done.1.mixed), custom_call_target="tpu_custom_call" | custom-call | flops 6710886400 | bytes 524288 | tf_op jit(solution)/shard_map/panel_inverse/pallas_call | solution.py:238
  62.5 0.0 collective-permute-done.1.prev
  62.5 6.1 %all-to-all-done.2.rest = f32[16,3,16,256]{3,2,1,0:T(8,128)S(1)} async-done(((f32[16,3,16,256]{3,2,1,0:T(8,128)}), f32[16,3,16,256]{3,2,1,0:T(8,128)S(1)}, u32[]{:S(2)}, u32[]{:S(2)}) %all-to-all-start.2) | async-done | bytes 786464 | tf_op jit(solution)/shard_map/all_to_all | solution.py:195
  68.7 12.6 %panel_update.1 = (f32[512,512]{1,0:T(8,128)}, f32[512,256]{1,0:T(8,128)}) custom-call(s32[1]{0:T(128)} %bitcast.row_index, f32[256,256]{1,0:T(8,128)S(1)} %panel_inverse.1.inverse0, f32[16,24,256]{2,1,0:T(8,128)S(1)} %all-to-all-done.1.mixed, f32[16,3,16,256]{3,2,1,0:T(8,128)S(1)} %all-to-all-done.2.rest, f32[512,768]{1,0:T(8,128)S(1)} %bitcast.16, ...), custom_call_target="tpu_custom_call" | custom-call | tf_op jit(solution)/shard_map/panel_update/pallas_call | solution.py:249
  (8 shorter events, 0.1 us)
Async XLA Ops:
  0.6 3.4 %copy-start = (f32[1,512,768]{2,1,0:T(8,128)S(1)}, f32[1,512,768]{2,1,0:T(8,128)}, u32[]{:S(2)}) copy-start(f32[1,512,768]{2,1,0:T(8,128)} %param.2) | copy-start | bytes 4718596
  2.1 11.9 %collective-permute-start = (f32[16,40,256]{2,1,0:T(8,128)S(1)}, f32[16,40,256]{2,1,0:T(8,128)S(1)}, u32[]{:S(2)}, u32[]{:S(2)}) collective-permute-start(f32[16,40,256]{2,1,0:T(8,128)S(1)} %fusion.1), channel_id=1, source_target_pairs={{0,16},{16,32},{32,48},{48,64},{64,80},{80,96},{96,112},{112,128},... | collective-permute-start | bytes 1966088 | tf_op jit(solution)/shard_map/ppermute | solution.py:227
  14.9 21.0 %all-to-all-start = ((f32[16,40,256]{2,1,0:T(8,128)}), f32[16,40,256]{2,1,0:T(8,128)S(1)}, u32[]{:S(2)}, u32[]{:S(2)}) async-start(f32[16,40,256]{2,1,0:T(8,128)} %fusion.3), calls=%async_computation | async-start | bytes 1310720 | tf_op jit(solution)/shard_map/all_to_all | solution.py:195
  22.0 40.5 %collective-permute-start.1 = (f32[512,768]{1,0:T(8,128)}, f32[512,768]{1,0:T(8,128)}, u32[]{:S(2)}, u32[]{:S(2)}) collective-permute-start(f32[512,768]{1,0:T(8,128)} %bitcast.24), channel_id=1, source_target_pairs={{0,16},{16,32},{32,48},{48,64},{64,80},{80,96},{96,112},{112,128},... | collective-permute-start | bytes 4718600 | tf_op jit(solution)/shard_map/ppermute | solution.py:231
  36.7 13.8 %all-to-all-start.1 = ((f32[16,24,256]{2,1,0:T(8,128)}), f32[16,24,256]{2,1,0:T(8,128)S(1)}, u32[]{:S(2)}, u32[]{:S(2)}) async-start(f32[16,24,256]{2,1,0:T(8,128)} %broadcast_in_dim.53), calls=%async_computation.1 | async-start | bytes 786432 | tf_op jit(solution)/shard_map/all_to_all | solution.py:195
  51.4 17.2 %all-to-all-start.2 = ((f32[16,3,16,256]{3,2,1,0:T(8,128)}), f32[16,3,16,256]{3,2,1,0:T(8,128)S(1)}, u32[]{:S(2)}, u32[]{:S(2)}) async-start(f32[16,3,16,256]{3,2,1,0:T(8,128)} %broadcast_in_dim.51), calls=%async_computation.2 | async-start | bytes 1572864 | tf_op jit(solution)/shard_map/all_to_all | solution.py:195

commit v7 on v6

--- a/solution.py
+++ b/solution.py
@@ -42,18 +42,30 @@
         u = [jnp.broadcast_to(start[i : i + 1, :], (SUB, NB)) for i in range(SUB)]
         inv = [None] * SUB
         low = [[None] * SUB for _ in range(SUB)]
-        for j in range(0, SUB, 2):
-            p, q = a[j][j], a[j + 1][j]
-            det = p * a[j + 1][j + 1] - q * q
+        for j in range(0, SUB, 4):
+            p, q, r = a[j][j], a[j + 1][j], a[j + 1][j + 1]
+            det = p * r - q * q
+            left = {m: r * a[m][j] - q * a[m][j + 1] for m in (j + 2, j + 3)}
+            right = {m: p * a[m][j + 1] - q * a[m][j] for m in (j + 2, j + 3)}
+            scaled = lambda m, n: det * a[m][n] - (a[n][j] * left[m] + a[n][j + 1] * right[m])
+            third = scaled(j + 2, j + 2)
+            cross = scaled(j + 3, j + 2)
+            both = third * scaled(j + 3, j + 3) - cross * cross
             inv[j] = lax.rsqrt(p)
-            inv[j + 1] = (p * inv[j]) * lax.rsqrt(det)
-            for k in range(j + 1, SUB):
-                low[k][j] = a[k][j] * inv[j]
-            for k in range(j + 2, SUB):
-                low[k][j + 1] = (a[k][j + 1] - low[k][j] * low[j + 1][j]) * inv[j + 1]
-                for m in range(j + 2, k + 1):
-                    a[k][m] = a[k][m] - low[k][j] * low[m][j]
-                    a[k][m] = a[k][m] - low[k][j + 1] * low[m][j + 1]
+            root, root_third = lax.rsqrt(det), lax.rsqrt(third)
+            inv[j + 1] = (p * inv[j]) * root
+            inv[j + 2] = (det * root) * root_third
+            inv[j + 3] = ((det * root) * (third * root_third)) * lax.rsqrt(both)
+            for c in range(j, j + 4):
+                for k in range(c + 1, SUB):
+                    value = a[k][c]
+                    for e in range(j, c):
+                        value = value - low[k][e] * low[c][e]
+                    low[k][c] = value * inv[c]
+            for k in range(j + 4, SUB):
+                for m in range(j + 4, k + 1):
+                    for c in range(j, j + 4):
+                        a[k][m] = a[k][m] - low[k][c] * low[m][c]
         wide = lambda x: jnp.concatenate([x, x], axis=1)
         for j in range(SUB):
             u[j] = u[j] * wide(inv[j])
@@ -91,7 +103,20 @@
     )
 
 
-def invert_factor(work, between=None):
+def scales(diagonal):
+    row = lax.rsqrt(diagonal)
+    on_diagonal = lax.broadcasted_iota(jnp.int32, (NB, NB), 0) == lax.broadcasted_iota(
+        jnp.int32, (NB, NB), 1)
+    return row, jnp.sum(jnp.where(on_diagonal, row, 0.0), axis=1, keepdims=True)
+
+
+def diagonal_of(block):
+    on_diagonal = lax.broadcasted_iota(jnp.int32, (NB, NB), 0) == lax.broadcasted_iota(
+        jnp.int32, (NB, NB), 1)
+    return jnp.sum(jnp.where(on_diagonal, block, 0.0), axis=0, keepdims=True)
+
+
+def invert_factor(work, scale, between=None):
     groups = STRIP // SUB
     for half in range(NB // LANES):
         top = half * LANES
@@ -106,7 +131,7 @@
             lane = lax.broadcasted_iota(jnp.int32, (STRIP, NB), 1)
             row = lax.broadcasted_iota(jnp.int32, (STRIP, NB), 0) + first
             strip = jnp.where((lane > row) & (lane < after), 0.0, strip)
-            work[first:after, :] = jnp.where(lane < after, strip, 0.0)
+            work[first:after, :] = jnp.where(lane < after, strip, 0.0) * scale
             end = top + LANES
             if after < end:
                 update = gram(thirds(strip), columns)[after - top :, :]
@@ -131,8 +156,10 @@
 
 
 def first_kernel(mixed, inverse):
-    inverse[...] = block_of(mixed[:, :PART])
-    invert_factor(inverse)
+    block = block_of(mixed[:, :PART])
+    row, column = scales(diagonal_of(block))
+    inverse[...] = block * row * column
+    invert_factor(inverse, row)
 
 
 def second_kernel(
@@ -148,7 +175,9 @@
     diagonal = jnp.concatenate([diagonal] * (NB // STRIP), axis=0)
     block = jnp.where(strip_row < strip_col, block_of(mixed[:, :PART]).T, diagonal)
     w1 = dot(x0, block_of(rest[:, 0]), (1, 0))
-    work[...] = block - dot(w1, w1, (0, 0))
+    scale, column = scales(diagonal_of(diagonal) - jnp.sum(w1 * w1, axis=0, keepdims=True))
+    reduced = block[:LANES] - dot(w1[:, :LANES], w1, (0, 0))
+    work[:LANES, :] = reduced * scale * column[:LANES]
     w2 = dot(x0, block_of(rest[:, 1]), (1, 1))
     cross = block_of(rest[:, 2]) - dot(w2, w1, (0, 0))
     rows_here = own.shape[0]
@@ -165,6 +194,8 @@
     def between(s):
         at = pl.ds(s % steps * piece, piece)
         if s == 0:
+            reduced = block[LANES:] - dot(w1[:, LANES:], w1, (0, 0))
+            work[LANES:, :] = reduced * scale * column[LANES:]
             fetch.wait()
         if s < steps:
             lower = dot(own[at, :NB] - before[at, :NB], x0, (1, 1))
@@ -179,7 +210,7 @@
         right[at, :LANES] = jnp.where(row[s % steps * piece :][:piece, :LANES] >= NB, lower, 0.0)
         tail[at, :] = tail[at, :] - dot(lower, window[0], (1, 0))
 
-    invert_factor(work, between)
+    invert_factor(work, scale, between)
     x1 = work[LANES:, :]
     window.append(dot(x1, cross, (1, 1)))
     lower = dot(middle[...], x1, (1, 1))

time: 81.7 us -> 81.6 us (level)
  no operation moved by 1% of the time
where the time goes in v7:
time: 81.6 us; the launch traced here: 81.1 us
  waiting for transfers between devices  37.5 us (46%)
  Pallas kernels  20.1 us (25%)
  starting transfers between devices  18.5 us (23%)
  other arithmetic  2.49 us (3%)
  local copies, waits for them, and re-layouts  1.76 us (2%)
    all_to_all x3, waiting for transfers between devices, exchange(): return lax.all_to_all(blocks, 'row', 0, 0, tiled=True)  27.7 us
    all_to_all x3, starting transfers between devices, exchange(): return lax.all_to_all(blocks, 'row', 0, 0, tiled=True)  14.2 us
    pallas_call x1, Pallas kernels, per_device(): pl.pallas_call(second_kernel, out_shape=(jax.ShapeDtypeStruct((rows_here,...  12.5 us
    ppermute x1, waiting for transfers between devices, per_device(): came = lax.ppermute(sent, 'slab', pairs)  9.81 us
    pallas_call x1, Pallas kernels, per_device(): pl.pallas_call(first_kernel, out_shape=jax.ShapeDtypeStruct((NB, NB), jnp...  7.6 us
    ppermute x1, starting transfers between devices, per_device(): prev = lax.ppermute(out, 'slab', pairs)  2.39 us
    ppermute x1, starting transfers between devices, per_device(): came = lax.ppermute(sent, 'slab', pairs)  1.92 us
    broadcast_in_dim x3, local copies, waits for them, and re-layouts, copies(): return jnp.broadcast_to(share[None], (count,) + share.shape)  1.75 us
  transfers between devices with their start and end apart: 5, of which 4 were waited for; matrix products, arithmetic and copies ran while one was open for 2% of the time, Pallas kernels for 9%

profile of v7, /device:TPU:224, one launch (start us, length us, event | category | flops | bytes accessed | tf_op | source)
XLA Modules:
  0.0 81.1 jit_solution(812409769518547270)
XLA Ops:
  0.6 0.0 copy-start
  0.7 1.3 %slice_select_fusion = (f32[256,256]{1,0:T(8,128)S(1)}, f32[256,256]{1,0:T(8,128)S(1)}, f32[256,256]{1,0:T(8,128)S(1)}) fusion(f32[512,768]{1,0:T(8,128)} %bitcast.23, s32[256]{0:T(256)S(1)} %and_select_fusion, pred[]{:T(512)S(6)} %eq.35), kind=kLoop, calls=%fused_computation.7 | loop fusion | flops 196608 | bytes 1574913 | tf_op jit(solution)/shard_map/jit(_where)/select_n | solution.py:233
  2.1 1.9 %collective-permute-start = (f32[16,40,256]{2,1,0:T(8,128)S(1)}, f32[16,40,256]{2,1,0:T(8,128)S(1)}, u32[]{:S(2)}, u32[]{:S(2)}) collective-permute-start(f32[16,40,256]{2,1,0:T(8,128)S(1)} %fusion.1), channel_id=1, source_target_pairs={{0,16},{16,32},{32,48},{48,64},{64,80},{80,96},{96,112},{112,128},... | collective-permute-start | bytes 1966088 | tf_op jit(solution)/shard_map/ppermute | solution.py:258
  4.0 0.0 copy-done
  4.0 0.1 slice_select_fusion.1
  4.2 9.8 %collective-permute-done = f32[16,40,256]{2,1,0:T(8,128)S(1)} collective-permute-done((f32[16,40,256]{2,1,0:T(8,128)S(1)}, f32[16,40,256]{2,1,0:T(8,128)S(1)}, u32[]{:S(2)}, u32[]{:S(2)}) %collective-permute-start) | collective-permute-done | bytes 655392 | tf_op jit(solution)/shard_map/ppermute | solution.py:258
  14.0 0.9 %fusion.3 = f32[16,40,256]{2,1,0:T(8,128)} fusion(f32[16,40,256]{2,1,0:T(8,128)S(1)} %collective-permute-done, f32[16,16,256]{2,1,0:T(8,128)S(1)} %bitcast.18, f32[4,8,256]{2,1,0:T(8,128)S(1)} %bitcast.25, f32[16,16,256]{2,1,0:T(8,128)S(1)} %bitcast.17), kind=kLoop, calls=%fused_computation.19 | loop fusion | flops 1146880 | bytes 1867776 | tf_op jit(solution)/shard_map/sub | solution.py:263
  14.9 7.0 %all-to-all-start = ((f32[16,40,256]{2,1,0:T(8,128)}), f32[16,40,256]{2,1,0:T(8,128)S(1)}, u32[]{:S(2)}, u32[]{:S(2)}) async-start(f32[16,40,256]{2,1,0:T(8,128)} %fusion.3), calls=%async_computation | async-start | bytes 1310720 | tf_op jit(solution)/shard_map/all_to_all | solution.py:226
  22.0 2.4 %collective-permute-start.1 = (f32[512,768]{1,0:T(8,128)}, f32[512,768]{1,0:T(8,128)}, u32[]{:S(2)}, u32[]{:S(2)}) collective-permute-start(f32[512,768]{1,0:T(8,128)} %bitcast.24), channel_id=1, source_target_pairs={{0,16},{16,32},{32,48},{48,64},{64,80},{80,96},{96,112},{112,128},... | collective-permute-start | bytes 4718600 | tf_op jit(solution)/shard_map/ppermute | solution.py:262
  24.4 11.6 %all-to-all-done = f32[16,40,256]{2,1,0:T(8,128)S(1)} async-done(((f32[16,40,256]{2,1,0:T(8,128)}), f32[16,40,256]{2,1,0:T(8,128)S(1)}, u32[]{:S(2)}, u32[]{:S(2)}) %all-to-all-start) | async-done | bytes 655392 | tf_op jit(solution)/shard_map/all_to_all | solution.py:226
  35.9 0.8 broadcast_in_dim.53
  36.7 3.6 %all-to-all-start.1 = ((f32[16,24,256]{2,1,0:T(8,128)}), f32[16,24,256]{2,1,0:T(8,128)S(1)}, u32[]{:S(2)}, u32[]{:S(2)}) async-start(f32[16,24,256]{2,1,0:T(8,128)} %broadcast_in_dim.53), calls=%async_computation.1 | async-start | bytes 786432 | tf_op jit(solution)/shard_map/all_to_all | solution.py:226
  40.3 10.2 %all-to-all-done.1.mixed = f32[16,24,256]{2,1,0:T(8,128)S(1)} async-done(((f32[16,24,256]{2,1,0:T(8,128)}), f32[16,24,256]{2,1,0:T(8,128)S(1)}, u32[]{:S(2)}, u32[]{:S(2)}) %all-to-all-start.1) | async-done | bytes 393248 | tf_op jit(solution)/shard_map/all_to_all | solution.py:226
  50.5 1.0 %broadcast_in_dim.51 = f32[16,3,16,256]{3,2,1,0:T(8,128)} broadcast(f32[3,16,256]{2,1,0:T(8,128)S(1)} %pad_maximum_fusion), dimensions={1,2,3} | broadcast | bytes 835584 | tf_op jit(solution)/shard_map/broadcast_in_dim | solution.py:243
  51.4 3.6 %all-to-all-start.2 = ((f32[16,3,16,256]{3,2,1,0:T(8,128)}), f32[16,3,16,256]{3,2,1,0:T(8,128)S(1)}, u32[]{:S(2)}, u32[]{:S(2)}) async-start(f32[16,3,16,256]{3,2,1,0:T(8,128)} %broadcast_in_dim.51), calls=%async_computation.2 | async-start | bytes 1572864 | tf_op jit(solution)/shard_map/all_to_all | solution.py:226
  55.1 7.6 %panel_inverse.1.inverse0 = f32[256,256]{1,0:T(8,128)S(1)} custom-call(f32[16,24,256]{2,1,0:T(8,128)S(1)} %all-to-all-done.1.mixed), custom_call_target="tpu_custom_call" | custom-call | flops 6710886400 | bytes 524288 | tf_op jit(solution)/shard_map/panel_inverse/pallas_call | solution.py:269
  62.7 0.0 collective-permute-done.1.prev
  62.7 6.0 %all-to-all-done.2.rest = f32[16,3,16,256]{3,2,1,0:T(8,128)S(1)} async-done(((f32[16,3,16,256]{3,2,1,0:T(8,128)}), f32[16,3,16,256]{3,2,1,0:T(8,128)S(1)}, u32[]{:S(2)}, u32[]{:S(2)}) %all-to-all-start.2) | async-done | bytes 786464 | tf_op jit(solution)/shard_map/all_to_all | solution.py:226
  68.7 12.5 %panel_update.1 = (f32[512,512]{1,0:T(8,128)}, f32[512,256]{1,0:T(8,128)}) custom-call(s32[1]{0:T(128)} %bitcast.row_index, f32[256,256]{1,0:T(8,128)S(1)} %panel_inverse.1.inverse0, f32[16,24,256]{2,1,0:T(8,128)S(1)} %all-to-all-done.1.mixed, f32[16,3,16,256]{3,2,1,0:T(8,128)S(1)} %all-to-all-done.2.rest, f32[512,768]{1,0:T(8,128)S(1)} %bitcast.16, ...), custom_call_target="tpu_custom_call" | custom-call | tf_op jit(solution)/shard_map/panel_update/pallas_call | solution.py:280
  (8 shorter events, 0.1 us)
Async XLA Ops:
  0.6 3.4 %copy-start = (f32[1,512,768]{2,1,0:T(8,128)S(1)}, f32[1,512,768]{2,1,0:T(8,128)}, u32[]{:S(2)}) copy-start(f32[1,512,768]{2,1,0:T(8,128)} %param.2) | copy-start | bytes 4718596
  2.1 11.9 %collective-permute-start = (f32[16,40,256]{2,1,0:T(8,128)S(1)}, f32[16,40,256]{2,1,0:T(8,128)S(1)}, u32[]{:S(2)}, u32[]{:S(2)}) collective-permute-start(f32[16,40,256]{2,1,0:T(8,128)S(1)} %fusion.1), channel_id=1, source_target_pairs={{0,16},{16,32},{32,48},{48,64},{64,80},{80,96},{96,112},{112,128},... | collective-permute-start | bytes 1966088 | tf_op jit(solution)/shard_map/ppermute | solution.py:258
  14.9 21.0 %all-to-all-start = ((f32[16,40,256]{2,1,0:T(8,128)}), f32[16,40,256]{2,1,0:T(8,128)S(1)}, u32[]{:S(2)}, u32[]{:S(2)}) async-start(f32[16,40,256]{2,1,0:T(8,128)} %fusion.3), calls=%async_computation | async-start | bytes 1310720 | tf_op jit(solution)/shard_map/all_to_all | solution.py:226
  22.0 40.7 %collective-permute-start.1 = (f32[512,768]{1,0:T(8,128)}, f32[512,768]{1,0:T(8,128)}, u32[]{:S(2)}, u32[]{:S(2)}) collective-permute-start(f32[512,768]{1,0:T(8,128)} %bitcast.24), channel_id=1, source_target_pairs={{0,16},{16,32},{32,48},{48,64},{64,80},{80,96},{96,112},{112,128},... | collective-permute-start | bytes 4718600 | tf_op jit(solution)/shard_map/ppermute | solution.py:262
  36.7 13.8 %all-to-all-start.1 = ((f32[16,24,256]{2,1,0:T(8,128)}), f32[16,24,256]{2,1,0:T(8,128)S(1)}, u32[]{:S(2)}, u32[]{:S(2)}) async-start(f32[16,24,256]{2,1,0:T(8,128)} %broadcast_in_dim.53), calls=%async_computation.1 | async-start | bytes 786432 | tf_op jit(solution)/shard_map/all_to_all | solution.py:226
  51.4 17.2 %all-to-all-start.2 = ((f32[16,3,16,256]{3,2,1,0:T(8,128)}), f32[16,3,16,256]{3,2,1,0:T(8,128)S(1)}, u32[]{:S(2)}, u32[]{:S(2)}) async-start(f32[16,3,16,256]{3,2,1,0:T(8,128)} %broadcast_in_dim.51), calls=%async_computation.2 | async-start | bytes 1572864 | tf_op jit(solution)/shard_map/all_to_all | solution.py:226

commit v8 on v7

--- a/solution.py
+++ b/solution.py
@@ -255,7 +255,8 @@
     params = pltpu.CompilerParams(vmem_limit_bytes=VMEM_BYTES)
 
     sent = head_shares(out, row_index, count)
-    came = lax.ppermute(sent, "slab", pairs)
+    holders = [(s * count + r, t * count + r) for s, t in pairs for r in range(2)]
+    came = lax.ppermute(sent, ("slab", "row"), holders)
     own, _ = lax.optimization_barrier((own, sent))
     kept = head_shares(own, row_index, count)
     out, _ = lax.optimization_barrier((out, kept))

time: 81.6 us -> 79.2 us (0.971)
  starting transfers between devices: 18.5 us -> 15.4 us
    all_to_all x3, starting transfers between devices: 14.2 us -> 10.8 us  [exchange(): return lax.all_to_all(blocks, 'row', 0, 0, tiled=True)]
  transfers between devices with their start and end apart: 5 -> 5, of which waited for: 4 -> 4; matrix products, arithmetic and copies ran while one was open for 2% -> 2% of each run, Pallas kernels for 9% -> 10%
where the time goes in v8:
time: 79.2 us; the launch traced here: 78.7 us
  waiting for transfers between devices  38.3 us (48%)
  Pallas kernels  20.1 us (25%)
  starting transfers between devices  15.4 us (19%)
  other arithmetic  2.49 us (3%)
  local copies, waits for them, and re-layouts  1.76 us (2%)
    all_to_all x3, waiting for transfers between devices, exchange(): return lax.all_to_all(blocks, 'row', 0, 0, tiled=True)  28.5 us
    pallas_call x1, Pallas kernels, per_device(): pl.pallas_call(second_kernel, out_shape=(jax.ShapeDtypeStruct((rows_here,...  12.5 us
    all_to_all x3, starting transfers between devices, exchange(): return lax.all_to_all(blocks, 'row', 0, 0, tiled=True)  10.8 us
    ppermute x1, waiting for transfers between devices, per_device(): came = lax.ppermute(sent, ('slab', 'row'), holders)  9.81 us
    pallas_call x1, Pallas kernels, per_device(): pl.pallas_call(first_kernel, out_shape=jax.ShapeDtypeStruct((NB, NB), jnp...  7.6 us
    ppermute x1, starting transfers between devices, per_device(): prev = lax.ppermute(out, 'slab', pairs)  2.67 us
    ppermute x1, starting transfers between devices, per_device(): came = lax.ppermute(sent, ('slab', 'row'), holders)  1.92 us
    broadcast_in_dim x3, local copies, waits for them, and re-layouts, copies(): return jnp.broadcast_to(share[None], (count,) + share.shape)  1.75 us
  transfers between devices with their start and end apart: 5, of which 4 were waited for; matrix products, arithmetic and copies ran while one was open for 2% of the time, Pallas kernels for 10%

profile of v8, /device:TPU:224, one launch (start us, length us, event | category | flops | bytes accessed | tf_op | source)
XLA Modules:
  0.0 78.7 jit_solution(10733812388011010005)
XLA Ops:
  0.6 0.0 copy-start
  0.7 1.3 %slice_select_fusion = (f32[256,256]{1,0:T(8,128)S(1)}, f32[256,256]{1,0:T(8,128)S(1)}, f32[256,256]{1,0:T(8,128)S(1)}) fusion(f32[512,768]{1,0:T(8,128)} %bitcast.23, s32[256]{0:T(256)S(1)} %and_select_fusion, pred[]{:T(512)S(6)} %eq.35), kind=kLoop, calls=%fused_computation.7 | loop fusion | flops 196608 | bytes 1574913 | tf_op jit(solution)/shard_map/jit(_where)/select_n | solution.py:233
  2.1 1.9 %collective-permute-start = (f32[16,40,256]{2,1,0:T(8,128)S(1)}, f32[16,40,256]{2,1,0:T(8,128)S(1)}, u32[]{:S(2)}, u32[]{:S(2)}) collective-permute-start(f32[16,40,256]{2,1,0:T(8,128)S(1)} %fusion.1), channel_id=1, source_target_pairs={{0,16},{1,17},{16,32},{17,33},{32,48},{33,49},{48,64},{49,65},{64,... | collective-permute-start | bytes 1966088 | tf_op jit(solution)/shard_map/ppermute | solution.py:259
  4.0 0.0 copy-done
  4.0 0.1 slice_select_fusion.1
  4.2 9.8 %collective-permute-done = f32[16,40,256]{2,1,0:T(8,128)S(1)} collective-permute-done((f32[16,40,256]{2,1,0:T(8,128)S(1)}, f32[16,40,256]{2,1,0:T(8,128)S(1)}, u32[]{:S(2)}, u32[]{:S(2)}) %collective-permute-start) | collective-permute-done | bytes 655392 | tf_op jit(solution)/shard_map/ppermute | solution.py:259
  14.0 0.9 %fusion.3 = f32[16,40,256]{2,1,0:T(8,128)} fusion(f32[16,40,256]{2,1,0:T(8,128)S(1)} %collective-permute-done, f32[16,16,256]{2,1,0:T(8,128)S(1)} %bitcast.18, f32[4,8,256]{2,1,0:T(8,128)S(1)} %bitcast.25, f32[16,16,256]{2,1,0:T(8,128)S(1)} %bitcast.17), kind=kLoop, calls=%fused_computation.19 | loop fusion | flops 1146880 | bytes 1867776 | tf_op jit(solution)/shard_map/sub | solution.py:264
  14.9 3.6 %all-to-all-start = ((f32[16,40,256]{2,1,0:T(8,128)}), f32[16,40,256]{2,1,0:T(8,128)S(1)}, u32[]{:S(2)}, u32[]{:S(2)}) async-start(f32[16,40,256]{2,1,0:T(8,128)} %fusion.3), calls=%async_computation | async-start | bytes 1310720 | tf_op jit(solution)/shard_map/all_to_all | solution.py:226
  18.5 2.7 %collective-permute-start.1 = (f32[512,768]{1,0:T(8,128)}, f32[512,768]{1,0:T(8,128)}, u32[]{:S(2)}, u32[]{:S(2)}) collective-permute-start(f32[512,768]{1,0:T(8,128)} %bitcast.24), channel_id=1, source_target_pairs={{0,16},{16,32},{32,48},{48,64},{64,80},{80,96},{96,112},{112,128},... | collective-permute-start | bytes 4718600 | tf_op jit(solution)/shard_map/ppermute | solution.py:263
  21.2 11.9 %all-to-all-done = f32[16,40,256]{2,1,0:T(8,128)S(1)} async-done(((f32[16,40,256]{2,1,0:T(8,128)}), f32[16,40,256]{2,1,0:T(8,128)S(1)}, u32[]{:S(2)}, u32[]{:S(2)}) %all-to-all-start) | async-done | bytes 655392 | tf_op jit(solution)/shard_map/all_to_all | solution.py:226
  33.1 0.8 broadcast_in_dim.53
  33.9 3.6 %all-to-all-start.1 = ((f32[16,24,256]{2,1,0:T(8,128)}), f32[16,24,256]{2,1,0:T(8,128)S(1)}, u32[]{:S(2)}, u32[]{:S(2)}) async-start(f32[16,24,256]{2,1,0:T(8,128)} %broadcast_in_dim.53), calls=%async_computation.1 | async-start | bytes 786432 | tf_op jit(solution)/shard_map/all_to_all | solution.py:226
  37.5 10.4 %all-to-all-done.1.mixed = f32[16,24,256]{2,1,0:T(8,128)S(1)} async-done(((f32[16,24,256]{2,1,0:T(8,128)}), f32[16,24,256]{2,1,0:T(8,128)S(1)}, u32[]{:S(2)}, u32[]{:S(2)}) %all-to-all-start.1) | async-done | bytes 393248 | tf_op jit(solution)/shard_map/all_to_all | solution.py:226
  47.9 1.0 %broadcast_in_dim.51 = f32[16,3,16,256]{3,2,1,0:T(8,128)} broadcast(f32[3,16,256]{2,1,0:T(8,128)S(1)} %pad_maximum_fusion), dimensions={1,2,3} | broadcast | bytes 835584 | tf_op jit(solution)/shard_map/broadcast_in_dim | solution.py:243
  48.9 3.6 %all-to-all-start.2 = ((f32[16,3,16,256]{3,2,1,0:T(8,128)}), f32[16,3,16,256]{3,2,1,0:T(8,128)S(1)}, u32[]{:S(2)}, u32[]{:S(2)}) async-start(f32[16,3,16,256]{3,2,1,0:T(8,128)} %broadcast_in_dim.51), calls=%async_computation.2 | async-start | bytes 1572864 | tf_op jit(solution)/shard_map/all_to_all | solution.py:226
  52.5 7.6 %panel_inverse.1.inverse0 = f32[256,256]{1,0:T(8,128)S(1)} custom-call(f32[16,24,256]{2,1,0:T(8,128)S(1)} %all-to-all-done.1.mixed), custom_call_target="tpu_custom_call" | custom-call | flops 6710886400 | bytes 524288 | tf_op jit(solution)/shard_map/panel_inverse/pallas_call | solution.py:270
  60.1 0.0 collective-permute-done.1.prev
  60.1 6.1 %all-to-all-done.2.rest = f32[16,3,16,256]{3,2,1,0:T(8,128)S(1)} async-done(((f32[16,3,16,256]{3,2,1,0:T(8,128)}), f32[16,3,16,256]{3,2,1,0:T(8,128)S(1)}, u32[]{:S(2)}, u32[]{:S(2)}) %all-to-all-start.2) | async-done | bytes 786464 | tf_op jit(solution)/shard_map/all_to_all | solution.py:226
  66.2 12.5 %panel_update.1 = (f32[512,512]{1,0:T(8,128)}, f32[512,256]{1,0:T(8,128)}) custom-call(s32[1]{0:T(128)} %bitcast.row_index, f32[256,256]{1,0:T(8,128)S(1)} %panel_inverse.1.inverse0, f32[16,24,256]{2,1,0:T(8,128)S(1)} %all-to-all-done.1.mixed, f32[16,3,16,256]{3,2,1,0:T(8,128)S(1)} %all-to-all-done.2.rest, f32[512,768]{1,0:T(8,128)S(1)} %bitcast.16, ...), custom_call_target="tpu_custom_call" | custom-call | tf_op jit(solution)/shard_map/panel_update/pallas_call | solution.py:281
  (8 shorter events, 0.1 us)
Async XLA Ops:
  0.6 3.4 %copy-start = (f32[1,512,768]{2,1,0:T(8,128)S(1)}, f32[1,512,768]{2,1,0:T(8,128)}, u32[]{:S(2)}) copy-start(f32[1,512,768]{2,1,0:T(8,128)} %param.2) | copy-start | bytes 4718596
  2.1 11.9 %collective-permute-start = (f32[16,40,256]{2,1,0:T(8,128)S(1)}, f32[16,40,256]{2,1,0:T(8,128)S(1)}, u32[]{:S(2)}, u32[]{:S(2)}) collective-permute-start(f32[16,40,256]{2,1,0:T(8,128)S(1)} %fusion.1), channel_id=1, source_target_pairs={{0,16},{1,17},{16,32},{17,33},{32,48},{33,49},{48,64},{49,65},{64,... | collective-permute-start | bytes 1966088 | tf_op jit(solution)/shard_map/ppermute | solution.py:259
  14.9 18.2 %all-to-all-start = ((f32[16,40,256]{2,1,0:T(8,128)}), f32[16,40,256]{2,1,0:T(8,128)S(1)}, u32[]{:S(2)}, u32[]{:S(2)}) async-start(f32[16,40,256]{2,1,0:T(8,128)} %fusion.3), calls=%async_computation | async-start | bytes 1310720 | tf_op jit(solution)/shard_map/all_to_all | solution.py:226
  18.5 41.6 %collective-permute-start.1 = (f32[512,768]{1,0:T(8,128)}, f32[512,768]{1,0:T(8,128)}, u32[]{:S(2)}, u32[]{:S(2)}) collective-permute-start(f32[512,768]{1,0:T(8,128)} %bitcast.24), channel_id=1, source_target_pairs={{0,16},{16,32},{32,48},{48,64},{64,80},{80,96},{96,112},{112,128},... | collective-permute-start | bytes 4718600 | tf_op jit(solution)/shard_map/ppermute | solution.py:263
  33.9 14.0 %all-to-all-start.1 = ((f32[16,24,256]{2,1,0:T(8,128)}), f32[16,24,256]{2,1,0:T(8,128)S(1)}, u32[]{:S(2)}, u32[]{:S(2)}) async-start(f32[16,24,256]{2,1,0:T(8,128)} %broadcast_in_dim.53), calls=%async_computation.1 | async-start | bytes 786432 | tf_op jit(solution)/shard_map/all_to_all | solution.py:226
  48.9 17.4 %all-to-all-start.2 = ((f32[16,3,16,256]{3,2,1,0:T(8,128)}), f32[16,3,16,256]{3,2,1,0:T(8,128)S(1)}, u32[]{:S(2)}, u32[]{:S(2)}) async-start(f32[16,3,16,256]{3,2,1,0:T(8,128)} %broadcast_in_dim.51), calls=%async_computation.2 | async-start | bytes 1572864 | tf_op jit(solution)/shard_map/all_to_all | solution.py:226

commit v9 on v8

--- a/solution.py
+++ b/solution.py
@@ -9,6 +9,7 @@
 PANELW = 512
 COLS = 768
 PART = 16
+HALVES = 2 * PART
 STRIP = 32
 SUB = 8
 LANES = 128
@@ -152,11 +153,12 @@
 
 
 def block_of(shares):
-    return shares.reshape((NB, NB))
+    left, right = shares[:, :PART].reshape((NB, LANES)), shares[:, PART:].reshape((NB, LANES))
+    return jnp.concatenate([left, right], axis=1)
 
 
 def first_kernel(mixed, inverse):
-    block = block_of(mixed[:, :PART])
+    block = block_of(mixed[:, :HALVES])
     row, column = scales(diagonal_of(block))
     inverse[...] = block * row * column
     invert_factor(inverse, row)
@@ -171,9 +173,10 @@
     x0 = inverse0[...]
     strip_row = lax.broadcasted_iota(jnp.int32, (NB, NB), 0) // STRIP
     strip_col = lax.broadcasted_iota(jnp.int32, (NB, NB), 1) // STRIP
-    diagonal = mixed[: STRIP // SUB, PART:].reshape((STRIP, NB))
+    pieces = mixed[: 2 * STRIP // SUB, HALVES:].reshape((2 * STRIP, LANES))
+    diagonal = jnp.concatenate([pieces[:STRIP], pieces[STRIP:]], axis=1)
     diagonal = jnp.concatenate([diagonal] * (NB // STRIP), axis=0)
-    block = jnp.where(strip_row < strip_col, block_of(mixed[:, :PART]).T, diagonal)
+    block = jnp.where(strip_row < strip_col, block_of(mixed[:, :HALVES]).T, diagonal)
     w1 = dot(x0, block_of(rest[:, 0]), (1, 0))
     scale, column = scales(diagonal_of(diagonal) - jnp.sum(w1 * w1, axis=0, keepdims=True))
     reduced = block[:LANES] - dot(w1[:, :LANES], w1, (0, 0))
@@ -226,17 +229,43 @@
     return lax.all_to_all(blocks, "row", 0, 0, tiled=True)
 
 
+def share_kernel(row_index, block, shares):
+    strip_row = lax.broadcasted_iota(jnp.int32, (NB, NB), 0) // STRIP
+    strip_col = lax.broadcasted_iota(jnp.int32, (NB, NB), 1) // STRIP
+    upper = (strip_row <= strip_col) | (row_index[0] == 1)
+    mixed = jnp.where(upper, block[:NB, :NB], block[NB:, NB:])
+    strip = lax.broadcasted_iota(jnp.int32, (STRIP, NB), 1) // STRIP
+    diagonal = jnp.zeros((STRIP, NB), jnp.float32)
+    for i in range(NB // STRIP):
+        rows = block[NB + STRIP * i : NB + STRIP * (i + 1), NB:]
+        diagonal = jnp.where(strip == i, rows, diagonal)
+    count = shares.shape[0]
+    pieces = STRIP // SUB
+    half = lambda x, i: x[:, i * LANES : (i + 1) * LANES]
+    shares[2 * pieces :, HALVES : HALVES + SUB] = jnp.zeros(
+        (count - 2 * pieces, SUB, LANES), jnp.float32)
+    for i in range(2):
+        shares[i * pieces : (i + 1) * pieces, HALVES : HALVES + SUB] = half(diagonal, i).reshape(
+            (pieces, SUB, LANES))
+        shares[:, i * PART : (i + 1) * PART] = half(mixed, i).reshape((count, PART, LANES))
+        at = HALVES + SUB + i * PART
+        shares[:, at : at + PART] = half(block[:NB, NB:], i).reshape((count, PART, LANES))
+
+
 def head_shares(block, row_index, count):
-    first, second = block[:NB, :NB], block[NB:PANELW, NB:PANELW]
-    strip_row = jnp.arange(NB)[:, None] // STRIP
-    strip_col = jnp.arange(NB)[None, :] // STRIP
-    mixed = jnp.where((strip_row <= strip_col) | (row_index == 1), first, second)
-    strips = second.reshape(NB // STRIP, STRIP, NB)
-    own_strip = jnp.arange(NB // STRIP)[:, None, None] == strip_col[None]
-    diagonal = jnp.sum(jnp.where(own_strip, strips, 0.0), axis=0).reshape(-1, SUB, NB)
-    diagonal = jnp.pad(diagonal, ((0, count - diagonal.shape[0]), (0, 0), (0, 0)))
-    parts = [mixed.reshape(count, PART, NB), diagonal, block[:NB, NB:PANELW].reshape(count, PART, NB)]
-    return jnp.concatenate(parts, axis=1)
+    shape = (count, 2 * HALVES + SUB, LANES)
+    return pl.pallas_call(
+        share_kernel,
+        grid=(1,),
+        out_shape=jax.ShapeDtypeStruct(shape, jnp.float32),
+        in_specs=[
+            pl.BlockSpec(memory_space=pltpu.SMEM),
+            pl.BlockSpec((PANELW, PANELW), lambda i: (0, 0)),
+        ],
+        out_specs=pl.BlockSpec(shape, lambda i: (0, 0, 0)),
+        compiler_params=pltpu.CompilerParams(vmem_limit_bytes=VMEM_BYTES),
+        name="head_shares",
+    )(row_index[None], block)
 
 
 def copies(share, count):
@@ -262,8 +291,8 @@
     out, _ = lax.optimization_barrier((out, kept))
     prev = lax.ppermute(out, "slab", pairs)
     shares = exchange(kept - came)[:2]
-    mixed = exchange(copies(shares[0, : PART + SUB], count))
-    rest = jnp.stack([shares[0, PART + SUB :], shares[1, :PART], shares[1, PART + SUB :]])
+    mixed = exchange(copies(shares[0, : HALVES + SUB], count))
+    rest = jnp.stack([shares[0, HALVES + SUB :], shares[1, :HALVES], shares[1, HALVES + SUB :]])
     rest, mixed = lax.optimization_barrier((copies(rest, count), mixed))
     rest = exchange(rest)
 

time: 79.2 us -> 76.8 us (0.970)
  waiting for transfers between devices: 38.3 us -> 36.1 us
  other arithmetic: 2.49 us -> 0.88 us
  Pallas kernels: 20.1 us -> 21.5 us
    all_to_all x3, waiting for transfers between devices: 28.5 us -> 26.9 us  [exchange(): return lax.all_to_all(blocks, 'row', 0, 0, tiled=True)]
    pallas_call x0 -> x2, Pallas kernels: none -> 1.47 us  [head_shares(): pl.pallas_call(share_kernel, grid=(1,), out_shape=jax.ShapeDtypeStruct(sh...]
    select_n x3 -> x0, other arithmetic: 1.46 us -> none  [the longest x2 1.45 us: head_shares(): jnp.where((strip_row <= strip_col) | (row_index == 1), first, second)]
where the time goes in v9:
time: 76.8 us; the launch traced here: 76.3 us
  waiting for transfers between devices  36.1 us (47%)
  Pallas kernels  21.5 us (28%)
  starting transfers between devices  15.3 us (20%)
  local copies, waits for them, and re-layouts  1.73 us (2%)
  other arithmetic  0.88 us (1%)
    all_to_all x3, waiting for transfers between devices, exchange(): return lax.all_to_all(blocks, 'row', 0, 0, tiled=True)  26.9 us
    pallas_call x1, Pallas kernels, per_device(): pl.pallas_call(second_kernel, out_shape=(jax.ShapeDtypeStruct((rows_here,...  12.5 us
    all_to_all x3, starting transfers between devices, exchange(): return lax.all_to_all(blocks, 'row', 0, 0, tiled=True)  10.7 us
    ppermute x1, waiting for transfers between devices, per_device(): came = lax.ppermute(sent, ('slab', 'row'), holders)  9.19 us
    pallas_call x1, Pallas kernels, per_device(): pl.pallas_call(first_kernel, out_shape=jax.ShapeDtypeStruct((NB, NB), jnp...  7.6 us
    ppermute x1, starting transfers between devices, per_device(): prev = lax.ppermute(out, 'slab', pairs)  2.67 us
    ppermute x1, starting transfers between devices, per_device(): came = lax.ppermute(sent, ('slab', 'row'), holders)  1.92 us
    broadcast_in_dim x3, local copies, waits for them, and re-layouts, copies(): return jnp.broadcast_to(share[None], (count,) + share.shape)  1.72 us
  transfers between devices with their start and end apart: 5, of which 4 were waited for; matrix products, arithmetic and copies ran while one was open for 2% of the time, Pallas kernels for 10%

profile of v9, /device:TPU:224, one launch (start us, length us, event | category | flops | bytes accessed | tf_op | source)
XLA Modules:
  0.0 76.3 jit_solution(16181678691618552343)
XLA Ops:
  0.6 0.0 copy-start
  0.6 1.4 %head_shares.2 = f32[16,72,128]{2,1,0:T(8,128)S(1)} custom-call(s32[1]{0:T(128)} %bitcast.row_index, f32[512,768]{1,0:T(8,128)} %bitcast.2.block), custom_call_target="tpu_custom_call" | custom-call | tf_op jit(solution)/shard_map/head_shares/pallas_call | solution.py:257
  2.1 1.9 %collective-permute-start = (f32[16,72,128]{2,1,0:T(8,128)S(1)}, f32[16,72,128]{2,1,0:T(8,128)S(1)}, u32[]{:S(2)}, u32[]{:S(2)}) collective-permute-start(f32[16,72,128]{2,1,0:T(8,128)S(1)} %head_shares.2), channel_id=1, source_target_pairs={{0,16},{1,17},{16,32},{17,33},{32,48},{33,49},{48,64},{49,65},{64,... | collective-permute-start | bytes 1769480 | tf_op jit(solution)/shard_map/ppermute | solution.py:288
  4.0 0.0 copy-done
  4.0 0.1 head_shares.3
  4.1 9.2 %collective-permute-done = f32[16,72,128]{2,1,0:T(8,128)S(1)} collective-permute-done((f32[16,72,128]{2,1,0:T(8,128)S(1)}, f32[16,72,128]{2,1,0:T(8,128)S(1)}, u32[]{:S(2)}, u32[]{:S(2)}) %collective-permute-start) | collective-permute-done | bytes 589856 | tf_op jit(solution)/shard_map/ppermute | solution.py:288
  13.3 0.9 %sub.3 = f32[16,72,128]{2,1,0:T(8,128)} subtract(f32[16,72,128]{2,1,0:T(8,128)S(1)} %head_shares.3, f32[16,72,128]{2,1,0:T(8,128)S(1)} %collective-permute-done) | non-fusion elementwise | flops 147456 | bytes 1769472 | tf_op jit(solution)/shard_map/sub | solution.py:293
  14.1 3.6 %all-to-all-start = ((f32[16,72,128]{2,1,0:T(8,128)}), f32[16,72,128]{2,1,0:T(8,128)S(1)}, u32[]{:S(2)}, u32[]{:S(2)}) async-start(f32[16,72,128]{2,1,0:T(8,128)} %sub.3), calls=%async_computation | async-start | bytes 1179648 | tf_op jit(solution)/shard_map/all_to_all | solution.py:229
  17.7 2.7 %collective-permute-start.1 = (f32[512,768]{1,0:T(8,128)}, f32[512,768]{1,0:T(8,128)}, u32[]{:S(2)}, u32[]{:S(2)}) collective-permute-start(f32[512,768]{1,0:T(8,128)} %bitcast.2.block), channel_id=1, source_target_pairs={{0,16},{16,32},{32,48},{48,64},{64,80},{80,96},{96,112},{112,128},... | collective-permute-start | bytes 4718600 | tf_op jit(solution)/shard_map/ppermute | solution.py:292
  20.4 11.1 %all-to-all-done = f32[16,72,128]{2,1,0:T(8,128)S(1)} async-done(((f32[16,72,128]{2,1,0:T(8,128)}), f32[16,72,128]{2,1,0:T(8,128)S(1)}, u32[]{:S(2)}, u32[]{:S(2)}) %all-to-all-start) | async-done | bytes 589856 | tf_op jit(solution)/shard_map/all_to_all | solution.py:229
  31.5 0.7 broadcast_in_dim.27
  32.2 3.5 %all-to-all-start.1 = ((f32[16,40,128]{2,1,0:T(8,128)}), f32[16,40,128]{2,1,0:T(8,128)S(1)}, u32[]{:S(2)}, u32[]{:S(2)}) async-start(f32[16,40,128]{2,1,0:T(8,128)} %broadcast_in_dim.27), calls=%async_computation.1 | async-start | bytes 655360 | tf_op jit(solution)/shard_map/all_to_all | solution.py:229
  35.8 9.7 %all-to-all-done.1.mixed = f32[16,40,128]{2,1,0:T(8,128)S(1)} async-done(((f32[16,40,128]{2,1,0:T(8,128)}), f32[16,40,128]{2,1,0:T(8,128)S(1)}, u32[]{:S(2)}, u32[]{:S(2)}) %all-to-all-start.1) | async-done | bytes 327712 | tf_op jit(solution)/shard_map/all_to_all | solution.py:229
  45.5 1.0 %broadcast_in_dim.25 = f32[16,3,32,128]{3,2,1,0:T(8,128)} broadcast(f32[3,32,128]{2,1,0:T(8,128)S(1)} %pad_maximum_fusion), dimensions={1,2,3} | broadcast | bytes 835584 | tf_op jit(solution)/shard_map/broadcast_in_dim | solution.py:272
  46.4 3.6 %all-to-all-start.2 = ((f32[16,3,32,128]{3,2,1,0:T(8,128)}), f32[16,3,32,128]{3,2,1,0:T(8,128)S(1)}, u32[]{:S(2)}, u32[]{:S(2)}) async-start(f32[16,3,32,128]{3,2,1,0:T(8,128)} %broadcast_in_dim.25), calls=%async_computation.2 | async-start | bytes 1572864 | tf_op jit(solution)/shard_map/all_to_all | solution.py:229
  50.1 7.6 %panel_inverse.1.inverse0 = f32[256,256]{1,0:T(8,128)S(1)} custom-call(f32[16,40,128]{2,1,0:T(8,128)S(1)} %all-to-all-done.1.mixed), custom_call_target="tpu_custom_call" | custom-call | flops 6710886400 | bytes 524288 | tf_op jit(solution)/shard_map/panel_inverse/pallas_call | solution.py:299
  57.7 0.0 collective-permute-done.1.prev
  57.7 6.2 %all-to-all-done.2.rest = f32[16,3,32,128]{3,2,1,0:T(8,128)S(1)} async-done(((f32[16,3,32,128]{3,2,1,0:T(8,128)}), f32[16,3,32,128]{3,2,1,0:T(8,128)S(1)}, u32[]{:S(2)}, u32[]{:S(2)}) %all-to-all-start.2) | async-done | bytes 786464 | tf_op jit(solution)/shard_map/all_to_all | solution.py:229
  63.9 12.5 %panel_update.1 = (f32[512,512]{1,0:T(8,128)}, f32[512,256]{1,0:T(8,128)}) custom-call(s32[1]{0:T(128)} %bitcast.row_index, f32[256,256]{1,0:T(8,128)S(1)} %panel_inverse.1.inverse0, f32[16,40,128]{2,1,0:T(8,128)S(1)} %all-to-all-done.1.mixed, f32[16,3,32,128]{3,2,1,0:T(8,128)S(1)} %all-to-all-done.2.rest, f32[512,768]{1,0:T(8,128)S(1)} %bitcast.8, ...), custom_call_target="tpu_custom_call" | custom-call | tf_op jit(solution)/shard_map/panel_update/pallas_call | solution.py:310
  (3 shorter events, 0.0 us)
Async XLA Ops:
  0.6 3.4 %copy-start = (f32[1,512,768]{2,1,0:T(8,128)S(1)}, f32[1,512,768]{2,1,0:T(8,128)}, u32[]{:S(2)}) copy-start(f32[1,512,768]{2,1,0:T(8,128)} %param.2) | copy-start | bytes 4718596
  2.1 11.2 %collective-permute-start = (f32[16,72,128]{2,1,0:T(8,128)S(1)}, f32[16,72,128]{2,1,0:T(8,128)S(1)}, u32[]{:S(2)}, u32[]{:S(2)}) collective-permute-start(f32[16,72,128]{2,1,0:T(8,128)S(1)} %head_shares.2), channel_id=1, source_target_pairs={{0,16},{1,17},{16,32},{17,33},{32,48},{33,49},{48,64},{49,65},{64,... | collective-permute-start | bytes 1769480 | tf_op jit(solution)/shard_map/ppermute | solution.py:288
  14.1 17.3 %all-to-all-start = ((f32[16,72,128]{2,1,0:T(8,128)}), f32[16,72,128]{2,1,0:T(8,128)S(1)}, u32[]{:S(2)}, u32[]{:S(2)}) async-start(f32[16,72,128]{2,1,0:T(8,128)} %sub.3), calls=%async_computation | async-start | bytes 1179648 | tf_op jit(solution)/shard_map/all_to_all | solution.py:229
  17.7 39.9 %collective-permute-start.1 = (f32[512,768]{1,0:T(8,128)}, f32[512,768]{1,0:T(8,128)}, u32[]{:S(2)}, u32[]{:S(2)}) collective-permute-start(f32[512,768]{1,0:T(8,128)} %bitcast.2.block), channel_id=1, source_target_pairs={{0,16},{16,32},{32,48},{48,64},{64,80},{80,96},{96,112},{112,128},... | collective-permute-start | bytes 4718600 | tf_op jit(solution)/shard_map/ppermute | solution.py:292
  32.2 13.2 %all-to-all-start.1 = ((f32[16,40,128]{2,1,0:T(8,128)}), f32[16,40,128]{2,1,0:T(8,128)S(1)}, u32[]{:S(2)}, u32[]{:S(2)}) async-start(f32[16,40,128]{2,1,0:T(8,128)} %broadcast_in_dim.27), calls=%async_computation.1 | async-start | bytes 655360 | tf_op jit(solution)/shard_map/all_to_all | solution.py:229
  46.4 17.4 %all-to-all-start.2 = ((f32[16,3,32,128]{3,2,1,0:T(8,128)}), f32[16,3,32,128]{3,2,1,0:T(8,128)S(1)}, u32[]{:S(2)}, u32[]{:S(2)}) async-start(f32[16,3,32,128]{3,2,1,0:T(8,128)} %broadcast_in_dim.25), calls=%async_computation.2 | async-start | bytes 1572864 | tf_op jit(solution)/shard_map/all_to_all | solution.py:229

commit v10 on v9

--- a/solution.py
+++ b/solution.py
@@ -88,6 +88,17 @@
     return rows
 
 
+def halves(x):
+    high = x.astype(jnp.bfloat16)
+    return high, (x - high.astype(jnp.float32)).astype(jnp.bfloat16)
+
+
+def dot_halves(a, b, contract):
+    product = lambda x, y: lax.dot_general(
+        x, y, ((contract[:1], contract[1:]), ((), ())), preferred_element_type=jnp.float32)
+    return product(a[0], b[0]) + (product(a[0], b[1]) + product(a[1], b[0]))
+
+
 def thirds(x):
     high = x.astype(jnp.bfloat16)
     rest = x - high.astype(jnp.float32)
@@ -194,6 +205,8 @@
         pltpu.make_async_copy(tail, trailing, leave.at[2]),
     ]
 
+    w2_halves = halves(w2)
+
     def between(s):
         at = pl.ds(s % steps * piece, piece)
         if s == 0:
@@ -204,22 +217,24 @@
             lower = dot(own[at, :NB] - before[at, :NB], x0, (1, 1))
             left[at, :] = lower
             middle[at, :] = own[at, NB:PANELW] - before[at, NB:PANELW] - dot(lower, w1, (1, 0))
-            tail[at, :] = own[at, PANELW:] - before[at, PANELW:] - dot(lower, w2, (1, 0))
+            update = dot_halves(halves(lower), w2_halves, (1, 0))
+            tail[at, :] = own[at, PANELW:] - before[at, PANELW:] - update
             return
         if s == steps:
             writes[0].start()
-            window.append(dot(work[:LANES, :LANES], cross[:, :LANES], (1, 1)))
+            window.append(halves(dot(work[:LANES, :LANES], cross[:, :LANES], (1, 1))))
         lower = dot(middle[at, :LANES], work[:LANES, :LANES], (1, 1))
         right[at, :LANES] = jnp.where(row[s % steps * piece :][:piece, :LANES] >= NB, lower, 0.0)
-        tail[at, :] = tail[at, :] - dot(lower, window[0], (1, 0))
+        tail[at, :] = tail[at, :] - dot_halves(halves(lower), window[0], (1, 0))
 
     invert_factor(work, scale, between)
     x1 = work[LANES:, :]
-    window.append(dot(x1, cross, (1, 1)))
+    window.append(halves(dot(x1, cross, (1, 1))))
     lower = dot(middle[...], x1, (1, 1))
     right[:, LANES:] = jnp.where(row[:, :LANES] >= NB, lower, 0.0)
     writes[1].start()
-    tail[...] = jnp.where(row >= PANELW, tail[...] - dot(lower, window[1], (1, 0)), 0.0)
+    total = tail[...] - dot_halves(halves(lower), window[1], (1, 0))
+    tail[...] = jnp.where(row >= PANELW, total, 0.0)
     writes[2].start()
     for write in writes:
         write.wait()

time: 76.8 us -> 77.2 us (level)
  no operation moved by 1% of the time
where the time goes in v10:
time: 77.2 us; the launch traced here: 76.8 us
  waiting for transfers between devices  36.1 us (47%)
  Pallas kernels  22 us (28%)
  starting transfers between devices  15.3 us (20%)
  local copies, waits for them, and re-layouts  1.73 us (2%)
  other arithmetic  0.88 us (1%)
    all_to_all x3, waiting for transfers between devices, exchange(): return lax.all_to_all(blocks, 'row', 0, 0, tiled=True)  26.9 us
    pallas_call x1, Pallas kernels, per_device(): pl.pallas_call(second_kernel, out_shape=(jax.ShapeDtypeStruct((rows_here,...  12.9 us
    all_to_all x3, starting transfers between devices, exchange(): return lax.all_to_all(blocks, 'row', 0, 0, tiled=True)  10.7 us
    ppermute x1, waiting for transfers between devices, per_device(): came = lax.ppermute(sent, ('slab', 'row'), holders)  9.19 us
    pallas_call x1, Pallas kernels, per_device(): pl.pallas_call(first_kernel, out_shape=jax.ShapeDtypeStruct((NB, NB), jnp...  7.6 us
    ppermute x1, starting transfers between devices, per_device(): prev = lax.ppermute(out, 'slab', pairs)  2.67 us
    ppermute x1, starting transfers between devices, per_device(): came = lax.ppermute(sent, ('slab', 'row'), holders)  1.92 us
    broadcast_in_dim x3, local copies, waits for them, and re-layouts, copies(): return jnp.broadcast_to(share[None], (count,) + share.shape)  1.72 us
  transfers between devices with their start and end apart: 5, of which 4 were waited for; matrix products, arithmetic and copies ran while one was open for 2% of the time, Pallas kernels for 10%

profile of v10, /device:TPU:224, one launch (start us, length us, event | category | flops | bytes accessed | tf_op | source)
XLA Modules:
  0.0 76.8 jit_solution(16276088374759954212)
XLA Ops:
  0.6 0.0 copy-start
  0.6 1.4 %head_shares.2 = f32[16,72,128]{2,1,0:T(8,128)S(1)} custom-call(s32[1]{0:T(128)} %bitcast.row_index, f32[512,768]{1,0:T(8,128)} %bitcast.2.block), custom_call_target="tpu_custom_call" | custom-call | tf_op jit(solution)/shard_map/head_shares/pallas_call | solution.py:272
  2.1 1.9 %collective-permute-start = (f32[16,72,128]{2,1,0:T(8,128)S(1)}, f32[16,72,128]{2,1,0:T(8,128)S(1)}, u32[]{:S(2)}, u32[]{:S(2)}) collective-permute-start(f32[16,72,128]{2,1,0:T(8,128)S(1)} %head_shares.2), channel_id=1, source_target_pairs={{0,16},{1,17},{16,32},{17,33},{32,48},{33,49},{48,64},{49,65},{64,... | collective-permute-start | bytes 1769480 | tf_op jit(solution)/shard_map/ppermute | solution.py:303
  4.0 0.0 copy-done
  4.0 0.1 head_shares.3
  4.1 9.2 %collective-permute-done = f32[16,72,128]{2,1,0:T(8,128)S(1)} collective-permute-done((f32[16,72,128]{2,1,0:T(8,128)S(1)}, f32[16,72,128]{2,1,0:T(8,128)S(1)}, u32[]{:S(2)}, u32[]{:S(2)}) %collective-permute-start) | collective-permute-done | bytes 589856 | tf_op jit(solution)/shard_map/ppermute | solution.py:303
  13.3 0.9 %sub.3 = f32[16,72,128]{2,1,0:T(8,128)} subtract(f32[16,72,128]{2,1,0:T(8,128)S(1)} %head_shares.3, f32[16,72,128]{2,1,0:T(8,128)S(1)} %collective-permute-done) | non-fusion elementwise | flops 147456 | bytes 1769472 | tf_op jit(solution)/shard_map/sub | solution.py:308
  14.1 3.6 %all-to-all-start = ((f32[16,72,128]{2,1,0:T(8,128)}), f32[16,72,128]{2,1,0:T(8,128)S(1)}, u32[]{:S(2)}, u32[]{:S(2)}) async-start(f32[16,72,128]{2,1,0:T(8,128)} %sub.3), calls=%async_computation | async-start | bytes 1179648 | tf_op jit(solution)/shard_map/all_to_all | solution.py:244
  17.7 2.7 %collective-permute-start.1 = (f32[512,768]{1,0:T(8,128)}, f32[512,768]{1,0:T(8,128)}, u32[]{:S(2)}, u32[]{:S(2)}) collective-permute-start(f32[512,768]{1,0:T(8,128)} %bitcast.2.block), channel_id=1, source_target_pairs={{0,16},{16,32},{32,48},{48,64},{64,80},{80,96},{96,112},{112,128},... | collective-permute-start | bytes 4718600 | tf_op jit(solution)/shard_map/ppermute | solution.py:307
  20.4 11.1 %all-to-all-done = f32[16,72,128]{2,1,0:T(8,128)S(1)} async-done(((f32[16,72,128]{2,1,0:T(8,128)}), f32[16,72,128]{2,1,0:T(8,128)S(1)}, u32[]{:S(2)}, u32[]{:S(2)}) %all-to-all-start) | async-done | bytes 589856 | tf_op jit(solution)/shard_map/all_to_all | solution.py:244
  31.5 0.7 broadcast_in_dim.27
  32.2 3.5 %all-to-all-start.1 = ((f32[16,40,128]{2,1,0:T(8,128)}), f32[16,40,128]{2,1,0:T(8,128)S(1)}, u32[]{:S(2)}, u32[]{:S(2)}) async-start(f32[16,40,128]{2,1,0:T(8,128)} %broadcast_in_dim.27), calls=%async_computation.1 | async-start | bytes 655360 | tf_op jit(solution)/shard_map/all_to_all | solution.py:244
  35.8 9.7 %all-to-all-done.1.mixed = f32[16,40,128]{2,1,0:T(8,128)S(1)} async-done(((f32[16,40,128]{2,1,0:T(8,128)}), f32[16,40,128]{2,1,0:T(8,128)S(1)}, u32[]{:S(2)}, u32[]{:S(2)}) %all-to-all-start.1) | async-done | bytes 327712 | tf_op jit(solution)/shard_map/all_to_all | solution.py:244
  45.5 1.0 %broadcast_in_dim.25 = f32[16,3,32,128]{3,2,1,0:T(8,128)} broadcast(f32[3,32,128]{2,1,0:T(8,128)S(1)} %pad_maximum_fusion), dimensions={1,2,3} | broadcast | bytes 835584 | tf_op jit(solution)/shard_map/broadcast_in_dim | solution.py:287
  46.4 3.6 %all-to-all-start.2 = ((f32[16,3,32,128]{3,2,1,0:T(8,128)}), f32[16,3,32,128]{3,2,1,0:T(8,128)S(1)}, u32[]{:S(2)}, u32[]{:S(2)}) async-start(f32[16,3,32,128]{3,2,1,0:T(8,128)} %broadcast_in_dim.25), calls=%async_computation.2 | async-start | bytes 1572864 | tf_op jit(solution)/shard_map/all_to_all | solution.py:244
  50.1 7.6 %panel_inverse.1.inverse0 = f32[256,256]{1,0:T(8,128)S(1)} custom-call(f32[16,40,128]{2,1,0:T(8,128)S(1)} %all-to-all-done.1.mixed), custom_call_target="tpu_custom_call" | custom-call | flops 6710886400 | bytes 524288 | tf_op jit(solution)/shard_map/panel_inverse/pallas_call | solution.py:314
  57.7 0.0 collective-permute-done.1.prev
  57.7 6.2 %all-to-all-done.2.rest = f32[16,3,32,128]{3,2,1,0:T(8,128)S(1)} async-done(((f32[16,3,32,128]{3,2,1,0:T(8,128)}), f32[16,3,32,128]{3,2,1,0:T(8,128)S(1)}, u32[]{:S(2)}, u32[]{:S(2)}) %all-to-all-start.2) | async-done | bytes 786464 | tf_op jit(solution)/shard_map/all_to_all | solution.py:244
  63.9 12.9 %panel_update.1 = (f32[512,512]{1,0:T(8,128)}, f32[512,256]{1,0:T(8,128)}) custom-call(s32[1]{0:T(128)} %bitcast.row_index, f32[256,256]{1,0:T(8,128)S(1)} %panel_inverse.1.inverse0, f32[16,40,128]{2,1,0:T(8,128)S(1)} %all-to-all-done.1.mixed, f32[16,3,32,128]{3,2,1,0:T(8,128)S(1)} %all-to-all-done.2.rest, f32[512,768]{1,0:T(8,128)S(1)} %bitcast.8, ...), custom_call_target="tpu_custom_call" | custom-call | tf_op jit(solution)/shard_map/panel_update/pallas_call | solution.py:325
  (3 shorter events, 0.0 us)
Async XLA Ops:
  0.6 3.4 %copy-start = (f32[1,512,768]{2,1,0:T(8,128)S(1)}, f32[1,512,768]{2,1,0:T(8,128)}, u32[]{:S(2)}) copy-start(f32[1,512,768]{2,1,0:T(8,128)} %param.2) | copy-start | bytes 4718596
  2.1 11.2 %collective-permute-start = (f32[16,72,128]{2,1,0:T(8,128)S(1)}, f32[16,72,128]{2,1,0:T(8,128)S(1)}, u32[]{:S(2)}, u32[]{:S(2)}) collective-permute-start(f32[16,72,128]{2,1,0:T(8,128)S(1)} %head_shares.2), channel_id=1, source_target_pairs={{0,16},{1,17},{16,32},{17,33},{32,48},{33,49},{48,64},{49,65},{64,... | collective-permute-start | bytes 1769480 | tf_op jit(solution)/shard_map/ppermute | solution.py:303
  14.1 17.3 %all-to-all-start = ((f32[16,72,128]{2,1,0:T(8,128)}), f32[16,72,128]{2,1,0:T(8,128)S(1)}, u32[]{:S(2)}, u32[]{:S(2)}) async-start(f32[16,72,128]{2,1,0:T(8,128)} %sub.3), calls=%async_computation | async-start | bytes 1179648 | tf_op jit(solution)/shard_map/all_to_all | solution.py:244
  17.7 39.9 %collective-permute-start.1 = (f32[512,768]{1,0:T(8,128)}, f32[512,768]{1,0:T(8,128)}, u32[]{:S(2)}, u32[]{:S(2)}) collective-permute-start(f32[512,768]{1,0:T(8,128)} %bitcast.2.block), channel_id=1, source_target_pairs={{0,16},{16,32},{32,48},{48,64},{64,80},{80,96},{96,112},{112,128},... | collective-permute-start | bytes 4718600 | tf_op jit(solution)/shard_map/ppermute | solution.py:307
  32.2 13.2 %all-to-all-start.1 = ((f32[16,40,128]{2,1,0:T(8,128)}), f32[16,40,128]{2,1,0:T(8,128)S(1)}, u32[]{:S(2)}, u32[]{:S(2)}) async-start(f32[16,40,128]{2,1,0:T(8,128)} %broadcast_in_dim.27), calls=%async_computation.1 | async-start | bytes 655360 | tf_op jit(solution)/shard_map/all_to_all | solution.py:244
  46.4 17.4 %all-to-all-start.2 = ((f32[16,3,32,128]{3,2,1,0:T(8,128)}), f32[16,3,32,128]{3,2,1,0:T(8,128)S(1)}, u32[]{:S(2)}, u32[]{:S(2)}) async-start(f32[16,3,32,128]{3,2,1,0:T(8,128)} %broadcast_in_dim.25), calls=%async_computation.2 | async-start | bytes 1572864 | tf_op jit(solution)/shard_map/all_to_all | solution.py:244

commit v11 on v9

--- a/solution.py
+++ b/solution.py
@@ -288,9 +288,9 @@
     came = lax.ppermute(sent, ("slab", "row"), holders)
     own, _ = lax.optimization_barrier((own, sent))
     kept = head_shares(own, row_index, count)
-    out, _ = lax.optimization_barrier((out, kept))
+    shares = exchange(kept - came)[:2]
+    out, _ = lax.optimization_barrier((out, shares))
     prev = lax.ppermute(out, "slab", pairs)
-    shares = exchange(kept - came)[:2]
     mixed = exchange(copies(shares[0, : HALVES + SUB], count))
     rest = jnp.stack([shares[0, HALVES + SUB :], shares[1, :HALVES], shares[1, HALVES + SUB :]])
     rest, mixed = lax.optimization_barrier((copies(rest, count), mixed))

time: 76.8 us -> 76.8 us (level)
  no operation moved by 1% of the time
where the time goes in v11:
time: 76.8 us; the launch traced here: 76.3 us
  waiting for transfers between devices  36.1 us (47%)
  Pallas kernels  21.5 us (28%)
  starting transfers between devices  15.3 us (20%)
  local copies, waits for them, and re-layouts  1.73 us (2%)
  other arithmetic  0.88 us (1%)
    all_to_all x3, waiting for transfers between devices, exchange(): return lax.all_to_all(blocks, 'row', 0, 0, tiled=True)  26.9 us
    pallas_call x1, Pallas kernels, per_device(): pl.pallas_call(second_kernel, out_shape=(jax.ShapeDtypeStruct((rows_here,...  12.5 us
    all_to_all x3, starting transfers between devices, exchange(): return lax.all_to_all(blocks, 'row', 0, 0, tiled=True)  10.7 us
    ppermute x1, waiting for transfers between devices, per_device(): came = lax.ppermute(sent, ('slab', 'row'), holders)  9.19 us
    pallas_call x1, Pallas kernels, per_device(): pl.pallas_call(first_kernel, out_shape=jax.ShapeDtypeStruct((NB, NB), jnp...  7.6 us
    ppermute x1, starting transfers between devices, per_device(): prev = lax.ppermute(out, 'slab', pairs)  2.67 us
    ppermute x1, starting transfers between devices, per_device(): came = lax.ppermute(sent, ('slab', 'row'), holders)  1.92 us
    broadcast_in_dim x3, local copies, waits for them, and re-layouts, copies(): return jnp.broadcast_to(share[None], (count,) + share.shape)  1.72 us
  transfers between devices with their start and end apart: 5, of which 4 were waited for; matrix products, arithmetic and copies ran while one was open for 2% of the time, Pallas kernels for 10%

profile of v11, /device:TPU:224, one launch (start us, length us, event | category | flops | bytes accessed | tf_op | source)
XLA Modules:
  0.0 76.3 jit_solution(16181678691618552343)
XLA Ops:
  0.6 0.0 copy-start
  0.6 1.4 %head_shares.2 = f32[16,72,128]{2,1,0:T(8,128)S(1)} custom-call(s32[1]{0:T(128)} %bitcast.row_index, f32[512,768]{1,0:T(8,128)} %bitcast.2.block), custom_call_target="tpu_custom_call" | custom-call | tf_op jit(solution)/shard_map/head_shares/pallas_call | solution.py:257
  2.1 1.9 %collective-permute-start = (f32[16,72,128]{2,1,0:T(8,128)S(1)}, f32[16,72,128]{2,1,0:T(8,128)S(1)}, u32[]{:S(2)}, u32[]{:S(2)}) collective-permute-start(f32[16,72,128]{2,1,0:T(8,128)S(1)} %head_shares.2), channel_id=1, source_target_pairs={{0,16},{1,17},{16,32},{17,33},{32,48},{33,49},{48,64},{49,65},{64,... | collective-permute-start | bytes 1769480 | tf_op jit(solution)/shard_map/ppermute | solution.py:288
  4.0 0.0 copy-done
  4.0 0.1 head_shares.3
  4.1 9.2 %collective-permute-done = f32[16,72,128]{2,1,0:T(8,128)S(1)} collective-permute-done((f32[16,72,128]{2,1,0:T(8,128)S(1)}, f32[16,72,128]{2,1,0:T(8,128)S(1)}, u32[]{:S(2)}, u32[]{:S(2)}) %collective-permute-start) | collective-permute-done | bytes 589856 | tf_op jit(solution)/shard_map/ppermute | solution.py:288
  13.3 0.9 %sub.3 = f32[16,72,128]{2,1,0:T(8,128)} subtract(f32[16,72,128]{2,1,0:T(8,128)S(1)} %head_shares.3, f32[16,72,128]{2,1,0:T(8,128)S(1)} %collective-permute-done) | non-fusion elementwise | flops 147456 | bytes 1769472 | tf_op jit(solution)/shard_map/sub | solution.py:291
  14.1 3.6 %all-to-all-start = ((f32[16,72,128]{2,1,0:T(8,128)}), f32[16,72,128]{2,1,0:T(8,128)S(1)}, u32[]{:S(2)}, u32[]{:S(2)}) async-start(f32[16,72,128]{2,1,0:T(8,128)} %sub.3), calls=%async_computation | async-start | bytes 1179648 | tf_op jit(solution)/shard_map/all_to_all | solution.py:229
  17.7 2.7 %collective-permute-start.1 = (f32[512,768]{1,0:T(8,128)}, f32[512,768]{1,0:T(8,128)}, u32[]{:S(2)}, u32[]{:S(2)}) collective-permute-start(f32[512,768]{1,0:T(8,128)} %bitcast.2.block), channel_id=1, source_target_pairs={{0,16},{16,32},{32,48},{48,64},{64,80},{80,96},{96,112},{112,128},... | collective-permute-start | bytes 4718600 | tf_op jit(solution)/shard_map/ppermute | solution.py:293
  20.4 11.1 %all-to-all-done = f32[16,72,128]{2,1,0:T(8,128)S(1)} async-done(((f32[16,72,128]{2,1,0:T(8,128)}), f32[16,72,128]{2,1,0:T(8,128)S(1)}, u32[]{:S(2)}, u32[]{:S(2)}) %all-to-all-start) | async-done | bytes 589856 | tf_op jit(solution)/shard_map/all_to_all | solution.py:229
  31.5 0.7 broadcast_in_dim.27
  32.2 3.5 %all-to-all-start.1 = ((f32[16,40,128]{2,1,0:T(8,128)}), f32[16,40,128]{2,1,0:T(8,128)S(1)}, u32[]{:S(2)}, u32[]{:S(2)}) async-start(f32[16,40,128]{2,1,0:T(8,128)} %broadcast_in_dim.27), calls=%async_computation.1 | async-start | bytes 655360 | tf_op jit(solution)/shard_map/all_to_all | solution.py:229
  35.8 9.7 %all-to-all-done.1.mixed = f32[16,40,128]{2,1,0:T(8,128)S(1)} async-done(((f32[16,40,128]{2,1,0:T(8,128)}), f32[16,40,128]{2,1,0:T(8,128)S(1)}, u32[]{:S(2)}, u32[]{:S(2)}) %all-to-all-start.1) | async-done | bytes 327712 | tf_op jit(solution)/shard_map/all_to_all | solution.py:229
  45.5 1.0 %broadcast_in_dim.25 = f32[16,3,32,128]{3,2,1,0:T(8,128)} broadcast(f32[3,32,128]{2,1,0:T(8,128)S(1)} %pad_maximum_fusion), dimensions={1,2,3} | broadcast | bytes 835584 | tf_op jit(solution)/shard_map/broadcast_in_dim | solution.py:272
  46.4 3.6 %all-to-all-start.2 = ((f32[16,3,32,128]{3,2,1,0:T(8,128)}), f32[16,3,32,128]{3,2,1,0:T(8,128)S(1)}, u32[]{:S(2)}, u32[]{:S(2)}) async-start(f32[16,3,32,128]{3,2,1,0:T(8,128)} %broadcast_in_dim.25), calls=%async_computation.2 | async-start | bytes 1572864 | tf_op jit(solution)/shard_map/all_to_all | solution.py:229
  50.1 7.6 %panel_inverse.1.inverse0 = f32[256,256]{1,0:T(8,128)S(1)} custom-call(f32[16,40,128]{2,1,0:T(8,128)S(1)} %all-to-all-done.1.mixed), custom_call_target="tpu_custom_call" | custom-call | flops 6710886400 | bytes 524288 | tf_op jit(solution)/shard_map/panel_inverse/pallas_call | solution.py:299
  57.7 0.0 collective-permute-done.1.prev
  57.7 6.2 %all-to-all-done.2.rest = f32[16,3,32,128]{3,2,1,0:T(8,128)S(1)} async-done(((f32[16,3,32,128]{3,2,1,0:T(8,128)}), f32[16,3,32,128]{3,2,1,0:T(8,128)S(1)}, u32[]{:S(2)}, u32[]{:S(2)}) %all-to-all-start.2) | async-done | bytes 786464 | tf_op jit(solution)/shard_map/all_to_all | solution.py:229
  63.9 12.5 %panel_update.1 = (f32[512,512]{1,0:T(8,128)}, f32[512,256]{1,0:T(8,128)}) custom-call(s32[1]{0:T(128)} %bitcast.row_index, f32[256,256]{1,0:T(8,128)S(1)} %panel_inverse.1.inverse0, f32[16,40,128]{2,1,0:T(8,128)S(1)} %all-to-all-done.1.mixed, f32[16,3,32,128]{3,2,1,0:T(8,128)S(1)} %all-to-all-done.2.rest, f32[512,768]{1,0:T(8,128)S(1)} %bitcast.8, ...), custom_call_target="tpu_custom_call" | custom-call | tf_op jit(solution)/shard_map/panel_update/pallas_call | solution.py:310
  (3 shorter events, 0.0 us)
Async XLA Ops:
  0.6 3.4 %copy-start = (f32[1,512,768]{2,1,0:T(8,128)S(1)}, f32[1,512,768]{2,1,0:T(8,128)}, u32[]{:S(2)}) copy-start(f32[1,512,768]{2,1,0:T(8,128)} %param.2) | copy-start | bytes 4718596
  2.1 11.2 %collective-permute-start = (f32[16,72,128]{2,1,0:T(8,128)S(1)}, f32[16,72,128]{2,1,0:T(8,128)S(1)}, u32[]{:S(2)}, u32[]{:S(2)}) collective-permute-start(f32[16,72,128]{2,1,0:T(8,128)S(1)} %head_shares.2), channel_id=1, source_target_pairs={{0,16},{1,17},{16,32},{17,33},{32,48},{33,49},{48,64},{49,65},{64,... | collective-permute-start | bytes 1769480 | tf_op jit(solution)/shard_map/ppermute | solution.py:288
  14.1 17.3 %all-to-all-start = ((f32[16,72,128]{2,1,0:T(8,128)}), f32[16,72,128]{2,1,0:T(8,128)S(1)}, u32[]{:S(2)}, u32[]{:S(2)}) async-start(f32[16,72,128]{2,1,0:T(8,128)} %sub.3), calls=%async_computation | async-start | bytes 1179648 | tf_op jit(solution)/shard_map/all_to_all | solution.py:229
  17.7 39.9 %collective-permute-start.1 = (f32[512,768]{1,0:T(8,128)}, f32[512,768]{1,0:T(8,128)}, u32[]{:S(2)}, u32[]{:S(2)}) collective-permute-start(f32[512,768]{1,0:T(8,128)} %bitcast.2.block), channel_id=1, source_target_pairs={{0,16},{16,32},{32,48},{48,64},{64,80},{80,96},{96,112},{112,128},... | collective-permute-start | bytes 4718600 | tf_op jit(solution)/shard_map/ppermute | solution.py:293
  32.2 13.2 %all-to-all-start.1 = ((f32[16,40,128]{2,1,0:T(8,128)}), f32[16,40,128]{2,1,0:T(8,128)S(1)}, u32[]{:S(2)}, u32[]{:S(2)}) async-start(f32[16,40,128]{2,1,0:T(8,128)} %broadcast_in_dim.27), calls=%async_computation.1 | async-start | bytes 655360 | tf_op jit(solution)/shard_map/all_to_all | solution.py:229
  46.4 17.4 %all-to-all-start.2 = ((f32[16,3,32,128]{3,2,1,0:T(8,128)}), f32[16,3,32,128]{3,2,1,0:T(8,128)S(1)}, u32[]{:S(2)}, u32[]{:S(2)}) async-start(f32[16,3,32,128]{3,2,1,0:T(8,128)} %broadcast_in_dim.25), calls=%async_computation.2 | async-start | bytes 1572864 | tf_op jit(solution)/shard_map/all_to_all | solution.py:229
